TPU v7x, 32 devices: a whole 2x2x4 slice. The times are simulated.
32 devices in a mesh: seq: 8 (over y, x, core), tp: 4 (over z).
Axes of the slice: x: 2, y: 2, z: 4, core: 2. Of those that a mesh axis runs over, the one named last changes fastest.
Arguments:
- hidden_in: bfloat16 [16, 512, 1024], P(None, 'seq', 'tp'), may hold values from -6 to 6
- norm_gain: float32 [1024], replicated, may hold values from 0.25 to 1.75
- norm_shift: float32 [1024], replicated, may hold values from -3 to 3
- query_weight: bfloat16 [1024, 1024], P(None, 'tp'), may hold values from -0.375 to 0.375
- query_bias: float32 [1024], P('tp'), may hold values from -3 to 3
- key_weight: bfloat16 [1024, 1024], P(None, 'tp'), may hold values from -0.1875 to 0.1875
- value_weight: bfloat16 [1024, 1024], P(None, 'tp'), may hold values from -0.1875 to 0.1875
- value_bias: float32 [1024], P('tp'), may hold values from -3 to 3
- output_weight: bfloat16 [1024, 1024], P('tp'), may hold values from -4 to 4
- output_bias: float32 [1024], replicated, may hold values from -3 to 3
- feed_gain: float32 [1024], replicated, may hold values from 0.25 to 1.75
- feed_shift: float32 [1024], replicated, may hold values from -3 to 3
- inner_weight: bfloat16 [1024, 4096], P(None, 'tp'), may hold values from -0.1875 to 0.1875
- inner_bias: float32 [4096], P('tp'), may hold values from -3 to 3
- outer_weight: bfloat16 [4096, 1024], P('tp'), may hold values from -0.09375 to 0.09375
- outer_bias: float32 [1024], replicated, may hold values from -3 to 3
- doc_blocks: int32 [32], replicated, may hold values from 1 to 64, 128 in all
- doc_padding: int32 [32], replicated, may hold values from 0 to 31
- random_picks: int32 [128, 3], replicated, may hold values from 0 to 4095
- cotangent: bfloat16 [16, 512, 1024], P(None, 'seq', 'tp'), may hold values from -6 to 6
Outputs:
- layer_out: bfloat16 [16, 512, 1024], P(None, 'seq', 'tp')
- grad_input: float32 [16, 512, 1024], P(None, 'seq', 'tp')
- grad_norm_gain: float32 [1024], replicated
- grad_norm_shift: float32 [1024], replicated
- grad_query_weight: float32 [1024, 1024], P('seq', 'tp')
- grad_query_bias: float32 [1024], P('tp')
- grad_key_weight: float32 [1024, 1024], P('seq', 'tp')
- grad_value_weight: float32 [1024, 1024], P('seq', 'tp')
- grad_value_bias: float32 [1024], P('tp')
- grad_output_weight: float32 [1024, 1024], P('tp', 'seq')
- grad_output_bias: float32 [1024], replicated
- grad_feed_gain: float32 [1024], replicated
- grad_feed_shift: float32 [1024], replicated
- grad_inner_weight: float32 [1024, 4096], P('seq', 'tp')
- grad_inner_bias: float32 [4096], P('tp')
- grad_outer_weight: float32 [4096, 1024], P('tp', 'seq')
- grad_outer_bias: float32 [1024], replicated
Inputs may be any that keep to these rules, and one draw needn't show every extreme that they name: `doc_blocks`: document lengths in blocks of 64 tokens; together they fill all 128 blocks.
All inputs are finite; a program needn't handle non-finite values.
Results may differ from a plain program's by a relative error of at most 0.02.
Values may be sent and summed in bfloat16 or wider, within the bound.
A program may use at most 192 MiB of HBM per device.

v0:
```python
import math

import jax
import jax.numpy as jnp
from jax import lax
from jax.sharding import PartitionSpec as P

HEAD_DIM = 64
BLK = 64
GLOBAL = 2


def layer_norm(value, gain, shift):
    mean = jnp.mean(value, axis=-1, keepdims=True)
    centered = value - mean
    spread = jnp.mean(centered * centered, axis=-1, keepdims=True)
    return centered * lax.rsqrt(spread + 1e-05) * gain + shift


def gelu_tanh(value):
    return jax.nn.gelu(value, approximate=True)


def block_tables(doc_blocks, doc_padding, random_picks, nblocks):
    ends = jnp.cumsum(doc_blocks)
    starts = ends - doc_blocks
    block_ids = jnp.arange(nblocks, dtype=jnp.int32)
    member = (
        (block_ids[:, None] >= starts[None, :]) & (block_ids[:, None] < ends[None, :])
    ).astype(jnp.int32)
    doc_index = jnp.arange(doc_blocks.shape[0], dtype=jnp.int32)
    doc_of = jnp.sum(member * doc_index[None, :], axis=1)
    first = jnp.sum(member * starts[None, :], axis=1)
    length = jnp.sum(member * doc_blocks[None, :], axis=1)
    padding = jnp.sum(member * doc_padding[None, :], axis=1)
    last_block = block_ids == first + length - 1
    live = jnp.where(last_block, BLK - padding, BLK)
    partner = first[:, None] + jnp.remainder(random_picks, length[:, None])
    return (doc_of, first, live, partner)


def key_allow(start, count, query_side, tables, shard_rows, nseq):
    doc_of, first, live, partner = tables
    query_blocks, query_doc, query_first, query_partner = query_side
    row_ids = start + jnp.arange(count, dtype=jnp.int32)
    local = row_ids % shard_rows
    key_blocks = local // BLK * nseq + row_ids // shard_rows
    key_doc = jnp.take(doc_of, key_blocks)
    key_first = jnp.take(first, key_blocks)
    key_live = local % BLK < jnp.take(live, key_blocks)
    same = query_doc[:, None] == key_doc[None, :]
    near = jnp.abs(query_blocks[:, None] - key_blocks[None, :]) <= 1
    glob = (key_blocks - key_first < GLOBAL)[None, :] | (query_blocks - query_first < GLOBAL)[
        :, None
    ]
    chosen = jnp.any(query_partner[:, :, None] == key_blocks[None, None, :], axis=1)
    return same & (near | glob | chosen) & key_live[None, :]


def side_slice(query_side, first_block, nblocks):
    return tuple((item[first_block : first_block + nblocks] for item in query_side))


def forward_fold(carry, piece, query_heads, query_side, tables, shard_rows, nseq):
    keys, values = piece
    count = keys.shape[0]
    width = math.gcd(count, 512)
    rows, heads = (query_heads.shape[0], query_heads.shape[1])
    group = math.gcd(rows, 512)
    ngroups = rows // group
    group_blocks = group // BLK

    def forward_inner(state, window):
        offset = window * width
        key_part = lax.dynamic_slice_in_dim(keys, offset, width, 0).reshape(width, heads, HEAD_DIM)
        value_part = lax.dynamic_slice_in_dim(values, offset, width, 0).reshape(
            width, heads, HEAD_DIM
        )
        accum_all, top_all, total_all = state
        accum_list, top_list, total_list = ([], [], [])
        for index in range(ngroups):
            qstart = index * group
            allow = key_allow(
                offset,
                width,
                side_slice(query_side, qstart // BLK, group_blocks),
                tables,
                shard_rows,
                nseq,
            )
            mask = allow[:, None, None, :]
            query_part = query_heads[qstart : qstart + group]
            scores = jnp.einsum(
                "qhe,khe->qhk", query_part, key_part, preferred_element_type=jnp.float32
            )
            scores = jnp.where(mask, scores.reshape(group_blocks, BLK, heads, width), -1e30)
            top = top_all[qstart : qstart + group]
            new_top = jnp.maximum(top, jnp.max(scores, axis=-1).reshape(group, heads))
            weights = jnp.where(
                mask, jnp.exp(scores - new_top.reshape(group_blocks, BLK, heads)[..., None]), 0.0
            )
            weights = weights.reshape(group, heads, width)
            decay = jnp.exp(top - new_top)
            total_list.append(
                total_all[qstart : qstart + group] * decay + jnp.sum(weights, axis=-1)
            )
            accum_list.append(
                accum_all[qstart : qstart + group] * decay[..., None]
                + jnp.einsum(
                    "qhk,khe->qhe",
                    weights.astype(jnp.bfloat16),
                    value_part,
                    preferred_element_type=jnp.float32,
                )
            )
            top_list.append(new_top)
        return (
            (
                jnp.concatenate(accum_list, axis=0),
                jnp.concatenate(top_list, axis=0),
                jnp.concatenate(total_list, axis=0),
            ),
            None,
        )

    carry, _ = lax.scan(forward_inner, carry, jnp.arange(count // width, dtype=jnp.int32))
    return carry


def backward_fold(
    carry, piece, query_heads, grad_heads, log_total, delta, query_side, tables, shard_rows, nseq
):
    keys, values = piece
    count = keys.shape[0]
    width = math.gcd(count, 512)
    rows, heads = (query_heads.shape[0], query_heads.shape[1])
    group = math.gcd(rows, 512)
    ngroups = rows // group
    group_blocks = group // BLK

    def backward_inner(state, window):
        offset = window * width
        key_part = lax.dynamic_slice_in_dim(keys, offset, width, 0).reshape(width, heads, HEAD_DIM)
        value_part = lax.dynamic_slice_in_dim(values, offset, width, 0).reshape(
            width, heads, HEAD_DIM
        )
        grad_query_all, grad_keys, grad_values = state
        key_sum = jnp.zeros((width, heads, HEAD_DIM), jnp.float32)
        value_sum = jnp.zeros((width, heads, HEAD_DIM), jnp.float32)
        query_list = []
        for index in range(ngroups):
            qstart = index * group
            allow = key_allow(
                offset,
                width,
                side_slice(query_side, qstart // BLK, group_blocks),
                tables,
                shard_rows,
                nseq,
            )
            mask = allow[:, None, None, :]
            query_part = query_heads[qstart : qstart + group]
            grad_part = grad_heads[qstart : qstart + group]
            log_part = log_total[qstart : qstart + group]
            delta_part = delta[qstart : qstart + group]
            scores = jnp.einsum(
                "qhe,khe->qhk", query_part, key_part, preferred_element_type=jnp.float32
            )
            probs = jnp.where(
                mask,
                jnp.exp(scores - log_part[..., None]).reshape(group_blocks, BLK, heads, width),
                0.0,
            )
            probs = probs.reshape(group, heads, width)
            grad_probs = jnp.einsum(
                "qhe,khe->qhk", grad_part, value_part, preferred_element_type=jnp.float32
            )
            grad_scores = (probs * (grad_probs - delta_part[..., None])).astype(jnp.bfloat16)
            value_sum = value_sum + jnp.einsum(
                "qhk,qhe->khe",
                probs.astype(jnp.bfloat16),
                grad_part,
                preferred_element_type=jnp.float32,
            )
            key_sum = key_sum + jnp.einsum(
                "qhk,qhe->khe", grad_scores, query_part, preferred_element_type=jnp.float32
            )
            query_list.append(
                grad_query_all[qstart : qstart + group]
                + jnp.einsum(
                    "qhk,khe->qhe", grad_scores, key_part, preferred_element_type=jnp.float32
                )
            )
        old_keys = lax.dynamic_slice_in_dim(grad_keys, offset, width, 0)
        old_values = lax.dynamic_slice_in_dim(grad_values, offset, width, 0)
        grad_keys = lax.dynamic_update_slice_in_dim(
            grad_keys, old_keys + key_sum.reshape(width, heads * HEAD_DIM), offset, 0
        )
        grad_values = lax.dynamic_update_slice_in_dim(
            grad_values, old_values + value_sum.reshape(width, heads * HEAD_DIM), offset, 0
        )
        return ((jnp.concatenate(query_list, axis=0), grad_keys, grad_values), None)

    carry, _ = lax.scan(backward_inner, carry, jnp.arange(count // width, dtype=jnp.int32))
    return carry


def contract_rows(left, right):
    return lax.dot_general(
        left, right, (((0,), (0,)), ((), ())), preferred_element_type=jnp.float32
    )


def contract_cols(left, right):
    return lax.dot_general(
        left, right, (((1,), (1,)), ((), ())), preferred_element_type=jnp.float32
    )


def on_device(
    hidden_in,
    norm_gain,
    norm_shift,
    query_weight,
    query_bias,
    key_weight,
    value_weight,
    value_bias,
    output_weight,
    output_bias,
    feed_gain,
    feed_shift,
    inner_weight,
    inner_bias,
    outer_weight,
    outer_bias,
    doc_blocks,
    doc_padding,
    random_picks,
    cotangent,
):
    blocks_here, block_len, part_width = hidden_in.shape
    shard_rows = blocks_here * block_len
    nseq = lax.axis_size("seq")
    seq_index = lax.axis_index("seq")
    tp_index = lax.axis_index("tp")
    local_width = query_weight.shape[1]
    heads = local_width // HEAD_DIM
    all_rows = shard_rows * nseq
    tables = block_tables(doc_blocks, doc_padding, random_picks, blocks_here * nseq)
    query_blocks = jnp.arange(blocks_here, dtype=jnp.int32) * nseq + seq_index
    query_side = (
        query_blocks,
        jnp.take(tables[0], query_blocks),
        jnp.take(tables[1], query_blocks),
        jnp.take(tables[3], query_blocks, axis=0),
    )
    gathered = lax.all_gather(hidden_in.reshape(shard_rows, part_width), "tp", axis=1, tiled=True)
    x_full = gathered.astype(jnp.float32)
    h1 = layer_norm(x_full, norm_gain, norm_shift).astype(jnp.bfloat16)
    queries = (
        (jnp.dot(h1, query_weight, preferred_element_type=jnp.float32) + query_bias) * 0.125
    ).astype(jnp.bfloat16)
    keys = jnp.dot(h1, key_weight, preferred_element_type=jnp.float32).astype(jnp.bfloat16)
    values = (jnp.dot(h1, value_weight, preferred_element_type=jnp.float32) + value_bias).astype(
        jnp.bfloat16
    )
    query_heads = queries.reshape(shard_rows, heads, HEAD_DIM)
    start_state = (
        jnp.zeros((shard_rows, heads, HEAD_DIM), jnp.float32),
        jnp.full((shard_rows, heads), -1e30, jnp.float32),
        jnp.zeros((shard_rows, heads), jnp.float32),
    )
    accum, top, total = forward_fold(
        start_state,
        (
            lax.all_gather(keys, "seq", axis=0, tiled=True),
            lax.all_gather(values, "seq", axis=0, tiled=True),
        ),
        query_heads,
        query_side,
        tables,
        shard_rows,
        nseq,
    )
    mixed_heads = accum / total[..., None]
    log_total = top + jnp.log(total)
    mixed = mixed_heads.reshape(shard_rows, local_width).astype(jnp.bfloat16)
    attn_part = jnp.dot(mixed, output_weight, preferred_element_type=jnp.float32)
    x1 = x_full + lax.psum(attn_part.astype(jnp.bfloat16), "tp").astype(jnp.float32) + output_bias
    h2_f, feed_pull = jax.vjp(layer_norm, x1, feed_gain, feed_shift)
    h2 = h2_f.astype(jnp.bfloat16)
    pre = jnp.dot(h2, inner_weight, preferred_element_type=jnp.float32) + inner_bias
    act_f, gelu_pull = jax.vjp(gelu_tanh, pre)
    act = act_f.astype(jnp.bfloat16)
    ffn_part = jnp.dot(act, outer_weight, preferred_element_type=jnp.float32)
    result = x1 + lax.psum(ffn_part.astype(jnp.bfloat16), "tp").astype(jnp.float32) + outer_bias
    result_part = lax.dynamic_slice_in_dim(result, tp_index * part_width, part_width, 1)
    layer_out = result_part.astype(jnp.bfloat16).reshape(hidden_in.shape)
    grad_out = lax.all_gather(cotangent.reshape(shard_rows, part_width), "tp", axis=1, tiled=True)
    grad_out_f = grad_out.astype(jnp.float32)
    grad_outer_bias = jnp.sum(grad_out_f, axis=0)
    grad_outer_weight = contract_rows(act, grad_out)
    grad_act = contract_cols(grad_out, outer_weight)
    grad_pre = gelu_pull(grad_act)[0].astype(jnp.bfloat16)
    grad_inner_bias = jnp.sum(grad_pre.astype(jnp.float32), axis=0)
    grad_inner_weight = contract_rows(h2, grad_pre)
    grad_h2 = lax.psum(contract_cols(grad_pre, inner_weight).astype(jnp.bfloat16), "tp").astype(
        jnp.float32
    )
    grad_x1_norm, grad_feed_gain, grad_feed_shift = feed_pull(grad_h2)
    grad_x1 = grad_out_f + grad_x1_norm
    grad_branch = grad_x1.astype(jnp.bfloat16)
    grad_output_bias = jnp.sum(grad_branch.astype(jnp.float32), axis=0)
    grad_output_weight = contract_rows(mixed, grad_branch)
    grad_mixed = contract_cols(grad_branch, output_weight).astype(jnp.bfloat16)
    grad_heads = grad_mixed.reshape(shard_rows, heads, HEAD_DIM)
    delta = jnp.sum(grad_heads.astype(jnp.float32) * mixed_heads, axis=-1)
    back_state = (
        jnp.zeros((shard_rows, heads, HEAD_DIM), jnp.float32),
        jnp.zeros((all_rows, local_width), jnp.float32),
        jnp.zeros((all_rows, local_width), jnp.float32),
    )
    grad_query, key_terms, value_terms = backward_fold(
        back_state,
        (
            lax.all_gather(keys, "seq", axis=0, tiled=True),
            lax.all_gather(values, "seq", axis=0, tiled=True),
        ),
        query_heads,
        grad_heads,
        log_total,
        delta,
        query_side,
        tables,
        shard_rows,
        nseq,
    )
    grad_keys_f, grad_values_f = (
        lax.psum_scatter(
            key_terms.astype(jnp.bfloat16), "seq", scatter_dimension=0, tiled=True
        ).astype(jnp.float32),
        lax.psum_scatter(
            value_terms.astype(jnp.bfloat16), "seq", scatter_dimension=0, tiled=True
        ).astype(jnp.float32),
    )
    grad_queries = grad_query.reshape(shard_rows, local_width).astype(jnp.bfloat16)
    grad_keys = grad_keys_f.astype(jnp.bfloat16)
    grad_values = grad_values_f.astype(jnp.bfloat16)
    grad_query_bias = 0.125 * jnp.sum(grad_queries.astype(jnp.float32), axis=0)
    grad_query_weight = 0.125 * contract_rows(h1, grad_queries)
    grad_key_weight = contract_rows(h1, grad_keys)
    grad_value_weight = contract_rows(h1, grad_values)
    grad_value_bias = jnp.sum(grad_values.astype(jnp.float32), axis=0)
    grad_h1_part = (
        0.125 * contract_cols(grad_queries, query_weight)
        + contract_cols(grad_keys, key_weight)
        + contract_cols(grad_values, value_weight)
    )
    grad_h1 = lax.psum(grad_h1_part.astype(jnp.bfloat16), "tp").astype(jnp.float32)
    _, norm_pull = jax.vjp(layer_norm, x_full, norm_gain, norm_shift)
    grad_x_norm, grad_norm_gain, grad_norm_shift = norm_pull(grad_h1)
    grad_full = grad_x1 + grad_x_norm
    grad_input = lax.dynamic_slice_in_dim(grad_full, tp_index * part_width, part_width, 1).reshape(
        hidden_in.shape
    )
    summed = (
        lax.psum_scatter(
            grad_query_weight.astype(jnp.bfloat16), "seq", scatter_dimension=0, tiled=True
        ).astype(jnp.float32),
        lax.psum_scatter(
            grad_key_weight.astype(jnp.bfloat16), "seq", scatter_dimension=0, tiled=True
        ).astype(jnp.float32),
        lax.psum_scatter(
            grad_value_weight.astype(jnp.bfloat16), "seq", scatter_dimension=0, tiled=True
        ).astype(jnp.float32),
        lax.psum_scatter(
            grad_inner_weight.astype(jnp.bfloat16), "seq", scatter_dimension=0, tiled=True
        ).astype(jnp.float32),
        lax.psum_scatter(
            grad_output_weight.astype(jnp.bfloat16), "seq", scatter_dimension=1, tiled=True
        ).astype(jnp.float32),
        lax.psum_scatter(
            grad_outer_weight.astype(jnp.bfloat16), "seq", scatter_dimension=1, tiled=True
        ).astype(jnp.float32),
    )
    vectors = lax.psum(
        (
            grad_norm_gain,
            grad_norm_shift,
            grad_query_bias,
            grad_value_bias,
            grad_output_bias,
            grad_feed_gain,
            grad_feed_shift,
            grad_inner_bias,
            grad_outer_bias,
        ),
        "seq",
    )
    return (
        layer_out,
        grad_input,
        vectors[0],
        vectors[1],
        summed[0],
        vectors[2],
        summed[1],
        summed[2],
        vectors[3],
        summed[4],
        vectors[4],
        vectors[5],
        vectors[6],
        summed[3],
        vectors[7],
        summed[5],
        vectors[8],
    )


def solution(mesh):
    return jax.shard_map(
        on_device,
        mesh=mesh,
        in_specs=(
            P(None, "seq", "tp"),
            P(),
            P(),
            P(None, "tp"),
            P("tp"),
            P(None, "tp"),
            P(None, "tp"),
            P("tp"),
            P("tp", None),
            P(),
            P(),
            P(),
            P(None, "tp"),
            P("tp"),
            P("tp", None),
            P(),
            P(),
            P(),
            P(),
            P(None, "seq", "tp"),
        ),
        out_specs=(
            P(None, "seq", "tp"),
            P(None, "seq", "tp"),
            P(),
            P(),
            P("seq", "tp"),
            P("tp"),
            P("seq", "tp"),
            P("seq", "tp"),
            P("tp"),
            P("tp", "seq"),
            P(),
            P(),
            P(),
            P("seq", "tp"),
            P("tp"),
            P("tp", "seq"),
            P(),
        ),
        check_vma=False,
    )
```

profile of v0, /device:TPU:8, one launch (start us, length us, event | category | flops | bytes accessed | tf_op | source)
XLA Modules:
  0.0 1723.7 jit_solution(4381591462469223975)
XLA Ops:
  8.0 47.7 %all-gather.5.cloned.1.call-done = bf16[1024,1024]{1,0:T(8,128)(2,1)} async-done(((bf16[1024,256]{1,0:T(8,128)(2,1)}), bf16[1024,1024]{1,0:T(8,128)(2,1)}) %all-gather.5.cloned.1.call-update) | async-done | bytes 2097168 | tf_op jit(solution)/shard_map/all_gather | solution.py:258
  73.7 27.2 %all-gather.9.cloned.1.call-done = bf16[8192,256]{1,0:T(8,128)(2,1)} async-done(((bf16[1024,256]{1,0:T(8,128)(2,1)}), bf16[8192,256]{1,0:T(8,128)(2,1)}) %all-gather.9.cloned.1.call-update) | async-done | bytes 4194320 | tf_op jit(solution)/shard_map/all_gather | solution.py:278
  100.9 6.3 copy.149
  107.2 32.9 %all-gather.7.cloned.1.call-done = bf16[8192,256]{1,0:T(8,128)(2,1)} async-done(((bf16[1024,256]{1,0:T(8,128)(2,1)}), bf16[8192,256]{1,0:T(8,128)(2,1)}) %all-gather.7.cloned.1.call-update) | async-done | bytes 4194320 | tf_op jit(solution)/shard_map/all_gather | solution.py:277
  140.1 6.4 copy.148
  147.6 335.6 %while.34 = (s32[]{:T(128)}, f32[1024,4,64]{0,2,1:T(8,128)}, f32[1024,4]{0,1:T(4,128)S(1)}, f32[1024,4]{0,1:T(4,128)S(1)}, s32[16]{0:T(128)S(1)}, /*index=5*/s32...) while((s32[]{:T(128)}, f32[1024,4,64]{0,2,1:T(8,128)}, ...), condition=%wide.region_14.17_spmd, body=%wide.region_7.0_spmd.sunk | while | flops 558852608 | bytes 39695688 | solution.py:126
  489.2 84.4 %all-reduce.6.cloned.1.call-done = bf16[1024,1024]{1,0:T(8,128)(2,1)} async-done(((bf16[1024,1024]{1,0:T(8,128)(2,1)}), bf16[1024,1024]{1,0:T(8,128)(2,1)}) %all-reduce.6.cloned.1.call-update) | async-done | bytes 2097168 | tf_op jit(solution)/shard_map/psum | solution.py:290
  584.2 36.3 %all-gather.11.cloned.1.call-done = bf16[1024,1024]{1,0:T(8,128)(2,1)} async-done(((bf16[1024,256]{1,0:T(8,128)(2,1)}), bf16[1024,1024]{1,0:T(8,128)(2,1)}) %all-gather.11.cloned.1.call-update) | async-done | bytes 2097168 | tf_op jit(solution)/shard_map/all_gather | solution.py:300
  620.5 8.1 convert_reduce_fusion.4
  633.6 84.7 %all-reduce.8.cloned.1.call-done = bf16[1024,1024]{1,0:T(8,128)(2,1)} async-done(((bf16[1024,1024]{1,0:T(8,128)(2,1)}), bf16[1024,1024]{1,0:T(8,128)(2,1)}) %all-reduce.8.cloned.1.call-update) | async-done | bytes 2097168 | tf_op jit(solution)/shard_map/psum | solution.py:308
  741.5 431.3 %while.35 = (s32[]{:T(128)}, f32[1024,4,64]{0,2,1:T(8,128)}, f32[8192,256]{0,1:T(8,128)}, f32[8192,256]{0,1:T(8,128)}, s32[16]{0:T(128)S(1)}, /*index=5*/bf16[81...) while((s32[]{:T(128)}, f32[1024,4,64]{0,2,1:T(8,128)}, ...), condition=%wide.region_26.29_spmd, body=%wide.region_23.28_spmd.sunk | while | flops 1360229376 | bytes 62059908 | solution.py:204
  1195.9 7.2 convolution_convert_fusion
  1207.2 7.0 convolution_convert_fusion.1
  1214.2 16.4 reduce-scatter.17.cloned.1.call-done
  1233.9 6.4 convolution_convert_fusion.3
  1243.1 42.6 %reduce-scatter.15.cloned.1.call-done = bf16[1024,256]{0,1:T(8,128)(2,1)} async-done(((bf16[8192,256]{0,1:T(8,128)(2,1)}), bf16[1024,256]{0,1:T(8,128)(2,1)}) %reduce-scatter.15.cloned.1.call-update) | async-done | bytes 524304 | tf_op jit(solution)/shard_map/reduce_scatter | solution.py:340
  1294.7 28.3 %reduce-scatter.27.cloned.1.call-done = bf16[128,256]{1,0:T(8,128)(2,1)} async-done(((bf16[1024,256]{1,0:T(8,128)(2,1)}), bf16[128,256]{1,0:T(8,128)(2,1)}) %reduce-scatter.27.cloned.1.call-update) | async-done | bytes 65552
  1324.6 36.4 %reduce-scatter.25.cloned.1.call-done = bf16[128,256]{1,0:T(8,128)(2,1)} async-done(((bf16[1024,256]{1,0:T(8,128)(2,1)}), bf16[128,256]{1,0:T(8,128)(2,1)}) %reduce-scatter.25.cloned.1.call-update) | async-done | bytes 65552
  1362.7 42.8 %reduce-scatter.29.cloned.1.call-done = bf16[128,1024]{1,0:T(8,128)(2,1)} async-done(((bf16[1024,1024]{1,0:T(8,128)(2,1)}), bf16[128,1024]{1,0:T(8,128)(2,1)}) %reduce-scatter.29.cloned.1.call-update) | async-done | bytes 262160
  1407.4 42.8 %reduce-scatter.23.cloned.1.call-done = bf16[128,1024]{1,0:T(8,128)(2,1)} async-done(((bf16[1024,1024]{1,0:T(8,128)(2,1)}), bf16[128,1024]{1,0:T(8,128)(2,1)}) %reduce-scatter.23.cloned.1.call-update) | async-done | bytes 262160 | tf_op jit(solution)/shard_map/reduce_scatter | solution.py:377
  1452.2 35.9 %reduce-scatter.21.cloned.1.call-done = bf16[128,256]{1,0:T(8,128)(2,1)} async-done(((bf16[1024,256]{1,0:T(8,128)(2,1)}), bf16[128,256]{1,0:T(8,128)(2,1)}) %reduce-scatter.21.cloned.1.call-update) | async-done | bytes 65552 | tf_op jit(solution)/shard_map/reduce_scatter | solution.py:374
  1489.5 36.5 %reduce-scatter.19.cloned.1.call-done = bf16[128,256]{1,0:T(8,128)(2,1)} async-done(((bf16[1024,256]{1,0:T(8,128)(2,1)}), bf16[128,256]{1,0:T(8,128)(2,1)}) %reduce-scatter.19.cloned.1.call-update) | async-done | bytes 65552 | tf_op jit(solution)/shard_map/reduce_scatter | solution.py:371
  1527.5 153.9 %all-reduce.10.cloned.1.call-done = (bf16[1024,1024]{1,0:T(8,128)(2,1)}, bf16[1024,1024]{1,0:T(8,128)(2,1)}) async-done(((bf16[1024,1024]{1,0:T(8,128)(2,1)}, bf16[1024,1024]{1,0:T(8,128)(2,1)}), (bf16[1024,1024]{1,0:T(8,128)(2,1)}, bf16[1024,1024]{1,0:T(8,128)(2,1)})) %all-reduce.10.cloned.1.call-update) | async-done | bytes 4194320 | tf_op jit(solution)/shard_map/psum | solution.py:297
  1692.1 24.9 %all-reduce = (f32[1024]{0:T(1024)}, f32[1024]{0:T(1024)}, f32[256]{0:T(256)}, f32[256]{0:T(256)}, f32[1024]{0:T(1024)}, /*index=5*/f32[1024]{0:T(1024)}, f32[1024]{0:T(1024)}, f32[1024]{0:T(1024)}, f32[1024]{0:T(1024)}) all-reduce(f32[1024]{0:T(1024)S(1)} %get-tuple-element.839, ...), channel_id=1, replica_groups=mesh['seq'=8,'tp'=4] {'seq'}, use_global_device_ids=true, to_apply=%region_33.36 | all-reduce | flops 7680 | bytes 61440 | tf_op jit(solution)/shard_map/psum | solution.py:387
  (1379 shorter events, 867.7 us)
Async XLA Ops:
  7.2 613.3 %copy-start = (bf16[1024,1024]{1,0:T(8,128)(2,1)S(1)}, bf16[1024,1024]{1,0:T(8,128)(2,1)}, u32[]{:S(2)}) copy-start(bf16[1024,1024]{1,0:T(8,128)(2,1)} %param.42) | copy-start | bytes 6291460
  7.2 53.5 %copy-start.34 = (f32[1024]{0:T(1024)S(1)}, f32[1024]{0:T(1024)}, u32[]{:S(2)}) copy-start(f32[1024]{0:T(1024)} %param.29) | copy-start | bytes 12292
  7.2 48.5 %all-gather.5.cloned.1.call-start = ((), (), s32[]{:S(2)}) async-start(), calls=%async_computation.8 | async-start | bytes 2621440 | tf_op jit(solution)/shard_map/all_gather | solution.py:258
  8.0 55.0 %copy-start.24 = (bf16[1024,256]{1,0:T(8,128)(2,1)S(1)}, bf16[1024,256]{1,0:T(8,128)(2,1)}, u32[]{:S(2)}) copy-start(bf16[1024,256]{1,0:T(8,128)(2,1)} %param.34) | copy-start | bytes 1572868
  8.0 55.0 %copy-start.48 = (f32[256]{0:T(256)S(1)}, f32[256]{0:T(256)}, u32[]{:S(2)}) copy-start(f32[256]{0:T(256)} %param.35) | copy-start | bytes 3076
  8.0 92.9 %all-gather.9.cloned.1.call-start = ((), (), s32[]{:S(2)}) async-start(), calls=%async_computation.10 | async-start | bytes 4718592 | tf_op jit(solution)/shard_map/all_gather | solution.py:278
  64.5 75.6 %all-gather.7.cloned.1.call-start = ((), (), s32[]{:S(2)}) async-start(), calls=%async_computation.9 | async-start | bytes 4718592 | tf_op jit(solution)/shard_map/all_gather | solution.py:277
  67.8 505.9 %all-reduce.6.cloned.1.call-start = ((), (), s32[]{:S(2)}) async-start(), calls=%async_computation.11 | async-start | bytes 4194304 | tf_op jit(solution)/shard_map/psum | solution.py:290
  483.1 90.5 %copy-start.38 = (f32[1024]{0:T(1024)S(1)}, f32[1024]{0:T(1024)}, u32[]{:S(2)}) copy-start(f32[1024]{0:T(1024)} %param.37) | copy-start | bytes 12292
  488.4 132.1 %all-gather.11.cloned.1.call-start = ((), (), s32[]{:S(2)}) async-start(), calls=%async_computation.12 | async-start | bytes 2621440 | tf_op jit(solution)/shard_map/all_gather | solution.py:300
  489.0 229.3 %all-reduce.8.cloned.1.call-start = ((), (), s32[]{:S(2)}) async-start(), calls=%async_computation.13 | async-start | bytes 4194304 | tf_op jit(solution)/shard_map/psum | solution.py:308
  633.6 597.0 %reduce-scatter.17.cloned.1.call-start = ((), (), s32[]{:S(2)}) async-start(), calls=%async_computation.15 | async-start | bytes 4718592 | tf_op jit(solution)/shard_map/reduce_scatter | solution.py:343
  1178.8 106.9 %reduce-scatter.15.cloned.1.call-start = ((), (), s32[]{:S(2)}) async-start(), calls=%async_computation.14 | async-start | bytes 4718592 | tf_op jit(solution)/shard_map/reduce_scatter | solution.py:340
  1184.8 138.2 %reduce-scatter.27.cloned.1.call-start = ((), (), s32[]{:S(2)}) async-start(), calls=%async_computation.20 | async-start | bytes 589824
  1191.0 170.0 %reduce-scatter.25.cloned.1.call-start = ((), (), s32[]{:S(2)}) async-start(), calls=%async_computation.19 | async-start | bytes 589824
  1195.4 210.0 %reduce-scatter.29.cloned.1.call-start = ((), (), s32[]{:S(2)}) async-start(), calls=%async_computation.21 | async-start | bytes 2359296
  1207.1 243.1 %reduce-scatter.23.cloned.1.call-start = ((), (), s32[]{:S(2)}) async-start(), calls=%async_computation.18 | async-start | bytes 2359296 | tf_op jit(solution)/shard_map/reduce_scatter | solution.py:377
  1214.2 273.9 %reduce-scatter.21.cloned.1.call-start = ((), (), s32[]{:S(2)}) async-start(), calls=%async_computation.17 | async-start | bytes 589824 | tf_op jit(solution)/shard_map/reduce_scatter | solution.py:374
  1233.9 292.1 %reduce-scatter.19.cloned.1.call-start = ((), (), s32[]{:S(2)}) async-start(), calls=%async_computation.16 | async-start | bytes 589824 | tf_op jit(solution)/shard_map/reduce_scatter | solution.py:371
  1289.0 392.5 %all-reduce.10.cloned.1.call-start = ((), (), s32[]{:S(2)}) async-start(), calls=%async_computation.22 | async-start | bytes 8388608 | tf_op jit(solution)/shard_map/psum | solution.py:297
  1293.8 387.7 %copy-start.28 = (f32[1024]{0:T(1024)S(1)}, f32[1024]{0:T(1024)}, u32[]{:S(2)}) copy-start(f32[1024]{0:T(1024)} %copy-done.27) | copy-start | bytes 12292
  1293.8 387.7 %copy-start.30 = (f32[1024]{0:T(1024)S(1)}, f32[1024]{0:T(1024)}, u32[]{:S(2)}) copy-start(f32[1024]{0:T(1024)} %copy-done.29) | copy-start | bytes 12292
  1293.8 387.7 %copy-start.35 = (f32[1024]{0:T(1024)S(1)}, f32[1024]{0:T(1024)}, u32[]{:S(2)}) copy-start(f32[1024]{0:T(1024)} %param.29) | copy-start | bytes 12292
  1293.8 391.6 %copy-start.33 = (f32[1024]{0:T(1024)S(1)}, f32[1024]{0:T(1024)}, u32[]{:S(2)}) copy-start(f32[1024]{0:T(1024)} %copy-done.32) | copy-start | bytes 12292
  (87 other events, 385.2 us)
Sparse Core Ops, SparseCore 0:
  9.6 46.0 all-gather.4
  64.6 36.2 all-gather.8
  103.4 36.7 all-gather.6
  488.5 85.0 all-reduce.5
  575.1 45.3 all-gather.10
  633.7 84.6 all-reduce.7
  1178.9 51.6 reduce-scatter.16
  1234.3 51.3 reduce-scatter.14
  1288.8 34.1 reduce-scatter.26
  1326.8 34.1 reduce-scatter.24
  1364.3 41.1 reduce-scatter.28
  1409.0 41.2 reduce-scatter.22
  1453.9 34.1 reduce-scatter.20
  1491.8 34.1 reduce-scatter.18
  1528.3 153.1 all-reduce.9
where the time goes:
time: 1730 us; the launch traced here: 1720 us
  waiting for transfers between devices  750 us (43%)
  local copies, waits for them, and re-layouts  473 us (27%)
  matrix products  272 us (16%)
  other arithmetic  161 us (9%)
  loops' own time  26.2 us (2%)
  blocking collectives  24.9 us (1%)
    psum x1, waiting for transfers between devices, on_device(): lax.psum(ffn_part.astype(jnp.bfloat16), 'tp').astype(jnp.float32)  154 us
    unnamed x18, waiting for transfers between devices  109 us
    gather x32, local copies, waits for them, and re-layouts, key_allow(): key_first = jnp.take(first, key_blocks)  107 us
    gather x32, local copies, waits for them, and re-layouts, key_allow(): key_live = local % BLK < jnp.take(live, key_blocks)  107 us
    gather x32, local copies, waits for them, and re-layouts, key_allow(): key_doc = jnp.take(doc_of, key_blocks)  107 us
    psum x1, waiting for transfers between devices, on_device(): lax.psum(contract_cols(grad_pre, inner_weight).astype(jnp.bfloat16), 'tp')  84.7 us
    psum x1, waiting for transfers between devices, on_device(): lax.psum(attn_part.astype(jnp.bfloat16), 'tp').astype(jnp.float32)  84.4 us
    all_gather x1, waiting for transfers between devices, on_device(): lax.all_gather(hidden_in.reshape(shard_rows, part_width), 'tp', axis=1, t...  47.7 us
  transfers between devices with their start and end apart: 15, of which 15 were waited for; matrix products, arithmetic and copies ran while one was open for 5% of the time, Pallas kernels for 0%

commit v1 on v0

v1 whole, which is shorter than its diff:
```python
import functools

import jax
import jax.numpy as jnp
from jax import lax
from jax.experimental import pallas as pl
from jax.experimental.pallas import tpu as pltpu
from jax.sharding import PartitionSpec as P

HEAD_DIM = 64
BLK = 64
GLOBAL = 2
SLOTS = 8
WIDE = 2 * HEAD_DIM
NEG = -1e30
NT = (((1,), (1,)), ((), ()))
TN = (((0,), (0,)), ((), ()))


def layer_norm(value, gain, shift):
    mean = jnp.mean(value, axis=-1, keepdims=True)
    centered = value - mean
    spread = jnp.mean(centered * centered, axis=-1, keepdims=True)
    return centered * lax.rsqrt(spread + 1e-05) * gain + shift


def gelu_tanh(value):
    return jax.nn.gelu(value, approximate=True)


def block_tables(doc_blocks, doc_padding, random_picks, nblocks):
    ends = jnp.cumsum(doc_blocks)
    starts = ends - doc_blocks
    block_ids = jnp.arange(nblocks, dtype=jnp.int32)
    member = (
        (block_ids[:, None] >= starts[None, :]) & (block_ids[:, None] < ends[None, :])
    ).astype(jnp.int32)
    first = jnp.sum(member * starts[None, :], axis=1)
    length = jnp.sum(member * doc_blocks[None, :], axis=1)
    padding = jnp.sum(member * doc_padding[None, :], axis=1)
    last_block = block_ids == first + length - 1
    live = jnp.where(last_block, BLK - padding, BLK)
    partner = first[:, None] + jnp.remainder(random_picks, length[:, None])
    return (first, length, live, partner)


def attention_tables(doc_blocks, doc_padding, random_picks, nrows, nseq, heads, part):
    share = nseq // heads
    nblocks = nrows * nseq
    first, length, live, partner = block_tables(doc_blocks, doc_padding, random_picks, nblocks)
    block = jnp.arange(nblocks, dtype=jnp.int32)
    holder = block % nseq
    slot_of = ((holder % share) * heads + holder // share) * nrows + block // nseq
    glob = block - first < GLOBAL
    last = first + length - 1
    step = jnp.arange(SLOTS, dtype=jnp.int32)
    near = jnp.stack([block - 1, block, block + 1, first, first + 1], axis=1)
    picks = jnp.concatenate([near, partner], axis=1)
    whole = first[:, None] + step[None, :]
    cand = jnp.where(glob[:, None], whole, picks)
    valid = (cand >= first[:, None]) & (cand <= last[:, None])
    same = (cand[:, :, None] == cand[:, None, :]) & valid[:, None, :]
    earlier = step[None, None, :] < step[None, :, None]
    valid = valid & ~jnp.any(same & earlier, axis=2)
    is_long = glob & (length > SLOTS)
    valid = valid & ~is_long[:, None]
    place = jnp.cumsum(valid.astype(jnp.int32), axis=1) - 1
    pick = (valid[:, :, None] & (place[:, :, None] == step[None, None, :])).astype(jnp.int32)
    order = jnp.sum(pick * cand[:, :, None], axis=1)
    filled = jnp.sum(pick, axis=1)
    onehot = (order[:, :, None] == block[None, None, :]).astype(jnp.int32)
    slots = jnp.sum(onehot * slot_of[None, None, :], axis=2) * BLK
    lives = filled * jnp.sum(onehot * live[None, None, :], axis=2)
    mine = lambda item: lax.dynamic_index_in_dim(
        jnp.moveaxis(item.reshape((nrows, heads, share) + item.shape[1:]), 2, 0), part, 0, False
    ).swapaxes(0, 1).reshape((nrows * heads,) + item.shape[1:])
    nquery = nrows * heads
    long_mine = mine(is_long.astype(jnp.int32))
    rank = jnp.cumsum(long_mine) - 1
    query = jnp.arange(nquery, dtype=jnp.int32)
    chosen = (long_mine[:, None] * (rank[:, None] == query[None, :])).astype(jnp.int32)
    long_query = jnp.sum(chosen * query[:, None], axis=0)
    long_first = jnp.sum(chosen * mine(first)[:, None], axis=0)
    long_len = jnp.sum(chosen * mine(length)[:, None], axis=0)
    near_table = jnp.concatenate([mine(slots).reshape(-1), mine(lives).reshape(-1)])
    long_table = jnp.concatenate([long_query, long_first, long_len, jnp.sum(long_mine)[None]])
    block_table = jnp.concatenate([slot_of * BLK, live])
    return near_table, long_table, block_table


def bias_row(lives):
    lane = lax.broadcasted_iota(jnp.int32, (1, WIDE), 1)
    parts = []
    for index in range(0, SLOTS, 2):
        bound = jnp.where(lane < BLK, lives[index], lives[index + 1] + BLK)
        parts.append(jnp.where(lane < bound, 0.0, NEG))
    return jnp.concatenate(parts, axis=1)


def near_slots(near_ref, query, nquery):
    base = query * SLOTS
    slots = [pl.multiple_of(near_ref[base + k], BLK) for k in range(SLOTS)]
    lives = [near_ref[nquery * SLOTS + base + k] for k in range(SLOTS)]
    return slots, lives


def long_slots(block_ref, nblocks, first, length, chunk):
    slots, lives = [], []
    for k in range(SLOTS):
        place = chunk * SLOTS + k
        block = first + jnp.minimum(place, length - 1)
        slots.append(pl.multiple_of(block_ref[block], BLK))
        lives.append(jnp.where(place < length, block_ref[nblocks + block], 0))
    return slots, lives


def take(ref, slots):
    return jnp.concatenate([ref[pl.ds(slot, BLK), :] for slot in slots], axis=0)


def forward_kernel(nquery, nblocks, unroll, near_ref, long_ref, block_ref, q_ref, kv_ref, out_ref):
    upper = lax.broadcasted_iota(jnp.int32, (BLK, WIDE), 1) >= HEAD_DIM

    def finish(query, top, total, accum):
        out_ref[pl.ds(query * BLK, BLK), :] = jnp.where(
            upper, accum / total, top + jnp.log(total)
        )

    def scores_of(query, slots, lives):
        kv = take(kv_ref, slots)
        scores = lax.dot_general(
            q_ref[pl.ds(query * BLK, BLK), :], kv, NT, preferred_element_type=jnp.float32
        )
        return kv, scores + bias_row(lives)

    def near_step(index, carry):
        for offset in range(unroll):
            query = index * unroll + offset
            kv, scores = scores_of(query, *near_slots(near_ref, query, nquery))
            top = jnp.max(scores, axis=1, keepdims=True)
            weights = jnp.exp(scores - top)
            total = jnp.sum(weights, axis=1, keepdims=True)
            accum = jnp.dot(weights.astype(jnp.bfloat16), kv, preferred_element_type=jnp.float32)
            finish(query, top, total, accum)
        return carry

    lax.fori_loop(0, nquery // unroll, near_step, 0)

    def long_step(index, carry):
        query = long_ref[index]
        first = long_ref[nquery + index]
        length = long_ref[2 * nquery + index]

        def chunk_step(chunk, state):
            top, total, accum = state
            kv, scores = scores_of(query, *long_slots(block_ref, nblocks, first, length, chunk))
            new_top = jnp.maximum(top, jnp.max(scores, axis=1, keepdims=True))
            weights = jnp.exp(scores - new_top)
            decay = jnp.exp(top - new_top)
            total = total * decay + jnp.sum(weights, axis=1, keepdims=True)
            accum = accum * decay + jnp.dot(
                weights.astype(jnp.bfloat16), kv, preferred_element_type=jnp.float32
            )
            return new_top, total, accum

        start = (
            jnp.full((BLK, 1), NEG, jnp.float32),
            jnp.zeros((BLK, 1), jnp.float32),
            jnp.zeros((BLK, WIDE), jnp.float32),
        )
        top, total, accum = lax.fori_loop(0, (length + SLOTS - 1) // SLOTS, chunk_step, start)
        finish(query, top, total, accum)
        return carry

    lax.fori_loop(0, long_ref[3 * nquery], long_step, 0)


def backward_kernel(
    nquery, nblocks, unroll,
    near_ref, long_ref, block_ref, q_ref, do_ref, res_ref, kv_ref, dq_ref, dkv_ref, sum_ref,
):
    sum_ref[...] = jnp.zeros_like(sum_ref)

    def load(query):
        rows = pl.ds(query * BLK, BLK)
        grad = do_ref[rows, :]
        both = jnp.concatenate([q_ref[rows, :], grad], axis=0)
        res = res_ref[rows, :]
        log_total = res[:, :1]
        delta = jnp.sum(res * grad.astype(jnp.float32), axis=1, keepdims=True)
        return both, log_total, delta

    def terms(both, log_total, delta, slots, lives):
        kv = take(kv_ref, slots)
        pair = lax.dot_general(both, kv, NT, preferred_element_type=jnp.float32)
        probs = jnp.exp(pair[:BLK] + bias_row(lives) - log_total)
        grad_scores = (probs * (pair[BLK:] - delta)).astype(jnp.bfloat16)
        weights = jnp.concatenate([grad_scores, probs.astype(jnp.bfloat16)], axis=0)
        dkv = lax.dot_general(weights, both, TN, preferred_element_type=jnp.float32)
        dq = jnp.dot(grad_scores, kv, preferred_element_type=jnp.float32)
        return dq, dkv

    def scatter(slots, dkv):
        for k, slot in enumerate(slots):
            sum_ref[pl.ds(slot, BLK), :] += dkv[k * BLK : (k + 1) * BLK]

    def near_step(index, carry):
        done = []
        for offset in range(unroll):
            query = index * unroll + offset
            slots, lives = near_slots(near_ref, query, nquery)
            dq, dkv = terms(*load(query), slots, lives)
            dq_ref[pl.ds(query * BLK, BLK), :] = dq.astype(jnp.bfloat16)
            done.append((slots, dkv))
        for slots, dkv in done:
            scatter(slots, dkv)
        return carry

    lax.fori_loop(0, nquery // unroll, near_step, 0)

    def long_step(index, carry):
        query = long_ref[index]
        first = long_ref[nquery + index]
        length = long_ref[2 * nquery + index]
        loaded = load(query)

        def chunk_step(chunk, total):
            slots, lives = long_slots(block_ref, nblocks, first, length, chunk)
            dq, dkv = terms(*loaded, slots, lives)
            scatter(slots, dkv)
            return total + dq

        total = lax.fori_loop(
            0, (length + SLOTS - 1) // SLOTS, chunk_step, jnp.zeros((BLK, WIDE), jnp.float32)
        )
        dq_ref[pl.ds(query * BLK, BLK), :] = total.astype(jnp.bfloat16)
        return carry

    lax.fori_loop(0, long_ref[3 * nquery], long_step, 0)
    dkv_ref[...] = sum_ref[...].astype(jnp.bfloat16)


def local_call(kernel, name, out_shape, nsmem, nvmem, scratch=(), flops=0):
    return pl.pallas_call(
        kernel,
        out_shape=out_shape,
        in_specs=[pl.BlockSpec(memory_space=pltpu.SMEM)] * nsmem
        + [pl.BlockSpec(memory_space=pltpu.VMEM)] * nvmem,
        out_specs=jax.tree.map(lambda _: pl.BlockSpec(memory_space=pltpu.VMEM), out_shape),
        scratch_shapes=list(scratch),
        name=name,
        cost_estimate=pl.CostEstimate(flops=flops, bytes_accessed=8 << 20, transcendentals=0),
        compiler_params=pltpu.CompilerParams(vmem_limit_bytes=56 << 20),
    )


def rows_product(left, right):
    return lax.dot_general(left, right, TN, preferred_element_type=jnp.float32)


def cols_product(left, right):
    return lax.dot_general(left, right, NT, preferred_element_type=jnp.float32)


def spread_heads(weight, heads, upper, axis):
    shape = weight.shape[:axis] + (heads, HEAD_DIM) + weight.shape[axis + 1 :]
    weight = weight.reshape(shape)
    pads = [(0, 0)] * len(shape)
    pads[axis + 1] = (HEAD_DIM, 0) if upper else (0, HEAD_DIM)
    weight = jnp.pad(weight, pads)
    return weight.reshape(shape[:axis] + (heads * WIDE,) + shape[axis + 2 :])


def pair_heads(left, right, heads):
    lead = left.shape[:-1]
    both = jnp.concatenate(
        [left.reshape(lead + (heads, HEAD_DIM)), right.reshape(lead + (heads, HEAD_DIM))], axis=-1
    )
    return both.reshape(lead + (heads * WIDE,))


def on_device(
    hidden_in,
    norm_gain,
    norm_shift,
    query_weight,
    query_bias,
    key_weight,
    value_weight,
    value_bias,
    output_weight,
    output_bias,
    feed_gain,
    feed_shift,
    inner_weight,
    inner_bias,
    outer_weight,
    outer_bias,
    doc_blocks,
    doc_padding,
    random_picks,
    cotangent,
):
    f32, bf16 = jnp.float32, jnp.bfloat16
    nrows, block_len, part_width = hidden_in.shape
    rows = nrows * block_len
    nseq, ntp = lax.axis_size("seq"), lax.axis_size("tp")
    seq_index, tp_index = lax.axis_index("seq"), lax.axis_index("tp")
    local_width = query_weight.shape[1]
    heads = local_width // HEAD_DIM
    share = nseq // heads
    nquery = nrows * heads
    nblocks = nrows * nseq
    tokens_part = rows // ntp
    across = [[h * share + r for h in range(heads)] for r in range(share)]
    within = [[h * share + r for r in range(share)] for h in range(heads)]

    def swap_heads(value):
        width = value.shape[1] // heads
        value = value.reshape(rows, heads, width).swapaxes(0, 1)
        value = lax.all_to_all(value, "seq", 0, 0, axis_index_groups=across, tiled=True)
        return value.reshape(heads * rows, width)

    def swap_back(value):
        width = value.shape[1]
        value = lax.all_to_all(
            value.reshape(heads, rows, width), "seq", 0, 0, axis_index_groups=across, tiled=True
        )
        return value.swapaxes(0, 1).reshape(rows, heads * width)

    tables = attention_tables(
        doc_blocks, doc_padding, random_picks, nrows, nseq, heads, seq_index % share
    )
    x_full = lax.all_gather(hidden_in.reshape(rows, part_width), "tp", axis=1, tiled=True).astype(f32)
    mean1 = jnp.mean(x_full, axis=-1, keepdims=True)
    centered = x_full - mean1
    scale1 = lax.rsqrt(jnp.mean(centered * centered, axis=-1, keepdims=True) + 1e-05)
    h1 = (centered * scale1 * norm_gain + norm_shift).astype(bf16)
    q_wide = (
        (
            jnp.dot(h1, spread_heads(query_weight, heads, False, 1), preferred_element_type=f32)
            + spread_heads(query_bias, heads, False, 0)
        )
        * 0.125
    ).astype(bf16)
    kv_bias = pair_heads(jnp.zeros_like(value_bias), value_bias, heads)
    kv = (
        jnp.dot(h1, pair_heads(key_weight, value_weight, heads), preferred_element_type=f32) + kv_bias
    ).astype(bf16)
    q_head = swap_heads(q_wide)
    kv_head = lax.all_gather(
        swap_heads(kv), "seq", axis=0, axis_index_groups=within, tiled=True
    )
    near_table, long_table, block_table = tables
    res = local_call(
        functools.partial(forward_kernel, nquery, nblocks, 2),
        "attention_forward",
        jax.ShapeDtypeStruct((nquery * BLK, WIDE), f32),
        3,
        2,
    )(near_table, long_table, block_table, q_head, kv_head)
    mixed = swap_back(res[:, HEAD_DIM:].astype(bf16))
    attn_part = jnp.dot(mixed, output_weight, preferred_element_type=f32).astype(bf16)
    attn = lax.psum_scatter(attn_part, "tp", scatter_dimension=0, tiled=True).astype(f32)
    token_start = tp_index * tokens_part
    x_part = lax.dynamic_slice_in_dim(x_full, token_start, tokens_part, 0)
    x1 = x_part + attn + output_bias
    h2_f, feed_pull = jax.vjp(layer_norm, x1, feed_gain, feed_shift)
    h2 = lax.all_gather(h2_f.astype(bf16), "tp", axis=0, tiled=True)
    pre = jnp.dot(h2, inner_weight, preferred_element_type=f32) + inner_bias
    act_f, gelu_pull = jax.vjp(gelu_tanh, pre)
    act = act_f.astype(bf16)
    ffn_part = jnp.dot(act, outer_weight, preferred_element_type=f32)
    own = lax.dynamic_slice_in_dim(ffn_part, token_start, tokens_part, 0) + x1
    ffn_part = lax.dynamic_update_slice_in_dim(ffn_part, own, token_start, 0).astype(bf16)
    result = lax.psum_scatter(ffn_part, "tp", scatter_dimension=1, tiled=True).astype(f32)
    bias_part = lax.dynamic_slice_in_dim(outer_bias, tp_index * part_width, part_width, 0)
    layer_out = (result + bias_part).astype(bf16).reshape(hidden_in.shape)

    cot = cotangent.reshape(rows, part_width)
    grad_out = lax.all_gather(cot, "tp", axis=1, tiled=True)
    grad_outer_bias_part = jnp.sum(cot.astype(f32), axis=0)
    grad_outer_weight = rows_product(act, grad_out)
    grad_act = cols_product(grad_out, outer_weight)
    grad_pre = gelu_pull(grad_act)[0].astype(bf16)
    grad_inner_bias = jnp.sum(grad_pre.astype(f32), axis=0)
    grad_inner_weight = rows_product(h2, grad_pre)
    grad_h2 = lax.psum_scatter(
        cols_product(grad_pre, inner_weight).astype(bf16), "tp", scatter_dimension=0, tiled=True
    ).astype(f32)
    grad_x1_norm, grad_feed_gain, grad_feed_shift = feed_pull(grad_h2)
    grad_out_part = lax.dynamic_slice_in_dim(grad_out, token_start, tokens_part, 0).astype(f32)
    grad_branch_part = (grad_out_part + grad_x1_norm).astype(bf16)
    grad_output_bias = jnp.sum(grad_branch_part.astype(f32), axis=0)
    grad_branch = lax.all_gather(grad_branch_part, "tp", axis=0, tiled=True)
    grad_output_weight = rows_product(mixed, grad_branch)
    do_wide = cols_product(grad_branch, spread_heads(output_weight, heads, True, 0)).astype(bf16)
    do_head = swap_heads(do_wide)
    dq_head, dkv_head = local_call(
        functools.partial(backward_kernel, nquery, nblocks, 2),
        "attention_backward",
        (
            jax.ShapeDtypeStruct((nquery * BLK, WIDE), bf16),
            jax.ShapeDtypeStruct((nblocks * BLK, WIDE), bf16),
        ),
        3,
        4,
        [pltpu.VMEM((nblocks * BLK, WIDE), f32)],
    )(near_table, long_table, block_table, q_head, do_head, res, kv_head)
    dq = swap_back(dq_head[:, :HEAD_DIM])
    dkv = swap_back(
        lax.psum_scatter(
            dkv_head, "seq", scatter_dimension=0, axis_index_groups=within, tiled=True
        )
    )
    split = dkv.reshape(rows, heads, 2, HEAD_DIM)
    dk, dv = (split[:, :, index].reshape(rows, local_width) for index in range(2))
    grad_query_bias = 0.125 * jnp.sum(dq.astype(f32), axis=0)
    grad_value_bias = jnp.sum(dv.astype(f32), axis=0)
    grad_query_weight = 0.125 * rows_product(h1, dq)
    grad_key_weight = rows_product(h1, dk)
    grad_value_weight = rows_product(h1, dv)
    grad_h1_part = (
        0.125 * cols_product(dq, query_weight)
        + cols_product(dk, key_weight)
        + cols_product(dv, value_weight)
    ).astype(bf16)
    grad_h1 = lax.psum_scatter(grad_h1_part, "tp", scatter_dimension=1, tiled=True).astype(f32)
    feature_start = tp_index * part_width
    my_gain = lax.dynamic_slice_in_dim(norm_gain, feature_start, part_width, 0)
    x_mine = hidden_in.reshape(rows, part_width).astype(f32)
    xhat = (x_mine - mean1) * scale1
    grad_hat = grad_h1 * my_gain
    sums = lax.psum(
        jnp.stack([jnp.sum(grad_hat, axis=1), jnp.sum(grad_hat * xhat, axis=1)]), "tp"
    ) * (1.0 / (part_width * ntp))
    grad_x_norm = scale1 * (grad_hat - sums[0][:, None] - xhat * sums[1][:, None])
    grad_x1_mine = lax.dynamic_slice_in_dim(grad_branch, feature_start, part_width, 1).astype(f32)
    grad_input = (grad_x1_mine + grad_x_norm).reshape(hidden_in.shape)

    def scatter_grad(value, dimension):
        return lax.psum_scatter(
            value.astype(bf16), "seq", scatter_dimension=dimension, tiled=True
        ).astype(f32)

    feature_sums = lax.all_gather(
        jnp.stack([jnp.sum(grad_h1 * xhat, axis=0), jnp.sum(grad_h1, axis=0), grad_outer_bias_part]),
        "tp",
        axis=1,
        tiled=True,
    )
    token_sums = lax.psum(jnp.stack([grad_output_bias, grad_feed_gain, grad_feed_shift]), "tp")
    vectors = lax.psum(
        jnp.concatenate(
            [
                feature_sums.reshape(-1),
                token_sums.reshape(-1),
                grad_query_bias,
                grad_value_bias,
                grad_inner_bias,
            ]
        ),
        "seq",
    )
    features = part_width * ntp
    wide = vectors[: 6 * features].reshape(6, features)
    rest = vectors[6 * features :]
    return (
        layer_out,
        grad_input,
        wide[0],
        wide[1],
        scatter_grad(grad_query_weight, 0),
        rest[:local_width],
        scatter_grad(grad_key_weight, 0),
        scatter_grad(grad_value_weight, 0),
        rest[local_width : 2 * local_width],
        scatter_grad(grad_output_weight, 1),
        wide[3],
        wide[4],
        wide[5],
        scatter_grad(grad_inner_weight, 0),
        rest[2 * local_width :],
        scatter_grad(grad_outer_weight, 1),
        wide[2],
    )


def solution(mesh):
    return jax.shard_map(
        on_device,
        mesh=mesh,
        in_specs=(
            P(None, "seq", "tp"),
            P(),
            P(),
            P(None, "tp"),
            P("tp"),
            P(None, "tp"),
            P(None, "tp"),
            P("tp"),
            P("tp", None),
            P(),
            P(),
            P(),
            P(None, "tp"),
            P("tp"),
            P("tp", None),
            P(),
            P(),
            P(),
            P(),
            P(None, "seq", "tp"),
        ),
        out_specs=(
            P(None, "seq", "tp"),
            P(None, "seq", "tp"),
            P(),
            P(),
            P("seq", "tp"),
            P("tp"),
            P("seq", "tp"),
            P("seq", "tp"),
            P("tp"),
            P("tp", "seq"),
            P(),
            P(),
            P(),
            P("seq", "tp"),
            P("tp"),
            P("tp", "seq"),
            P(),
        ),
        check_vma=False,
    )
```

time: 1730 us -> 882 us (0.51)
  local copies, waits for them, and re-layouts: 473 us -> 31.8 us
  matrix products: 272 us -> 63.5 us
  waiting for transfers between devices: 750 us -> 553 us
  other arithmetic: 161 us -> 49.4 us
  Pallas kernels: 0 us -> 59.7 us
  blocking collectives: 24.9 us -> 80.8 us
  loops' own time: 26.2 us -> 0 us
    gather x99 -> x0, local copies, waits for them, and re-layouts: 323 us -> none  [the longest x32 107 us: key_allow(): key_first = jnp.take(first, key_blocks)]
    psum x3 -> x0, waiting for transfers between devices: 323 us -> none  [the longest x1 154 us: on_device(): lax.psum(ffn_part.astype(jnp.bfloat16), 'tp').astype(jnp.float32)]
    dot_general x242 -> x17, matrix products: 272 us -> 63.5 us  [the longest x6 22.2 us: rows_product(): return lax.dot_general(left, right, TN, preferred_element_type=jnp.float32)]
    reduce_scatter x5 -> x9, waiting for transfers between devices: 174 us -> 302 us  [the longest x4 148 us: scatter_grad(): lax.psum_scatter(value.astype(bf16), 'seq', scatter_dimension=dimension,...]
    unnamed x18, waiting for transfers between devices: 109 us -> 37.8 us
    dynamic_slice x81 -> x2, local copies, waits for them, and re-layouts: 68.7 us -> 0.84 us  [the longest x1 0.76 us: on_device(): lax.dynamic_slice_in_dim(outer_bias, tp_index * part_width, part_width, 0)]
    pallas_call x0 -> x2, Pallas kernels: none -> 59.7 us  [the longest x1 31.6 us: on_device(): local_call(functools.partial(backward_kernel, nquery, nblocks, 2), 'atten...]
    all_to_all x0 -> x4, waiting for transfers between devices: none -> 41.8 us  [the longest x2 24.4 us: swap_heads(): lax.all_to_all(value, 'seq', 0, 0, axis_index_groups=across, tiled=True)]
  transfers between devices with their start and end apart: 15 -> 20, of which waited for: 15 -> 17; matrix products, arithmetic and copies ran while one was open for 5% -> 11% of each run, Pallas kernels for 0% -> 0%
where the time goes in v1:
time: 882 us; the launch traced here: 869 us
  waiting for transfers between devices  553 us (63%)
  blocking collectives  80.8 us (9%)
  matrix products  63.5 us (7%)
  Pallas kernels  59.7 us (7%)
  other arithmetic  49.4 us (6%)
  local copies, waits for them, and re-layouts  31.8 us (4%)
  starting transfers between devices  15.3 us (2%)
  between operations  15.1 us (2%)
    reduce_scatter x4, waiting for transfers between devices, scatter_grad(): lax.psum_scatter(value.astype(bf16), 'seq', scatter_dimension=dimension,...  148 us
    all_gather x1, waiting for transfers between devices, on_device(): grad_branch = lax.all_gather(grad_branch_part, 'tp', axis=0, tiled=True)  45.9 us
    all_gather x1, waiting for transfers between devices, on_device(): h2 = lax.all_gather(h2_f.astype(bf16), 'tp', axis=0, tiled=True)  45.4 us
    reduce_scatter x1, waiting for transfers between devices, on_device(): lax.psum_scatter(grad_h1_part, 'tp', scatter_dimension=1, tiled=True)  42.3 us
    reduce_scatter x1, waiting for transfers between devices, on_device(): lax.psum_scatter(ffn_part, 'tp', scatter_dimension=1, tiled=True)  42.2 us
    all_gather x1, waiting for transfers between devices, on_device(): grad_out = lax.all_gather(cot, 'tp', axis=1, tiled=True)  40.3 us
    all_gather x1, waiting for transfers between devices, on_device(): lax.all_gather(hidden_in.reshape(rows, part_width), 'tp', axis=1, tiled=T...  39.8 us
    unnamed x18, waiting for transfers between devices  37.8 us
  transfers between devices with their start and end apart: 20, of which 17 were waited for; matrix products, arithmetic and copies ran while one was open for 11% of the time, Pallas kernels for 0%

profile of v1, /device:TPU:8, one launch (start us, length us, event | category | flops | bytes accessed | tf_op | source)
XLA Modules:
  0.0 869.0 jit_solution(14461192978520849346)
XLA Ops:
  16.0 39.8 %all-gather.6.cloned.1.call-done = bf16[1024,1024]{1,0:T(8,128)(2,1)} async-done(((bf16[1024,256]{1,0:T(8,128)(2,1)}), bf16[1024,1024]{1,0:T(8,128)(2,1)}) %all-gather.6.cloned.1.call-update) | async-done | bytes 2097168 | tf_op jit(solution)/shard_map/all_gather | solution.py:334
  69.3 13.5 %all-to-all-done.1 = bf16[4,1024,128]{2,1,0:T(8,128)(2,1)S(1)} async-done(((bf16[4,1024,128]{2,1,0:T(8,128)(2,1)}), bf16[4,1024,128]{2,1,0:T(8,128)(2,1)S(1)}, u32[]{:S(2)}, u32[]{:S(2)}) %all-to-all-start.1) | async-done | bytes 1048608 | tf_op jit(solution)/shard_map/all_to_all | solution.py:321
  102.1 10.9 %all-to-all-done = bf16[4,1024,128]{2,1,0:T(8,128)(2,1)S(1)} async-done(((bf16[4,1024,128]{2,1,0:T(8,128)(2,1)}), bf16[4,1024,128]{2,1,0:T(8,128)(2,1)S(1)}, u32[]{:S(2)}, u32[]{:S(2)}) %all-to-all-start) | async-done | bytes 1048608 | tf_op jit(solution)/shard_map/all_to_all | solution.py:321
  113.9 28.2 %attention_forward.1.res_ref = f32[4096,128]{1,0:T(8,128)} custom-call(s32[1024]{0:T(1024)} %copy-done.19, s32[193]{0:T(256)} %pad_add_fusion.long_ref, s32[256]{0:T(256)} %pad_add_fusion.1.block_ref, bf16[4096,128]{1,0:T(8,128)(2,1)} %bitcast.114, bf16[8192,128]{1,0:T(8,128)(2,1)} %all-gather.8.cloned.1.call-done.kv_ref), custom_call_target="tpu_custom_call" | custom-call | bytes 8388608 | tf_op jit(solution)/shard_map/attention_forward/pallas_call | solution.py:355
  145.1 11.4 %all_to_all.30 = bf16[4,1024,64]{1,2,0:T(8,128)(2,1)S(1)} all-to-all(bf16[4,1024,64]{1,2,0:T(8,128)(2,1)} %copy.151), channel_id=1, replica_groups={{0,8,16,24},{4,12,20,28},{1,9,17,25},{5,13,21,29},{2,10,18,26},{6,14,22..., dimensions={0} | all-to-all | bytes 1048576 | tf_op jit(solution)/shard_map/all_to_all | solution.py:326
  164.6 36.3 %reduce-scatter.16.cloned.1.call-done = bf16[256,1024]{1,0:T(8,128)(2,1)} async-done(((bf16[1024,1024]{1,0:T(8,128)(2,1)}), bf16[256,1024]{1,0:T(8,128)(2,1)}) %reduce-scatter.16.cloned.1.call-update) | async-done | bytes 524304 | tf_op jit(solution)/shard_map/reduce_scatter | solution.py:364
  204.5 45.4 %all-gather.10.cloned.1.call-done = bf16[1024,1024]{1,0:T(8,128)(2,1)} async-done(((bf16[256,1024]{1,0:T(8,128)(2,1)}), bf16[1024,1024]{1,0:T(8,128)(2,1)}) %all-gather.10.cloned.1.call-update) | async-done | bytes 2097168 | tf_op jit(solution)/shard_map/all_gather | solution.py:369
  256.4 40.3 %all-gather.12.cloned.1.call-done = bf16[1024,1024]{1,0:T(8,128)(2,1)} async-done(((bf16[1024,256]{1,0:T(8,128)(2,1)}), bf16[1024,1024]{1,0:T(8,128)(2,1)}) %all-gather.12.cloned.1.call-update) | async-done | bytes 2097168 | tf_op jit(solution)/shard_map/all_gather | solution.py:381
  296.7 7.5 convert_reduce_fusion
  316.4 34.1 %reduce-scatter.20.cloned.1.call-done = bf16[256,1024]{1,0:T(8,128)(2,1)} async-done(((bf16[1024,1024]{1,0:T(8,128)(2,1)}), bf16[256,1024]{1,0:T(8,128)(2,1)}) %reduce-scatter.20.cloned.1.call-update) | async-done | bytes 524304 | tf_op jit(solution)/shard_map/reduce_scatter | solution.py:388
  356.8 45.9 %all-gather.14.cloned.1.call-done = bf16[1024,1024]{1,0:T(8,128)(2,1)} async-done(((bf16[256,1024]{1,0:T(8,128)(2,1)}), bf16[1024,1024]{1,0:T(8,128)(2,1)}) %all-gather.14.cloned.1.call-update) | async-done | bytes 2097168 | tf_op jit(solution)/shard_map/all_gather | solution.py:395
  406.2 17.4 %all_to_all.31 = bf16[4,1024,128]{2,1,0:T(8,128)(2,1)} all-to-all(bf16[4,1024,128]{2,1,0:T(8,128)(2,1)S(1)} %bitcast.126), channel_id=1, replica_groups={{0,8,16,24},{4,12,20,28},{1,9,17,25},{5,13,21,29},{2,10,18,26},{6,14,22..., dimensions={0} | all-to-all | bytes 2097152 | tf_op jit(solution)/shard_map/all_to_all | solution.py:321
  423.7 31.6 %attention_backward.1 = (bf16[4096,128]{1,0:T(8,128)(2,1)}, bf16[8192,128]{1,0:T(8,128)(2,1)}) custom-call(s32[1024]{0:T(1024)} %copy-done.19, s32[193]{0:T(256)} %pad_add_fusion.long_ref, s32[256]{0:T(256)} %pad_add_fusion.1.block_ref, bf16[4096,128]{1,0:T(8,128)(2,1)} %bitcast.115, bf16[4096,128]{1,0:T(8,128)(2,1)} %bitcast.122, ...), custom_call_target="tpu_custom_call" | custom-call | bytes 8388608 | tf_op jit(solution)/shard_map/attention_backward/pallas_call | solution.py:399
  495.9 13.2 %all-to-all-done.5 = bf16[4,1024,128]{1,2,0:T(8,128)(2,1)S(1)} async-done(((bf16[4,1024,128]{1,2,0:T(8,128)(2,1)}), bf16[4,1024,128]{1,2,0:T(8,128)(2,1)S(1)}, u32[]{:S(2)}, u32[]{:S(2)}) %all-to-all-start.5) | async-done | bytes 1048608 | tf_op jit(solution)/shard_map/all_to_all | solution.py:326
  524.4 39.9 %reduce-scatter.32.cloned.1.call-done = bf16[128,1024]{1,0:T(8,128)(2,1)} async-done(((bf16[1024,1024]{1,0:T(8,128)(2,1)}), bf16[128,1024]{1,0:T(8,128)(2,1)}) %reduce-scatter.32.cloned.1.call-update) | async-done | bytes 262160 | tf_op jit(solution)/shard_map/reduce_scatter | solution.py:442
  566.1 36.3 %reduce-scatter.34.cloned.1.call-done = bf16[128,256]{1,0:T(8,128)(2,1)} async-done(((bf16[1024,256]{1,0:T(8,128)(2,1)}), bf16[128,256]{1,0:T(8,128)(2,1)}) %reduce-scatter.34.cloned.1.call-update) | async-done | bytes 65552
  604.0 42.2 %reduce-scatter.18.cloned.1.call-done = bf16[1024,256]{1,0:T(8,128)(2,1)} async-done(((bf16[1024,1024]{1,0:T(8,128)(2,1)}), bf16[1024,256]{1,0:T(8,128)(2,1)}) %reduce-scatter.18.cloned.1.call-update) | async-done | bytes 524304 | tf_op jit(solution)/shard_map/reduce_scatter | solution.py:376
  649.4 35.9 %reduce-scatter.26.cloned.1.call-done = bf16[128,256]{1,0:T(8,128)(2,1)} async-done(((bf16[1024,256]{1,0:T(8,128)(2,1)}), bf16[128,256]{1,0:T(8,128)(2,1)}) %reduce-scatter.26.cloned.1.call-update) | async-done | bytes 65552 | tf_op jit(solution)/shard_map/reduce_scatter | solution.py:442
  687.0 35.9 %reduce-scatter.28.cloned.1.call-done = bf16[128,256]{1,0:T(8,128)(2,1)} async-done(((bf16[1024,256]{1,0:T(8,128)(2,1)}), bf16[128,256]{1,0:T(8,128)(2,1)}) %reduce-scatter.28.cloned.1.call-update) | async-done | bytes 65552 | tf_op jit(solution)/shard_map/reduce_scatter | solution.py:442
  724.4 35.9 %reduce-scatter.30.cloned.1.call-done = bf16[128,256]{1,0:T(8,128)(2,1)} async-done(((bf16[1024,256]{1,0:T(8,128)(2,1)}), bf16[128,256]{1,0:T(8,128)(2,1)}) %reduce-scatter.30.cloned.1.call-update) | async-done | bytes 65552 | tf_op jit(solution)/shard_map/reduce_scatter | solution.py:442
  761.8 42.3 %reduce-scatter.24.cloned.1.call-done = bf16[1024,256]{1,0:T(8,128)(2,1)} async-done(((bf16[1024,1024]{1,0:T(8,128)(2,1)}), bf16[1024,256]{1,0:T(8,128)(2,1)}) %reduce-scatter.24.cloned.1.call-update) | async-done | bytes 524304 | tf_op jit(solution)/shard_map/reduce_scatter | solution.py:428
  806.0 13.6 %all_gather.23 = f32[3,1024]{1,0:T(4,128)S(1)} all-gather(f32[3,256]{1,0:T(4,128)S(1)} %pad_maximum_fusion.3), channel_id=1, replica_groups=mesh['seq'=8,'tp'=4] {'tp'}, dimensions={1}, use_global_device_ids=true | all-gather | bytes 15360 | tf_op jit(solution)/shard_map/all_gather | solution.py:446
  819.6 16.0 %all-reduce.4 = (f32[2,1024]{1,0:T(2,128)S(1)}, f32[3072]{0:T(1024)S(1)}) all-reduce(f32[2,1024]{1,0:T(2,128)S(1)} %pad_maximum_fusion.2, f32[3072]{0:T(1024)S(1)} %reshape.870), channel_id=1, replica_groups=mesh['seq'=8,'tp'=4] {'tp'}, use_global_device_ids=true, to_apply=%region_28.29 | all-reduce | flops 5120 | bytes 40960 | tf_op jit(solution)/shard_map/psum | solution.py:434
  835.7 22.4 %psum.23 = f32[7680]{0:T(1024)S(1)} all-reduce(f32[7680]{0:T(1024)S(1)} %constant_dynamic-update-slice_fusion.3), channel_id=1, replica_groups=mesh['seq'=8,'tp'=4] {'seq'}, use_global_device_ids=true, to_apply=%region_39.40 | all-reduce | flops 7680 | bytes 61440 | tf_op jit(solution)/shard_map/psum | solution.py:453
  (233 shorter events, 158.2 us)
Async XLA Ops:
  7.2 289.5 %copy-start = (bf16[1024,1024]{1,0:T(8,128)(2,1)S(1)}, bf16[1024,1024]{1,0:T(8,128)(2,1)}, u32[]{:S(2)}) copy-start(bf16[1024,1024]{1,0:T(8,128)(2,1)} %param.34) | copy-start | bytes 6291460
  7.2 48.5 %all-gather.6.cloned.1.call-start = ((), (), s32[]{:S(2)}) async-start(), calls=%async_computation.17 | async-start | bytes 2621440 | tf_op jit(solution)/shard_map/all_gather | solution.py:334
  11.4 48.7 %copy-start.20 = (f32[1024]{0:T(1024)S(1)}, f32[1024]{0:T(1024)}, u32[]{:S(2)}) copy-start(f32[1024]{0:T(1024)} %param.21) | copy-start | bytes 12292
  65.6 17.2 %all-to-all-start.1 = ((bf16[4,1024,128]{2,1,0:T(8,128)(2,1)}), bf16[4,1024,128]{2,1,0:T(8,128)(2,1)S(1)}, u32[]{:S(2)}, u32[]{:S(2)}) async-start(bf16[4,1024,128]{2,1,0:T(8,128)(2,1)} %bitcast.125), calls=%async_computation.1 | async-start | bytes 2097152 | tf_op jit(solution)/shard_map/all_to_all | solution.py:321
  69.1 43.9 %all-gather.8.cloned.1.call-start = ((), (), s32[]{:S(2)}) async-start(), calls=%async_computation.18 | async-start | bytes 3145728 | tf_op jit(solution)/shard_map/all_gather | solution.py:351
  96.2 16.8 %all-to-all-start = ((bf16[4,1024,128]{2,1,0:T(8,128)(2,1)}), bf16[4,1024,128]{2,1,0:T(8,128)(2,1)S(1)}, u32[]{:S(2)}, u32[]{:S(2)}) async-start(bf16[4,1024,128]{2,1,0:T(8,128)(2,1)} %bitcast.124), calls=%async_computation | async-start | bytes 2097152 | tf_op jit(solution)/shard_map/all_to_all | solution.py:321
  99.7 101.2 %reduce-scatter.16.cloned.1.call-start = ((), (), s32[]{:S(2)}) async-start(), calls=%async_computation.19 | async-start | bytes 2621440 | tf_op jit(solution)/shard_map/reduce_scatter | solution.py:364
  160.5 89.4 %all-gather.10.cloned.1.call-start = ((), (), s32[]{:S(2)}) async-start(), calls=%async_computation.20 | async-start | bytes 2621440 | tf_op jit(solution)/shard_map/all_gather | solution.py:369
  203.9 92.8 %all-gather.12.cloned.1.call-start = ((), (), s32[]{:S(2)}) async-start(), calls=%async_computation.22 | async-start | bytes 2621440 | tf_op jit(solution)/shard_map/all_gather | solution.py:381
  204.5 92.3 %copy-start.26 = (f32[1024]{0:T(1024)S(1)}, f32[1024]{0:T(1024)}, u32[]{:S(2)}) copy-start(f32[1024]{0:T(1024)} %param.33) | copy-start | bytes 12292
  204.5 146.0 %reduce-scatter.20.cloned.1.call-start = ((), (), s32[]{:S(2)}) async-start(), calls=%async_computation.23 | async-start | bytes 2621440 | tf_op jit(solution)/shard_map/reduce_scatter | solution.py:388
  309.2 93.5 %all-gather.14.cloned.1.call-start = ((), (), s32[]{:S(2)}) async-start(), calls=%async_computation.24 | async-start | bytes 2621440 | tf_op jit(solution)/shard_map/all_gather | solution.py:395
  356.6 125.9 %reduce-scatter.22.cloned.1.call-start = ((), (), s32[]{:S(2)}) async-start(), calls=%async_computation.25 | async-start | bytes 3145728 | tf_op jit(solution)/shard_map/reduce_scatter | solution.py:412
  455.3 67.0 %reduce-scatter.36.cloned.1.call-start = ((), (), s32[]{:S(2)}) async-start(), calls=%async_computation.32 | async-start | bytes 2359296
  463.9 100.4 %reduce-scatter.32.cloned.1.call-start = ((), (), s32[]{:S(2)}) async-start(), calls=%async_computation.30 | async-start | bytes 2359296 | tf_op jit(solution)/shard_map/reduce_scatter | solution.py:442
  470.0 132.3 %reduce-scatter.34.cloned.1.call-start = ((), (), s32[]{:S(2)}) async-start(), calls=%async_computation.31 | async-start | bytes 589824
  473.7 172.5 %reduce-scatter.18.cloned.1.call-start = ((), (), s32[]{:S(2)}) async-start(), calls=%async_computation.21 | async-start | bytes 2621440 | tf_op jit(solution)/shard_map/reduce_scatter | solution.py:376
  479.0 10.0 %all-to-all-start.4 = ((bf16[4,1024,64]{1,2,0:T(8,128)(2,1)}), bf16[4,1024,64]{1,2,0:T(8,128)(2,1)S(1)}, u32[]{:S(2)}, u32[]{:S(2)}) async-start(bf16[4,1024,64]{1,2,0:T(8,128)(2,1)} %copy.153), calls=%async_computation.7 | async-start | bytes 1048576 | tf_op jit(solution)/shard_map/all_to_all | solution.py:326
  489.0 20.0 %all-to-all-start.5 = ((bf16[4,1024,128]{1,2,0:T(8,128)(2,1)}), bf16[4,1024,128]{1,2,0:T(8,128)(2,1)S(1)}, u32[]{:S(2)}, u32[]{:S(2)}) async-start(bf16[4,1024,128]{1,2,0:T(8,128)(2,1)} %copy.154), calls=%async_computation.9 | async-start | bytes 2097152 | tf_op jit(solution)/shard_map/all_to_all | solution.py:326
  492.6 192.7 %reduce-scatter.26.cloned.1.call-start = ((), (), s32[]{:S(2)}) async-start(), calls=%async_computation.27 | async-start | bytes 589824 | tf_op jit(solution)/shard_map/reduce_scatter | solution.py:442
  495.8 227.1 %reduce-scatter.28.cloned.1.call-start = ((), (), s32[]{:S(2)}) async-start(), calls=%async_computation.28 | async-start | bytes 589824 | tf_op jit(solution)/shard_map/reduce_scatter | solution.py:442
  512.3 248.0 %reduce-scatter.30.cloned.1.call-start = ((), (), s32[]{:S(2)}) async-start(), calls=%async_computation.29 | async-start | bytes 589824 | tf_op jit(solution)/shard_map/reduce_scatter | solution.py:442
  516.7 287.4 %reduce-scatter.24.cloned.1.call-start = ((), (), s32[]{:S(2)}) async-start(), calls=%async_computation.26 | async-start | bytes 2621440 | tf_op jit(solution)/shard_map/reduce_scatter | solution.py:428
  522.2 339.8 %copy-start.1 = (bf16[1024,1024]{1,0:T(8,128)(2,1)S(1)}, bf16[1024,1024]{1,0:T(8,128)(2,1)}, u32[]{:S(2)}) copy-start(bf16[1024,1024]{1,0:T(8,128)(2,1)} %param.34) | copy-start | bytes 6291460
  (24 other events, 372.2 us)
Sparse Core Ops, SparseCore 0:
  9.6 46.0 all-gather.5
  83.9 9.8 all-gather.7
  160.6 40.2 reduce-scatter.15
  204.0 45.8 all-gather.9
  251.4 45.2 all-gather.11
  309.3 41.1 reduce-scatter.19
  356.7 45.9 all-gather.13
  455.4 9.1 reduce-scatter.21
  468.3 51.5 reduce-scatter.35
  523.0 41.1 reduce-scatter.31
  568.2 34.1 reduce-scatter.33
  604.5 41.6 reduce-scatter.17
  649.5 35.6 reduce-scatter.25
  688.8 34.1 reduce-scatter.27
  726.1 34.1 reduce-scatter.29
  762.5 41.5 reduce-scatter.23

commit v2 on v1

--- a/solution.py
+++ b/solution.py
@@ -254,6 +254,419 @@
     )
 
 
+MESH = pl.DeviceIdType.MESH
+CHUNKS = 4
+
+
+def remote(src, dst, send_sem, recv_sem, device):
+    return pltpu.make_async_remote_copy(
+        src_ref=src, dst_ref=dst, send_sem=send_sem, recv_sem=recv_sem,
+        device_id=device, device_id_type=MESH,
+    )
+
+
+def greet(seq, tp, nseq, ntp):
+    barrier = pltpu.get_barrier_semaphore()
+    for step in range(1, nseq):
+        peer = (lax.rem(seq + step, nseq), tp)
+        pl.semaphore_signal(barrier, inc=1, device_id=peer, device_id_type=MESH)
+    for step in range(1, ntp):
+        peer = (seq, lax.rem(tp + step, ntp))
+        pl.semaphore_signal(barrier, inc=1, device_id=peer, device_id_type=MESH)
+    pl.semaphore_wait(barrier, nseq + ntp - 2)
+
+
+def add_bf16(*terms):
+    total = terms[0].astype(jnp.float32)
+    for term in terms[1:]:
+        total = total + term.astype(jnp.float32)
+    return total
+
+
+class GradScatter:
+    def __init__(self, dims, place, source, land, pair, far, sems):
+        self.heads, self.share, self.nseq = dims
+        self.seq, self.tp, self.head, self.part = place
+        self.source, self.land, self.pair, self.far = source, land, pair, far
+        self.send1, self.recv1, self.send2, self.recv2 = sems
+
+    def near(self, step):
+        other = lax.rem(self.part + step, self.share)
+        return remote(
+            self.source.at[:, other], self.land.at[step - 1],
+            self.send1.at[step - 1], self.recv1.at[step - 1],
+            (self.head * self.share + other, self.tp),
+        )
+
+    def across(self, step):
+        other = lax.rem(self.head + step, self.heads)
+        return remote(
+            self.pair.at[other], self.far.at[step - 1],
+            self.send2.at[step - 1], self.recv2.at[step - 1],
+            (other * self.share + self.part, self.tp),
+        )
+
+    def start_near(self):
+        for step in range(1, self.share):
+            self.near(step).start()
+
+    def start_across(self):
+        for step in range(1, self.share):
+            self.near(step).wait_recv()
+
+        def body(head, carry):
+            parts = [self.source[head, self.part]]
+            parts += [self.land[step, head] for step in range(self.share - 1)]
+            self.pair[head] = add_bf16(*parts).astype(jnp.bfloat16)
+            return carry
+
+        lax.fori_loop(0, self.heads, body, 0)
+        for step in range(1, self.heads):
+            self.across(step).start()
+
+    def result(self):
+        for step in range(1, self.heads):
+            self.across(step).wait_recv()
+        parts = [self.pair[self.head]] + [self.far[step] for step in range(self.heads - 1)]
+        return add_bf16(*parts)
+
+    def finish(self):
+        for step in range(1, self.share):
+            self.near(step).wait_send()
+        for step in range(1, self.heads):
+            self.across(step).wait_send()
+
+
+def tail_kernel(
+    dims,
+    dq_ref, dkv_ref, h1_ref, x_ref, stat_ref, gain_ref, wq_ref, wkv_ref, da_ref,
+    gi_ref, gu_ref, gw_ref, vec_ref,
+    gx_ref, oi_ref, ou_ref, ow_ref, oq_ref, okv_ref, vout_ref,
+    dq_in, dkv_in, dkv_land, dkv_sum, pbuf, from_left, from_right,
+    sums, sums_land, vbuf, vec_land, vsum, vec_far, gq, gkv,
+    *rest,
+):
+    heads, share, nseq, ntp = dims
+    lands, sems = rest[:15], rest[15:]
+    rows, features = h1_ref.shape
+    part_width = features // ntp
+    chunk_rows = rows // CHUNKS
+    seq, tp = lax.axis_index("seq"), lax.axis_index("tp")
+    head, part = seq // share, lax.rem(seq, share)
+    place = (seq, tp, head, part)
+    (dq_s, dq_r, kv1_s, kv1_r, kv2_s, kv2_r, right_s, right_r, left_s, left_r,
+     st_s, st_r, v1_s, v1_r, v2_s, v2_r, g1_s, g1_r, g2_s, g2_r) = sems
+    f32, bf16 = jnp.float32, jnp.bfloat16
+
+    def chunk_of(chunk):
+        return pl.ds(chunk * chunk_rows, chunk_rows)
+
+    scatters = [
+        GradScatter(
+            (heads, share, nseq), place, source, *lands[3 * k : 3 * k + 3],
+            (g1_s.at[k], g1_r.at[k], g2_s.at[k], g2_r.at[k]),
+        )
+        for k, source in enumerate((gi_ref, gu_ref, gw_ref, gq, gkv))
+    ]
+
+    def dq_copy(chunk, step):
+        other = lax.rem(head + step, heads)
+        return remote(
+            dq_ref.at[other, chunk_of(chunk)], dq_in.at[head, chunk_of(chunk)],
+            dq_s.at[chunk, step - 1], dq_r.at[chunk, step - 1], (other * share + part, tp),
+        )
+
+    def dkv_near(step):
+        other = lax.rem(part + step, share)
+        return remote(
+            dkv_ref.at[other], dkv_land.at[step - 1], kv1_s.at[step - 1], kv1_r.at[step - 1],
+            (head * share + other, tp),
+        )
+
+    def dkv_copy(chunk, step):
+        other = lax.rem(head + step, heads)
+        return remote(
+            dkv_sum.at[other, chunk_of(chunk)], dkv_in.at[head, chunk_of(chunk)],
+            kv2_s.at[chunk, step - 1], kv2_r.at[chunk, step - 1], (other * share + part, tp),
+        )
+
+    def rightward(chunk, index):
+        return remote(
+            pbuf.at[chunk, index], from_left.at[chunk, index],
+            right_s.at[chunk, index], right_r.at[chunk, index], (seq, tp + 1),
+        )
+
+    def leftward(chunk, index):
+        return remote(
+            pbuf.at[chunk, index], from_right.at[chunk, index],
+            left_s.at[chunk, index], left_r.at[chunk, index], (seq, tp - 1),
+        )
+
+    def sums_copy(step):
+        return remote(
+            sums, sums_land.at[step - 1], st_s.at[step - 1], st_r.at[step - 1],
+            (seq, lax.rem(tp + step, ntp)),
+        )
+
+    def vec_copy(step):
+        return remote(
+            vbuf, vec_land.at[step - 1], v1_s.at[step - 1], v1_r.at[step - 1],
+            (lax.rem(seq + step, nseq), tp),
+        )
+
+    def vec_far_copy(step):
+        return remote(
+            vsum, vec_far.at[step - 1], v2_s.at[step - 1], v2_r.at[step - 1],
+            (seq, lax.rem(tp + step, ntp)),
+        )
+
+    greet(seq, tp, nseq, ntp)
+    for step in range(1, share):
+        dkv_near(step).start()
+    for chunk in range(CHUNKS):
+        for step in range(1, heads):
+            dq_copy(chunk, step).start()
+    for scatter in scatters[:3]:
+        scatter.start_near()
+    dq_in[head] = dq_ref[head]
+    for step in range(1, share):
+        dkv_near(step).wait_recv()
+    for chunk in range(CHUNKS):
+        for target in range(heads):
+            where = (target, chunk_of(chunk))
+            parts = [dkv_ref[(part,) + where]]
+            parts += [dkv_land[(step,) + where] for step in range(share - 1)]
+            dkv_sum[where] = add_bf16(*parts).astype(bf16)
+        for step in range(1, heads):
+            dkv_copy(chunk, step).start()
+    dkv_in[head] = dkv_sum[head]
+    for scatter in scatters[:3]:
+        scatter.start_across()
+
+    vbuf[...] = vec_ref[...]
+    gain = gain_ref[...]
+    lane = lax.broadcasted_iota(jnp.int32, (chunk_rows, WIDE), 1)
+    per = features // WIDE
+
+    def partial_step(chunk):
+        here = chunk_of(chunk)
+        for step in range(1, heads):
+            dq_copy(chunk, step).wait_recv()
+            dkv_copy(chunk, step).wait_recv()
+        dq = jnp.concatenate([dq_in[index, here] for index in range(heads)], axis=1)
+        dkv = jnp.concatenate([dkv_in[index, here] for index in range(heads)], axis=1)
+        grad = lax.dot_general(dq, wq_ref[...], NT, preferred_element_type=f32)
+        grad = grad + lax.dot_general(dkv, wkv_ref[...], NT, preferred_element_type=f32)
+        mean, scale = stat_ref[here, 0:1], stat_ref[here, 1:2]
+        sum0 = jnp.zeros((chunk_rows, 1), f32)
+        sum1 = jnp.zeros((chunk_rows, 1), f32)
+        for index in range(ntp):
+            cols = slice(index * part_width, (index + 1) * part_width)
+            piece = grad[:, cols]
+            xhat = (x_ref[index, here].astype(f32) - mean) * scale
+            weighted = piece * gain[:, cols]
+            product = piece * xhat
+            sum0 = sum0 + jnp.sum(weighted, axis=1, keepdims=True)
+            sum1 = sum1 + jnp.sum(weighted * xhat, axis=1, keepdims=True)
+            col0 = jnp.sum(product, axis=0, keepdims=True)
+            col1 = jnp.sum(piece, axis=0, keepdims=True)
+            for sub in range(part_width // WIDE):
+                row = index * (part_width // WIDE) + sub
+                lanes = slice(sub * WIDE, (sub + 1) * WIDE)
+                vbuf[row : row + 1, :] += col0[:, lanes]
+                vbuf[per + row : per + row + 1, :] += col1[:, lanes]
+            pbuf[chunk, index] = piece.astype(bf16)
+        both = jnp.where(lane == 0, sum0, jnp.where(lane == 1, sum1, 0.0))
+        sums[:, here] = both.T[:8]
+        base = 6 * per
+        for index in range(heads):
+            lanes = slice(index * WIDE, (index + 1) * WIDE)
+            vbuf[base + index : base + index + 1, :] += jnp.sum(
+                dq[:, lanes].astype(f32), axis=0, keepdims=True
+            )
+            vbuf[base + heads + index : base + heads + index + 1, :] += jnp.sum(
+                dkv[:, lanes].astype(f32), axis=0, keepdims=True
+            )
+
+    def pass_on(chunk):
+        for step in range(ntp - 1):
+            far = ntp - 1 - step
+
+            @pl.when(tp < far)
+            def _():
+                @pl.when(tp > 0)
+                def _():
+                    rightward(chunk, far).wait_recv()
+                    pbuf[chunk, far] = add_bf16(pbuf[chunk, far], from_left[chunk, far]).astype(bf16)
+
+                rightward(chunk, far).start()
+
+            @pl.when(tp > step)
+            def _():
+                @pl.when(tp < ntp - 1)
+                def _():
+                    leftward(chunk, step).wait_recv()
+                    pbuf[chunk, step] = add_bf16(pbuf[chunk, step], from_right[chunk, step]).astype(bf16)
+
+                leftward(chunk, step).start()
+
+    for chunk in range(CHUNKS):
+        partial_step(chunk)
+        if chunk > 0:
+            pass_on(chunk - 1)
+    for step in range(1, ntp):
+        sums_copy(step).start()
+    for step in range(1, nseq):
+        vec_copy(step).start()
+
+    halves = [dq_in[index][:, :HEAD_DIM] for index in range(heads)]
+    dq_all = jnp.concatenate(halves, axis=1)
+    dkv_all = jnp.concatenate([dkv_in[index] for index in range(heads)], axis=1)
+    band = features // heads
+
+    def grad_step(index, carry):
+        left = h1_ref[:, pl.ds(pl.multiple_of(index * band, band), band)]
+        shape = (share, band // share, -1)
+        gq[index] = (
+            0.125 * lax.dot_general(left, dq_all, TN, preferred_element_type=f32)
+        ).astype(bf16).reshape(shape)
+        gkv[index] = lax.dot_general(left, dkv_all, TN, preferred_element_type=f32).astype(
+            bf16
+        ).reshape(shape)
+        return carry
+
+    lax.fori_loop(0, heads, grad_step, 0)
+    for scatter in scatters[3:]:
+        scatter.start_near()
+    pass_on(CHUNKS - 1)
+    for step in range(1, nseq):
+        vec_copy(step).wait_recv()
+    total = vbuf[...]
+    for step in range(nseq - 1):
+        total = total + vec_land[step]
+    vsum[...] = total
+    for step in range(1, ntp):
+        vec_far_copy(step).start()
+    for scatter in scatters[3:]:
+        scatter.start_across()
+
+    for step in range(1, ntp):
+        sums_copy(step).wait_recv()
+    my_gain = gain_ref[:, pl.ds(pl.multiple_of(tp * part_width, part_width), part_width)]
+    for chunk in range(CHUNKS):
+        here = chunk_of(chunk)
+        both = sums[:, here]
+        for step in range(ntp - 1):
+            both = both + sums_land[step, :, here]
+        both = jnp.concatenate([both, jnp.zeros((WIDE - 8, chunk_rows), f32)], axis=0).T
+        both = both * (1.0 / features)
+
+        @pl.when(tp > 0)
+        def _():
+            rightward(chunk, tp).wait_recv()
+
+        @pl.when(tp < ntp - 1)
+        def _():
+            leftward(chunk, tp).wait_recv()
+
+        grad = pbuf[chunk, tp].astype(f32)
+        grad = grad + jnp.where(tp > 0, from_left[chunk, tp].astype(f32), 0.0)
+        grad = grad + jnp.where(tp < ntp - 1, from_right[chunk, tp].astype(f32), 0.0)
+        mean, scale = stat_ref[here, 0:1], stat_ref[here, 1:2]
+        xhat = (x_ref[tp, here].astype(f32) - mean) * scale
+        inner = grad * my_gain - both[:, 0:1] - xhat * both[:, 1:2]
+        gx_ref[here] = da_ref[here].astype(f32) + scale * inner
+    for scatter, out in zip(scatters, (oi_ref, ou_ref, ow_ref, oq_ref, okv_ref)):
+        out[...] = scatter.result()
+    for step in range(1, ntp):
+        vec_far_copy(step).wait_recv()
+    vout_ref[...] = vsum[...]
+    for step in range(ntp - 1):
+        vout_ref[: 6 * per] += vec_far[step, : 6 * per]
+
+    for step in range(1, share):
+        dkv_near(step).wait_send()
+    for chunk in range(CHUNKS):
+        for step in range(1, heads):
+            dq_copy(chunk, step).wait_send()
+            dkv_copy(chunk, step).wait_send()
+        for index in range(ntp):
+            @pl.when(tp < index)
+            def _():
+                rightward(chunk, index).wait_send()
+
+            @pl.when(tp > index)
+            def _():
+                leftward(chunk, index).wait_send()
+
+    for step in range(1, ntp):
+        sums_copy(step).wait_send()
+        vec_far_copy(step).wait_send()
+    for step in range(1, nseq):
+        vec_copy(step).wait_send()
+    for scatter in scatters:
+        scatter.finish()
+
+
+def run_tail(dims, dq, dkv, h1, x_parts, stats, gain, wq, wkv, da, grads, vec):
+    heads, share, nseq, ntp = dims
+    f32, bf16 = jnp.float32, jnp.bfloat16
+    rows, features = h1.shape
+    width = features // ntp
+    band = features // nseq
+    columns = [grad.shape[-1] for grad in grads] + [heads * HEAD_DIM, heads * WIDE]
+    sds = jax.ShapeDtypeStruct
+    outs = (
+        [sds((rows, width), f32)]
+        + [sds((band, cols), f32) for cols in columns]
+        + [sds(vec.shape, f32)]
+    )
+    lands = []
+    for cols in columns:
+        lands += [
+            pltpu.VMEM((max(share - 1, 1), heads, band, cols), bf16),
+            pltpu.VMEM((heads, band, cols), bf16),
+            pltpu.VMEM((max(heads - 1, 1), band, cols), bf16),
+        ]
+    pieces = (CHUNKS, ntp, rows // CHUNKS, width)
+    scratch = [
+        pltpu.VMEM((heads, rows, WIDE), bf16),
+        pltpu.VMEM((heads, rows, WIDE), bf16),
+        pltpu.VMEM((max(share - 1, 1), heads, rows, WIDE), bf16),
+        pltpu.VMEM((heads, rows, WIDE), bf16),
+        pltpu.VMEM(pieces, bf16),
+        pltpu.VMEM(pieces, bf16),
+        pltpu.VMEM(pieces, bf16),
+        pltpu.VMEM((8, rows), f32),
+        pltpu.VMEM((ntp - 1, 8, rows), f32),
+        pltpu.VMEM(vec.shape, f32),
+        pltpu.VMEM((nseq - 1,) + vec.shape, f32),
+        pltpu.VMEM(vec.shape, f32),
+        pltpu.VMEM((ntp - 1,) + vec.shape, f32),
+        pltpu.VMEM((heads, share, band, columns[3]), bf16),
+        pltpu.VMEM((heads, share, band, columns[4]), bf16),
+        *lands,
+    ]
+    dma = lambda *shape: pltpu.SemaphoreType.DMA(tuple(max(size, 1) for size in shape))
+    sems = (
+        [dma(CHUNKS, heads - 1)] * 2 + [dma(share - 1)] * 2 + [dma(CHUNKS, heads - 1)] * 2
+        + [dma(CHUNKS, ntp)] * 4 + [dma(ntp - 1)] * 2 + [dma(nseq - 1)] * 2 + [dma(ntp - 1)] * 2
+        + [dma(5, share - 1)] * 2 + [dma(5, heads - 1)] * 2
+    )
+    operands = (dq, dkv, h1, x_parts, stats, gain, wq, wkv, da, *grads, vec)
+    return pl.pallas_call(
+        functools.partial(tail_kernel, dims),
+        out_shape=outs,
+        in_specs=[pl.BlockSpec(memory_space=pltpu.VMEM)] * len(operands),
+        out_specs=[pl.BlockSpec(memory_space=pltpu.VMEM)] * len(outs),
+        scratch_shapes=scratch + sems,
+        name="tail",
+        compiler_params=pltpu.CompilerParams(
+            collective_id=3, has_side_effects=True, vmem_limit_bytes=60 << 20
+        ),
+    )(*operands)
+
+
 def rows_product(left, right):
     return lax.dot_general(left, right, TN, preferred_element_type=jnp.float32)
 
@@ -331,7 +744,8 @@
     tables = attention_tables(
         doc_blocks, doc_padding, random_picks, nrows, nseq, heads, seq_index % share
     )
-    x_full = lax.all_gather(hidden_in.reshape(rows, part_width), "tp", axis=1, tiled=True).astype(f32)
+    x_parts = lax.all_gather(hidden_in.reshape(rows, part_width), "tp", axis=0)
+    x_full = x_parts.swapaxes(0, 1).reshape(rows, ntp * part_width).astype(f32)
     mean1 = jnp.mean(x_full, axis=-1, keepdims=True)
     centered = x_full - mean1
     scale1 = lax.rsqrt(jnp.mean(centered * centered, axis=-1, keepdims=True) + 1e-05)
@@ -380,7 +794,7 @@
     cot = cotangent.reshape(rows, part_width)
     grad_out = lax.all_gather(cot, "tp", axis=1, tiled=True)
     grad_outer_bias_part = jnp.sum(cot.astype(f32), axis=0)
-    grad_outer_weight = rows_product(act, grad_out)
+    grad_outer_weight = rows_product(grad_out, act)
     grad_act = cols_product(grad_out, outer_weight)
     grad_pre = gelu_pull(grad_act)[0].astype(bf16)
     grad_inner_bias = jnp.sum(grad_pre.astype(f32), axis=0)
@@ -393,7 +807,7 @@
     grad_branch_part = (grad_out_part + grad_x1_norm).astype(bf16)
     grad_output_bias = jnp.sum(grad_branch_part.astype(f32), axis=0)
     grad_branch = lax.all_gather(grad_branch_part, "tp", axis=0, tiled=True)
-    grad_output_weight = rows_product(mixed, grad_branch)
+    grad_output_weight = rows_product(grad_branch, mixed)
     do_wide = cols_product(grad_branch, spread_heads(output_weight, heads, True, 0)).astype(bf16)
     do_head = swap_heads(do_wide)
     dq_head, dkv_head = local_call(
@@ -407,82 +821,65 @@
         4,
         [pltpu.VMEM((nblocks * BLK, WIDE), f32)],
     )(near_table, long_table, block_table, q_head, do_head, res, kv_head)
-    dq = swap_back(dq_head[:, :HEAD_DIM])
-    dkv = swap_back(
-        lax.psum_scatter(
-            dkv_head, "seq", scatter_dimension=0, axis_index_groups=within, tiled=True
-        )
-    )
-    split = dkv.reshape(rows, heads, 2, HEAD_DIM)
-    dk, dv = (split[:, :, index].reshape(rows, local_width) for index in range(2))
-    grad_query_bias = 0.125 * jnp.sum(dq.astype(f32), axis=0)
-    grad_value_bias = jnp.sum(dv.astype(f32), axis=0)
-    grad_query_weight = 0.125 * rows_product(h1, dq)
-    grad_key_weight = rows_product(h1, dk)
-    grad_value_weight = rows_product(h1, dv)
-    grad_h1_part = (
-        0.125 * cols_product(dq, query_weight)
-        + cols_product(dk, key_weight)
-        + cols_product(dv, value_weight)
-    ).astype(bf16)
-    grad_h1 = lax.psum_scatter(grad_h1_part, "tp", scatter_dimension=1, tiled=True).astype(f32)
     feature_start = tp_index * part_width
-    my_gain = lax.dynamic_slice_in_dim(norm_gain, feature_start, part_width, 0)
-    x_mine = hidden_in.reshape(rows, part_width).astype(f32)
-    xhat = (x_mine - mean1) * scale1
-    grad_hat = grad_h1 * my_gain
-    sums = lax.psum(
-        jnp.stack([jnp.sum(grad_hat, axis=1), jnp.sum(grad_hat * xhat, axis=1)]), "tp"
-    ) * (1.0 / (part_width * ntp))
-    grad_x_norm = scale1 * (grad_hat - sums[0][:, None] - xhat * sums[1][:, None])
-    grad_x1_mine = lax.dynamic_slice_in_dim(grad_branch, feature_start, part_width, 1).astype(f32)
-    grad_input = (grad_x1_mine + grad_x_norm).reshape(hidden_in.shape)
-
-    def scatter_grad(value, dimension):
-        return lax.psum_scatter(
-            value.astype(bf16), "seq", scatter_dimension=dimension, tiled=True
-        ).astype(f32)
-
-    feature_sums = lax.all_gather(
-        jnp.stack([jnp.sum(grad_h1 * xhat, axis=0), jnp.sum(grad_h1, axis=0), grad_outer_bias_part]),
-        "tp",
-        axis=1,
-        tiled=True,
-    )
-    token_sums = lax.psum(jnp.stack([grad_output_bias, grad_feed_gain, grad_feed_shift]), "tp")
-    vectors = lax.psum(
-        jnp.concatenate(
-            [
-                feature_sums.reshape(-1),
-                token_sums.reshape(-1),
-                grad_query_bias,
-                grad_value_bias,
-                grad_inner_bias,
-            ]
-        ),
-        "seq",
-    )
-    features = part_width * ntp
-    wide = vectors[: 6 * features].reshape(6, features)
-    rest = vectors[6 * features :]
+    per = part_width * ntp // WIDE
+    spread = lambda item: item.reshape(-1, WIDE)
+    outer_bias_sum = lax.dynamic_update_slice_in_dim(
+        jnp.zeros((part_width * ntp,), f32), grad_outer_bias_part, feature_start, 0
+    )
+    vec = jnp.concatenate(
+        [
+            jnp.zeros((2 * per, WIDE), f32),
+            spread(grad_output_bias),
+            spread(grad_feed_gain),
+            spread(grad_feed_shift),
+            spread(outer_bias_sum),
+            jnp.zeros((2 * heads, WIDE), f32),
+            spread(grad_inner_bias),
+        ]
+    )
+    ring = (heads, share, part_width * ntp // nseq)
+    grads = [
+        item.astype(bf16).reshape(ring + (-1,))
+        for item in (grad_inner_weight, grad_outer_weight, grad_output_weight)
+    ]
+    tail = run_tail(
+        (heads, share, nseq, ntp),
+        dq_head.reshape(heads, rows, WIDE),
+        dkv_head.reshape(share, heads, rows, WIDE),
+        h1,
+        x_parts,
+        jnp.concatenate([mean1, scale1], axis=1),
+        norm_gain[None, :],
+        spread_heads(query_weight, heads, False, 1) * 0.125,
+        pair_heads(key_weight, value_weight, heads),
+        lax.dynamic_slice_in_dim(grad_branch, feature_start, part_width, 1),
+        grads,
+        vec,
+    )
+    grad_x, inner_part, outer_part, output_part, query_part, kv_part, vectors = tail
+    split = kv_part.reshape(-1, heads, 2, HEAD_DIM)
+    key_part, value_part = (split[:, :, index].reshape(-1, local_width) for index in range(2))
+    wide = vectors[: 6 * per].reshape(6, -1)
+    biases = vectors[6 * per : 6 * per + 2 * heads].reshape(2, heads, 2, HEAD_DIM)
     return (
         layer_out,
-        grad_input,
+        grad_x.reshape(hidden_in.shape),
         wide[0],
         wide[1],
-        scatter_grad(grad_query_weight, 0),
-        rest[:local_width],
-        scatter_grad(grad_key_weight, 0),
-        scatter_grad(grad_value_weight, 0),
-        rest[local_width : 2 * local_width],
-        scatter_grad(grad_output_weight, 1),
+        query_part,
+        0.125 * biases[0, :, 0].reshape(-1),
+        key_part,
+        value_part,
+        biases[1, :, 1].reshape(-1),
+        output_part.T,
+        wide[2],
         wide[3],
         wide[4],
+        inner_part,
+        vectors[6 * per + 2 * heads :].reshape(-1),
+        outer_part.T,
         wide[5],
-        scatter_grad(grad_inner_weight, 0),
-        rest[2 * local_width :],
-        scatter_grad(grad_outer_weight, 1),
-        wide[2],
     )
 
 

time: 882 us -> 583 us (0.66)
  waiting for transfers between devices: 553 us -> 246 us
  Pallas kernels: 59.7 us -> 147 us
  blocking collectives: 80.8 us -> 11.4 us
  local copies, waits for them, and re-layouts: 31.8 us -> 53.9 us
  matrix products: 63.5 us -> 46.6 us
    reduce_scatter x6 -> x0, waiting for transfers between devices: 190 us -> none  [the longest x4 148 us: scatter_grad(): lax.psum_scatter(value.astype(bf16), 'seq', scatter_dimension=dimension,...]
    pallas_call x0 -> x1, Pallas kernels: none -> 88.5 us  [run_tail(): pl.pallas_call(functools.partial(tail_kernel, dims), out_shape=outs, in_s...]
    reduce_scatter x1, waiting for transfers between devices: 42.2 us -> 0.01 us  [on_device(): lax.psum_scatter(ffn_part, 'tp', scatter_dimension=1, tiled=True)]
    psum x2 -> x0, blocking collectives: 38.4 us -> none  [the longest x1 22.4 us: on_device(): lax.psum(jnp.concatenate([feature_sums.reshape(-1), token_sums.reshape(-1...]
    unnamed x18 -> x8, waiting for transfers between devices: 37.8 us -> 1.31 us
    all_gather x1, waiting for transfers between devices: 45.9 us -> 24.2 us  [on_device(): grad_branch = lax.all_gather(grad_branch_part, 'tp', axis=0, tiled=True)]
    all_to_all x1 -> x0, blocking collectives: 17.4 us -> none  [swap_heads(): lax.all_to_all(value, 'seq', 0, 0, axis_index_groups=across, tiled=True)]
    all_to_all x2 -> x0, waiting for transfers between devices: 17.4 us -> none  [swap_back(): lax.all_to_all(value.reshape(heads, rows, width), 'seq', 0, 0, axis_index...]
  transfers between devices with their start and end apart: 20 -> 11, of which waited for: 17 -> 9; matrix products, arithmetic and copies ran while one was open for 11% -> 16% of each run, Pallas kernels for 0% -> 21%
where the time goes in v2:
time: 583 us; the launch traced here: 572 us
  waiting for transfers between devices  246 us (42%)
  Pallas kernels  147 us (25%)
  local copies, waits for them, and re-layouts  53.9 us (9%)
  matrix products  46.6 us (8%)
  other arithmetic  41.4 us (7%)
  between operations  15.1 us (3%)
  starting transfers between devices  11.5 us (2%)
  blocking collectives  11.4 us (2%)
    pallas_call x1, Pallas kernels, run_tail(): pl.pallas_call(functools.partial(tail_kernel, dims), out_shape=outs, in_s...  88.5 us
    all_gather x1, waiting for transfers between devices, on_device(): h2 = lax.all_gather(h2_f.astype(bf16), 'tp', axis=0, tiled=True)  45.4 us
    all_gather x1, waiting for transfers between devices, on_device(): grad_out = lax.all_gather(cot, 'tp', axis=1, tiled=True)  40.3 us
    all_gather x1, waiting for transfers between devices, on_device(): x_parts = lax.all_gather(hidden_in.reshape(rows, part_width), 'tp', axis=0)  36 us
    reduce_scatter x1, waiting for transfers between devices, on_device(): lax.psum_scatter(cols_product(grad_pre, inner_weight).astype(bf16), 'tp',...  34.3 us
    all_to_all x3, waiting for transfers between devices, swap_heads(): lax.all_to_all(value, 'seq', 0, 0, axis_index_groups=across, tiled=True)  32.7 us
    reduce_scatter x1, waiting for transfers between devices, on_device(): lax.psum_scatter(attn_part, 'tp', scatter_dimension=0, tiled=True)  31.6 us
    pallas_call x1, Pallas kernels, on_device(): local_call(functools.partial(backward_kernel, nquery, nblocks, 2), 'atten...  30.9 us
  transfers between devices with their start and end apart: 11, of which 9 were waited for; matrix products, arithmetic and copies ran while one was open for 16% of the time, Pallas kernels for 21%

profile of v2, /device:TPU:8, one launch (start us, length us, event | category | flops | bytes accessed | tf_op | source)
XLA Modules:
  0.0 572.3 jit_solution(10463039383452926220)
XLA Ops:
  19.2 36.0 %all-gather.6.cloned.1.call-done.x_ref = bf16[4,1024,256]{2,1,0:T(8,128)(2,1)} async-done(((bf16[1,1024,256]{2,1,0:T(8,128)(2,1)}), bf16[4,1024,256]{2,1,0:T(8,128)(2,1)}) %all-gather.6.cloned.1.call-update) | async-done | bytes 2097168 | tf_op jit(solution)/shard_map/all_gather | solution.py:747
  55.2 4.0 copy.172
  72.6 13.3 %all-to-all-done.1 = bf16[4,1024,128]{2,1,0:T(8,128)(2,1)S(1)} async-done(((bf16[4,1024,128]{2,1,0:T(8,128)(2,1)}), bf16[4,1024,128]{2,1,0:T(8,128)(2,1)S(1)}, u32[]{:S(2)}, u32[]{:S(2)}) %all-to-all-start.1) | async-done | bytes 1048608 | tf_op jit(solution)/shard_map/all_to_all | solution.py:734
  88.7 4.5 select_reduce_fusion
  106.2 10.9 %all-to-all-done = bf16[4,1024,128]{2,1,0:T(8,128)(2,1)S(1)} async-done(((bf16[4,1024,128]{2,1,0:T(8,128)(2,1)}), bf16[4,1024,128]{2,1,0:T(8,128)(2,1)S(1)}, u32[]{:S(2)}, u32[]{:S(2)}) %all-to-all-start) | async-done | bytes 1048608 | tf_op jit(solution)/shard_map/all_to_all | solution.py:734
  118.1 27.3 %attention_forward.1.res_ref = f32[4096,128]{1,0:T(8,128)} custom-call(s32[1024]{0:T(1024)} %copy-done.22, s32[193]{0:T(256)} %pad_add_fusion.long_ref, s32[256]{0:T(256)} %pad_add_fusion.1.block_ref, bf16[4096,128]{1,0:T(8,128)(2,1)} %bitcast.119, bf16[8192,128]{1,0:T(8,128)(2,1)} %all-gather.8.cloned.1.call-done.kv_ref), custom_call_target="tpu_custom_call" | custom-call | bytes 8388608 | tf_op jit(solution)/shard_map/attention_forward/pallas_call | solution.py:769
  148.4 11.4 %all_to_all.20 = bf16[4,1024,64]{1,2,0:T(8,128)(2,1)S(1)} all-to-all(bf16[4,1024,64]{1,2,0:T(8,128)(2,1)} %copy.193), channel_id=1, replica_groups={{0,8,16,24},{4,12,20,28},{1,9,17,25},{5,13,21,29},{2,10,18,26},{6,14,22..., dimensions={0} | all-to-all | bytes 1048576 | tf_op jit(solution)/shard_map/all_to_all | solution.py:739
  163.9 4.0 convert_element_type.148
  167.9 5.5 copy.201
  173.4 31.6 %reduce-scatter.4.cloned.1.call-done = bf16[256,1024]{1,0:T(8,128)(2,1)} async-done(((bf16[1024,1024]{1,0:T(8,128)(2,1)}), bf16[256,1024]{1,0:T(8,128)(2,1)}) %reduce-scatter.4.cloned.1.call-update) | async-done | bytes 524304 | tf_op jit(solution)/shard_map/reduce_scatter | solution.py:778
  208.6 45.4 %all-gather.10.cloned.1.call-done = bf16[1024,1024]{1,0:T(8,128)(2,1)} async-done(((bf16[256,1024]{1,0:T(8,128)(2,1)}), bf16[1024,1024]{1,0:T(8,128)(2,1)}) %all-gather.10.cloned.1.call-update) | async-done | bytes 2097168 | tf_op jit(solution)/shard_map/all_gather | solution.py:783
  254.0 6.5 %fusion.32 = f32[1024,1024]{1,0:T(8,128)} fusion(bf16[1024,1024]{1,0:T(8,128)(2,1)} %all-gather.10.cloned.1.call-done, bf16[1024,1024]{1,0:T(8,128)(2,1)} %param.32), kind=kOutput, calls=%fused_computation.146 | convolution fusion | flops 2147483648 | bytes 8388608 | tf_op jit(solution)/shard_map/dot_general | solution.py:784
  260.6 40.3 %all-gather.12.cloned.1.call-done = bf16[1024,1024]{1,0:T(8,128)(2,1)} async-done(((bf16[1024,256]{1,0:T(8,128)(2,1)}), bf16[1024,1024]{1,0:T(8,128)(2,1)}) %all-gather.12.cloned.1.call-update) | async-done | bytes 2097168 | tf_op jit(solution)/shard_map/all_gather | solution.py:795
  300.8 7.5 %convert_reduce_fusion = (f32[1024]{0:T(1024)S(1)}, bf16[1024,1024]{1,0:T(8,128)(2,1)S(1)}) fusion(f32[1024,1024]{1,0:T(8,128)} %fusion.32, f32[1024]{0:T(1024)S(1)} %copy-done.28, bf16[1024,1024]{1,0:T(8,128)(2,1)} %all-gather.12.cloned.1.call-done, bf16[1024,1024]{1,0:T(8,128)(2,1)S(1)} %copy-done), kind=kOutput, calls=%fused_computation.10 | convolution fusion | flops 2171599872 | bytes 10493952 | tf_op jit(solution)/shard_map/dot_general | solution.py:675
  313.4 6.9 %fusion.26 = f32[1024,1024]{1,0:T(8,128)} fusion(bf16[1024,1024]{1,0:T(8,128)(2,1)S(1)} %copy-done, f32[1024,1024]{1,0:T(8,128)} %fusion.32, f32[1024]{0:T(1024)S(1)} %copy-done.28), kind=kOutput, calls=%fused_computation.141 | convolution fusion | flops 2157969408 | bytes 10489856 | tf_op jit(solution)/shard_map/dot_general | solution.py:787
  320.4 34.3 %reduce-scatter.8.cloned.1.call-done = bf16[256,1024]{1,0:T(8,128)(2,1)} async-done(((bf16[1024,1024]{1,0:T(8,128)(2,1)}), bf16[256,1024]{1,0:T(8,128)(2,1)}) %reduce-scatter.8.cloned.1.call-update) | async-done | bytes 524304 | tf_op jit(solution)/shard_map/reduce_scatter | solution.py:802
  366.6 3.8 convert_element_type.130
  370.5 4.6 add_convert_fusion.1.h1_ref
  375.2 3.7 convolution_convert_fusion.1
  378.9 4.0 convolution_convert_fusion
  382.9 24.2 %all-gather.14.cloned.1.call-done = bf16[1024,1024]{1,0:T(8,128)(2,1)} async-done(((bf16[256,1024]{1,0:T(8,128)(2,1)}), bf16[1024,1024]{1,0:T(8,128)(2,1)}) %all-gather.14.cloned.1.call-update) | async-done | bytes 2097168 | tf_op jit(solution)/shard_map/all_gather | solution.py:809
  420.1 8.4 %all-to-all-done.3 = bf16[4,1024,128]{2,1,0:T(8,128)(2,1)S(1)} async-done(((bf16[4,1024,128]{2,1,0:T(8,128)(2,1)}), bf16[4,1024,128]{2,1,0:T(8,128)(2,1)S(1)}, u32[]{:S(2)}, u32[]{:S(2)}) %all-to-all-start.3) | async-done | bytes 1048608 | tf_op jit(solution)/shard_map/all_to_all | solution.py:734
  429.5 30.9 %attention_backward.1 = (bf16[4096,128]{1,0:T(8,128)(2,1)}, bf16[8192,128]{1,0:T(8,128)(2,1)}) custom-call(s32[1024]{0:T(1024)} %copy-done.22, s32[193]{0:T(256)} %pad_add_fusion.long_ref, s32[256]{0:T(256)} %pad_add_fusion.1.block_ref, bf16[4096,128]{1,0:T(8,128)(2,1)} %bitcast.120, bf16[4096,128]{1,0:T(8,128)(2,1)} %bitcast.121, ...), custom_call_target="tpu_custom_call" | custom-call | bytes 8388608 | tf_op jit(solution)/shard_map/attention_backward/pallas_call | solution.py:813
  460.4 88.5 %tail.1 = (f32[1024,256]{1,0:T(8,128)}, f32[128,1024]{1,0:T(8,128)}, f32[128,1024]{1,0:T(8,128)}, f32[128,256]{1,0:T(8,128)}, f32[128,256]{1,0:T(8,128)}, /*index=5*/f32[128,512]{1,0:T(8,128)}, f32[64,128]{1,0:T(8,128)}) custom-call(bf16[4,1024,128]{2,1,0:T(8,128)(2,1)} %bitcast.142, bf16[2,4,1024,128]{3,2,1,0:T(8,128)(2,1)} %bitcast.141, ...), custom_call_target="tpu_custom_call" | custom-call | tf_op jit(solution)/shard_map/tail/pallas_call | solution.py:657
  (205 shorter events, 99.6 us)
Async XLA Ops:
  7.2 293.6 %copy-start = (bf16[1024,1024]{1,0:T(8,128)(2,1)S(1)}, bf16[1024,1024]{1,0:T(8,128)(2,1)}, u32[]{:S(2)}) copy-start(bf16[1024,1024]{1,0:T(8,128)(2,1)} %param.34) | copy-start | bytes 6291460
  7.2 48.0 %all-gather.6.cloned.1.call-start = ((), (), s32[]{:S(2)}) async-start(), calls=%async_computation.7 | async-start | bytes 2621440 | tf_op jit(solution)/shard_map/all_gather | solution.py:747
  19.2 45.1 %copy-start.5 = (bf16[1024,4,128]{0,2,1:T(8,128)(2,1)}, bf16[1024,4,128]{0,2,1:T(8,128)(2,1)S(1)}, u32[]{:S(2)}) copy-start(bf16[1024,4,128]{0,2,1:T(8,128)(2,1)S(1)} %pad_maximum_fusion) | copy-start | bytes 3145732
  66.6 21.5 %copy-start.25 = (f32[256]{0:T(256)S(1)}, f32[256]{0:T(256)}, u32[]{:S(2)}) copy-start(f32[256]{0:T(256)} %param.24) | copy-start | bytes 3076
  68.8 17.1 %all-to-all-start.1 = ((bf16[4,1024,128]{2,1,0:T(8,128)(2,1)}), bf16[4,1024,128]{2,1,0:T(8,128)(2,1)S(1)}, u32[]{:S(2)}, u32[]{:S(2)}) async-start(bf16[4,1024,128]{2,1,0:T(8,128)(2,1)} %bitcast.128), calls=%async_computation.1 | async-start | bytes 2097152 | tf_op jit(solution)/shard_map/all_to_all | solution.py:734
  72.5 44.6 %all-gather.8.cloned.1.call-start = ((), (), s32[]{:S(2)}) async-start(), calls=%async_computation.8 | async-start | bytes 3145728 | tf_op jit(solution)/shard_map/all_gather | solution.py:765
  100.3 16.8 %all-to-all-start = ((bf16[4,1024,128]{2,1,0:T(8,128)(2,1)}), bf16[4,1024,128]{2,1,0:T(8,128)(2,1)S(1)}, u32[]{:S(2)}, u32[]{:S(2)}) async-start(bf16[4,1024,128]{2,1,0:T(8,128)(2,1)} %bitcast.127), calls=%async_computation | async-start | bytes 2097152 | tf_op jit(solution)/shard_map/all_to_all | solution.py:734
  103.8 101.1 %reduce-scatter.4.cloned.1.call-start = ((), (), s32[]{:S(2)}) async-start(), calls=%async_computation.9 | async-start | bytes 2621440 | tf_op jit(solution)/shard_map/reduce_scatter | solution.py:778
  106.2 10.9 %copy-start.22 = (s32[1024]{0:T(1024)}, s32[1024]{0:T(1024)S(1)}, u32[]{:S(2)}) copy-start(s32[1024]{0:T(1024)S(1)} %constant_dynamic-update-slice_fusion.8.near_ref) | copy-start | bytes 12292
  163.9 90.2 %all-gather.10.cloned.1.call-start = ((), (), s32[]{:S(2)}) async-start(), calls=%async_computation.10 | async-start | bytes 2621440 | tf_op jit(solution)/shard_map/all_gather | solution.py:783
  167.9 37.0 %copy-start.23 = (f32[1024]{0:T(1024)S(1)}, f32[1024]{0:T(1024)}, u32[]{:S(2)}) copy-start(f32[1024]{0:T(1024)} %param.29) | copy-start | bytes 12292
  167.9 38.9 %copy-start.18 = (f32[1024]{0:T(1024)S(1)}, f32[1024]{0:T(1024)}, u32[]{:S(2)}) copy-start(f32[1024]{0:T(1024)} %param.30) | copy-start | bytes 12292
  167.9 38.9 %copy-start.24 = (f32[1024]{0:T(1024)S(1)}, f32[1024]{0:T(1024)}, u32[]{:S(2)}) copy-start(f32[1024]{0:T(1024)} %param.31) | copy-start | bytes 12292
  208.0 92.9 %all-gather.12.cloned.1.call-start = ((), (), s32[]{:S(2)}) async-start(), calls=%async_computation.12 | async-start | bytes 2621440 | tf_op jit(solution)/shard_map/all_gather | solution.py:795
  208.5 92.3 %copy-start.28 = (f32[1024]{0:T(1024)S(1)}, f32[1024]{0:T(1024)}, u32[]{:S(2)}) copy-start(f32[1024]{0:T(1024)} %param.33) | copy-start | bytes 12292
  208.6 146.1 %reduce-scatter.8.cloned.1.call-start = ((), (), s32[]{:S(2)}) async-start(), calls=%async_computation.13 | async-start | bytes 2621440 | tf_op jit(solution)/shard_map/reduce_scatter | solution.py:802
  300.8 8.9 %copy-start.26 = (bf16[1024,1024]{1,0:T(8,128)(2,1)S(1)}, bf16[1024,1024]{1,0:T(8,128)(2,1)}, u32[]{:S(2)}) copy-start(bf16[1024,1024]{1,0:T(8,128)(2,1)} %param.32) | copy-start | bytes 6291460
  313.4 93.7 %all-gather.14.cloned.1.call-start = ((), (), s32[]{:S(2)}) async-start(), calls=%async_computation.14 | async-start | bytes 2621440 | tf_op jit(solution)/shard_map/all_gather | solution.py:809
  320.4 40.9 %copy-start.6 = (bf16[1024,4,128]{0,2,1:T(8,128)(2,1)S(1)}, bf16[1024,4,128]{0,2,1:T(8,128)(2,1)}, u32[]{:S(2)}) copy-start(bf16[1024,4,128]{0,2,1:T(8,128)(2,1)} %copy-done.5) | copy-start | bytes 3145732
  361.0 198.6 %reduce-scatter.6.cloned.1.call-start = ((), (), s32[]{:S(2)}) async-start(), calls=%async_computation.11 | async-start | bytes 2621440 | tf_op jit(solution)/shard_map/reduce_scatter | solution.py:790
  411.3 17.1 %all-to-all-start.3 = ((bf16[4,1024,128]{2,1,0:T(8,128)(2,1)}), bf16[4,1024,128]{2,1,0:T(8,128)(2,1)S(1)}, u32[]{:S(2)}, u32[]{:S(2)}) async-start(bf16[4,1024,128]{2,1,0:T(8,128)(2,1)} %bitcast.45), calls=%async_computation.6 | async-start | bytes 2097152 | tf_op jit(solution)/shard_map/all_to_all | solution.py:734
  415.0 45.4 %copy-start.19 = (f32[64,128]{1,0:T(8,128)}, f32[64,128]{1,0:T(8,128)S(1)}, u32[]{:S(2)}) copy-start(f32[64,128]{1,0:T(8,128)S(1)} %constant_dynamic-update-slice_fusion.1.vec_ref) | copy-start | bytes 98308
  460.4 104.7 %copy-start.1 = (bf16[1024,1024]{1,0:T(8,128)(2,1)S(1)}, bf16[1024,1024]{1,0:T(8,128)(2,1)}, u32[]{:S(2)}) copy-start(bf16[1024,1024]{1,0:T(8,128)(2,1)} %param.34) | copy-start | bytes 6291460
  548.9 12.7 %copy-start.15 = (f32[1024,256]{1,0:T(8,128)S(1)}, f32[1024,256]{1,0:T(8,128)}, u32[]{:S(2)}) copy-start(f32[1024,256]{1,0:T(8,128)} %get-tuple-element.28) | copy-start | bytes 3145732
  (19 other events, 64.1 us)
Sparse Core Ops, SparseCore 0:
  9.6 45.5 all-gather.5
  87.1 10.6 all-gather.7
  164.0 40.9 reduce-scatter.3
  208.1 45.9 all-gather.9
  255.5 45.2 all-gather.11
  313.5 41.1 reduce-scatter.7
  361.1 45.9 all-gather.13
  409.4 41.9 reduce-scatter.5

commit v3 on v2

v3 whole, which is shorter than its diff:
```python
import functools
import math

import jax
import jax.numpy as jnp
from jax import lax
from jax.experimental import pallas as pl
from jax.experimental.pallas import tpu as pltpu
from jax.sharding import PartitionSpec as P

HEAD_DIM = 64
BLK = 64
GLOBAL = 2
SLOTS = 8
WIDE = 2 * HEAD_DIM
CHUNKS = 4
ROUNDS = 2
NEG = -1e30
NT = (((1,), (1,)), ((), ()))
TN = (((0,), (0,)), ((), ()))
MESH = pl.DeviceIdType.MESH
F32, BF16 = jnp.float32, jnp.bfloat16


def split_by(value, count):
    if count & (count - 1) == 0:
        return value >> (count.bit_length() - 1), value & (count - 1)
    return value // count, value % count


def remote(src, dst, send_sem, recv_sem, device):
    return pltpu.make_async_remote_copy(
        src_ref=src, dst_ref=dst, send_sem=send_sem, recv_sem=recv_sem,
        device_id=device, device_id_type=MESH,
    )


def greet(peers):
    barrier = pltpu.get_barrier_semaphore()
    for peer in peers:
        pl.semaphore_signal(barrier, inc=1, device_id=peer, device_id_type=MESH)
    pl.semaphore_wait(barrier, len(peers))


def add_up(*terms):
    total = terms[0].astype(F32)
    for term in terms[1:]:
        total = total + term.astype(F32)
    return total


def swap_halves(value):
    return pltpu.roll(value, HEAD_DIM, 1)


def low_half(value):
    return lax.broadcasted_iota(jnp.int32, value.shape, 1) < HEAD_DIM


def mix_pair(left, right):
    low = low_half(left)
    return (
        jnp.where(low, left, swap_halves(right)),
        jnp.where(low, swap_halves(left), right),
    )


def unpack_pair(left, right):
    even, odd = mix_pair(left.astype(F32), right.astype(F32))
    tiles = []
    for start in range(0, left.shape[0], BLK):
        tiles += [even[start : start + BLK], odd[start : start + BLK]]
    return jnp.concatenate(tiles, axis=0).astype(BF16)


def pack_pair(value):
    lefts, rights = [], []
    for start in range(0, value.shape[0], 2 * BLK):
        left, right = mix_pair(value[start : start + BLK], value[start + BLK : start + 2 * BLK])
        lefts.append(left)
        rights.append(right)
    return jnp.concatenate(lefts, axis=0).astype(BF16), jnp.concatenate(rights, axis=0).astype(BF16)


def dma(*shape):
    return pltpu.SemaphoreType.DMA(tuple(max(size, 1) for size in shape))


def vmem(*shape, dtype=BF16):
    return pltpu.VMEM(shape, dtype)


IN_VMEM = pl.BlockSpec(memory_space=pltpu.VMEM)
IN_SMEM = pl.BlockSpec(memory_space=pltpu.SMEM)
ANYWHERE = pl.BlockSpec(memory_space=pl.ANY)


class Place:
    def __init__(self, dims):
        self.heads, self.share, self.nseq, self.ntp = dims
        self.seq, self.tp = lax.axis_index("seq"), lax.axis_index("tp")
        self.head, self.part = self.seq // self.share, lax.rem(self.seq, self.share)

    def partner(self, step):
        other = lax.rem(self.part + step, self.share)
        return other, (self.head * self.share + other, self.tp)

    def across(self, step):
        other = lax.rem(self.head + step, self.heads)
        return other, (other * self.share + self.part, self.tp)

    def along(self, step):
        other = lax.rem(self.tp + step, self.ntp)
        return other, (self.seq, other)

    def apart(self, step):
        far, near = step // self.heads, step % self.heads
        head = lax.rem(self.head + near, self.heads)
        tp = lax.rem(self.tp + far, self.ntp)
        return head, tp, (head * self.share + self.part, tp)


def fill_table(place, docs_ref, pads_ref, picks_ref, table_ref, nrows):
    nblocks = table_ref.shape[1]
    block = lax.broadcasted_iota(jnp.int32, (1, nblocks), 1)

    def doc_step(doc, state):
        start, first, last, pad = state
        stop = start + docs_ref[doc]
        inside = (block >= start) & (block < stop)
        first = jnp.where(inside, start, first)
        last = jnp.where(inside, stop - 1, last)
        pad = jnp.where(inside, pads_ref[doc], pad)
        return stop, first, last, pad

    zero = jnp.zeros((1, nblocks), jnp.int32)
    _, first, last, pad = lax.fori_loop(
        0, docs_ref.shape[0], doc_step, (jnp.int32(0), zero, zero, zero)
    )
    length = last - first + 1
    picks = []
    for index in range(picks_ref.shape[0]):
        pick = picks_ref[index : index + 1, :]
        whole = (pick.astype(F32) / length.astype(F32)).astype(jnp.int32)
        left = pick - whole * length
        left = jnp.where(left < 0, left + length, left)
        left = jnp.where(left >= length, left - length, left)
        picks.append(first + left)
    glob = block - first < GLOBAL
    is_long = glob & (last - first >= SLOTS)
    never = block < 0
    p0, p1, p2 = picks
    fresh = lambda pick: (pick >= first + GLOBAL) & ((pick > block + 1) | (pick < block - 1))
    near = [
        (block - 1, ~never),
        (block, ~never),
        (block + 1, block < last),
        (first, ~never),
        (first + 1, block - 1 > first + 1),
        (p0, fresh(p0)),
        (p1, fresh(p1) & (p1 != p0)),
        (p2, fresh(p2) & (p2 != p0) & (p2 != p1)),
    ]
    for index, (other, use) in enumerate(near):
        whole = first + index
        use = (glob & (whole <= last) & ~is_long) | (~glob & use)
        other = jnp.where(use, jnp.where(glob, whole, other), block)
        live = jnp.where(use, jnp.where(other == last, BLK - pad, BLK), 0)
        table_ref[index : index + 1, :] = row_of(place, other, nrows) * WIDE + live
    table_ref[SLOTS : SLOTS + 1, :] = first
    table_ref[SLOTS + 1 : SLOTS + 2, :] = last
    table_ref[SLOTS + 2 : SLOTS + 3, :] = pad


def head_kernel(
    dims, nrows, docs_ref, pads_ref, picks_ref, x_ref, gain_ref, shift_ref,
    wq_ref, bq_ref, wk_ref, wv_ref, bv_ref,
    q_out, kv_out, h1_out, xs_out, xt_out, stat_out, table_out,
    xs, h1, qbuf, kvbuf, right_s, right_r, left_s, left_r, q_s, q_r, kv_s, kv_r, on_s, on_r, local,
):
    place = Place(dims)
    heads, share, nseq, ntp = dims
    head, part, seq, tp = place.head, place.part, place.seq, place.tp
    rows, width = x_ref.shape
    features = width * ntp
    chunk_rows = rows // CHUNKS

    def chunk_of(chunk):
        return pl.ds(chunk * chunk_rows, chunk_rows)

    def rightward(chunk, index):
        spot = xs.at[index, chunk_of(chunk)]
        return remote(
            spot, spot, right_s.at[chunk, index], right_r.at[chunk, index], (seq, tp + 1)
        )

    def leftward(chunk, index):
        spot = xs.at[index, chunk_of(chunk)]
        return remote(spot, spot, left_s.at[chunk, index], left_r.at[chunk, index], (seq, tp - 1))

    def q_copy(chunk, step):
        other, device = place.across(step)
        return remote(
            qbuf.at[other, chunk_of(chunk)], q_out.at[head, chunk_of(chunk)],
            q_s.at[chunk, step - 1], q_r.at[chunk, step - 1], device,
        )

    def kv_copy(chunk, step):
        other, device = place.across(step)
        return remote(
            kvbuf.at[other, chunk_of(chunk)], kv_out.at[part, head, chunk_of(chunk)],
            kv_s.at[chunk, step - 1], kv_r.at[chunk, step - 1], device,
        )

    def kv_on(chunk, hop, step):
        owner = lax.rem(head + heads - hop, heads)
        spot = kv_out.at[part, owner, chunk_of(chunk)]
        source = kvbuf.at[head, chunk_of(chunk)] if hop == 0 else spot
        return remote(
            source, spot, on_s.at[chunk, hop, step - 1], on_r.at[chunk, hop, step - 1],
            place.partner(step)[1],
        )

    def own_send(chunk):
        @pl.when(tp < ntp - 1)
        def _():
            rightward(chunk, tp).start()

        @pl.when(tp > 0)
        def _():
            leftward(chunk, tp).start()

    def pass_on(chunk):
        for hop in range(1, ntp):
            below, above = tp - hop, tp + hop

            @pl.when(below >= 0)
            def _():
                rightward(chunk, below).wait_recv()

                @pl.when(tp < ntp - 1)
                def _():
                    rightward(chunk, below).start()

            @pl.when(above < ntp)
            def _():
                leftward(chunk, above).wait_recv()

                @pl.when(tp > 0)
                def _():
                    leftward(chunk, above).start()

    def compute(chunk):
        here = chunk_of(chunk)
        x = jnp.concatenate([xs[index, here] for index in range(ntp)], axis=1).astype(F32)
        mean = jnp.sum(x, axis=1, keepdims=True) * (1.0 / features)
        centered = x - mean
        spread = jnp.sum(centered * centered, axis=1, keepdims=True) * (1.0 / features)
        scale = lax.rsqrt(spread + 1e-05)
        normed = (centered * scale * gain_ref[...] + shift_ref[...]).astype(BF16)
        h1[here] = normed
        stat_out[here, 0:1] = mean
        stat_out[here, 1:2] = scale
        q = (jnp.dot(normed, wq_ref[...], preferred_element_type=F32) + bq_ref[...]) * 0.125
        k = jnp.dot(normed, wk_ref[...], preferred_element_type=F32)
        v = jnp.dot(normed, wv_ref[...], preferred_element_type=F32) + bv_ref[...]
        for index in range(0, heads, 2):
            lanes = slice(index * HEAD_DIM, (index + 2) * HEAD_DIM)
            kv = mix_pair(k[:, lanes], v[:, lanes])
            low = low_half(q[:, lanes])
            qs = (q[:, lanes], swap_halves(q[:, lanes]))
            for off in range(2):
                kvbuf[index + off, here] = kv[off].astype(BF16)
                qbuf[index + off, here] = jnp.where(low, qs[off], 0.0).astype(BF16)

    def hand_on(chunk):
        for hop in range(heads):
            if hop:
                kv_copy(chunk, hop).wait_recv()
            for step in range(1, share):
                kv_on(chunk, hop, step).start()

    xs[tp] = x_ref[...]
    greet(
        [place.partner(step)[1] for step in range(1, share)]
        + [place.across(step)[1] for step in range(1, heads)]
        + [place.along(step)[1] for step in range(1, ntp)]
    )
    own_send(0)
    own_send(1)
    fill_table(place, docs_ref, pads_ref, picks_ref, table_out, nrows)
    for chunk in range(CHUNKS):
        if 0 < chunk < CHUNKS - 1:
            own_send(chunk + 1)
        pass_on(chunk)
        compute(chunk)
        for step in range(1, heads):
            kv_copy(chunk, step).start()
        for step in range(1, heads):
            q_copy(chunk, step).start()
        if chunk > 0:
            hand_on(chunk - 1)
    pairs = [
        (qbuf.at[head], q_out.at[head]),
        (kvbuf.at[head], kv_out.at[part, head]),
        (h1, h1_out),
        (xs, xs_out),
    ]
    copies = [
        pltpu.make_async_copy(source, target, local.at[index])
        for index, (source, target) in enumerate(pairs)
    ]
    for copy in copies:
        copy.start()
    mine = pl.ds(pl.multiple_of(tp * (rows // ntp), rows // ntp), rows // ntp)
    xt_out[...] = xs[:, mine]
    hand_on(CHUNKS - 1)
    for copy in copies:
        copy.wait()
    for chunk in range(CHUNKS):
        for step in range(1, heads):
            q_copy(chunk, step).wait_recv()
        for hop in range(heads):
            for step in range(1, share):
                kv_on(chunk, hop, step).wait_recv()
    for chunk in range(CHUNKS):
        for step in range(1, heads):
            q_copy(chunk, step).wait_send()
            kv_copy(chunk, step).wait_send()
        for hop in range(heads):
            for step in range(1, share):
                kv_on(chunk, hop, step).wait_send()
        for index in range(ntp):
            @pl.when((tp >= index) & (tp < ntp - 1))
            def _():
                rightward(chunk, index).wait_send()

            @pl.when((tp <= index) & (tp > 0))
            def _():
                leftward(chunk, index).wait_send()


def run_head(dims, nrows, docs, pads, picks, x, *params):
    heads, share, nseq, ntp = dims
    rows, width = x.shape
    nblocks = picks.shape[1]
    sds = jax.ShapeDtypeStruct
    outs = [
        sds((heads, rows, WIDE), BF16),
        sds((share, heads, rows, WIDE), BF16),
        sds((rows, width * ntp), BF16),
        sds((ntp, rows, width), BF16),
        sds((ntp, rows // ntp, width), BF16),
        sds((rows, 2), F32),
        sds((16, nblocks), jnp.int32),
    ]
    scratch = [
        vmem(ntp, rows, width),
        vmem(rows, width * ntp),
        vmem(heads, rows, WIDE),
        vmem(heads, rows, WIDE),
    ]
    sems = (
        [dma(CHUNKS, ntp)] * 4 + [dma(CHUNKS, heads - 1)] * 4
        + [dma(CHUNKS, heads, share - 1)] * 2 + [dma(4)]
    )
    return pl.pallas_call(
        functools.partial(head_kernel, dims, nrows),
        out_shape=outs,
        in_specs=[IN_SMEM, IN_SMEM] + [IN_VMEM] * (2 + len(params)),
        out_specs=[ANYWHERE] * 4 + [IN_VMEM] * 3,
        scratch_shapes=scratch + sems,
        name="head",
        compiler_params=pltpu.CompilerParams(
            collective_id=1, has_side_effects=True, vmem_limit_bytes=60 << 20
        ),
    )(docs, pads, picks, x, *params)


def block_of(place, query, nrows):
    source, row = split_by(query, nrows)
    return row * place.nseq + source * place.share + place.part


def row_of(place, block, nrows):
    row, holder = split_by(block, place.nseq)
    head, part = split_by(holder, place.share)
    return ((part * place.heads + head) * nrows + row) * BLK


def near_slots(table_ref, block):
    entries = [table_ref[index, block] for index in range(SLOTS)]
    slots = [pl.multiple_of(entry >> 7, BLK) for entry in entries]
    return slots, [entry & (WIDE - 1) for entry in entries]


def long_slots(place, table_ref, block, chunk, nrows):
    first, last = table_ref[SLOTS, block], table_ref[SLOTS + 1, block]
    final = BLK - table_ref[SLOTS + 2, block]
    slots, lives = [], []
    for index in range(SLOTS):
        wanted = first + chunk * SLOTS + index
        slots.append(pl.multiple_of(row_of(place, jnp.minimum(wanted, last), nrows), BLK))
        lives.append(jnp.where(wanted < last, BLK, jnp.where(wanted == last, final, 0)))
    return slots, lives


def for_long(place, table_ref, nquery, nrows, body):
    def step(query, carry):
        block = block_of(place, query, nrows)
        first, last = table_ref[SLOTS, block], table_ref[SLOTS + 1, block]

        @pl.when((block - first < GLOBAL) & (last - first >= SLOTS))
        def _():
            body(query, block, (last - first + SLOTS) >> 3)

        return carry

    lax.fori_loop(0, nquery, step, 0)


def bias_row(lives):
    lane = lax.broadcasted_iota(jnp.int32, (1, WIDE), 1)
    parts = []
    for index in range(0, SLOTS, 2):
        bound = jnp.where(lane < BLK, lives[index], lives[index + 1] + BLK)
        parts.append(jnp.where(lane < bound, 0.0, NEG))
    return jnp.concatenate(parts, axis=1)


def take(ref, slots):
    return jnp.concatenate([ref[pl.ds(slot, BLK), :] for slot in slots], axis=0)


def forward_kernel(dims, nrows, unroll, table_ref, q_ref, kv_ref, out_ref, res_ref):
    place = Place(dims)
    nquery = q_ref.shape[0] // BLK
    upper = lax.broadcasted_iota(jnp.int32, (BLK, WIDE), 1) >= HEAD_DIM

    def finish(query, top, total, accum):
        value = accum / total
        res_ref[pl.ds(query * BLK, BLK), :] = jnp.where(upper, value, top + jnp.log(total))
        return value

    def scores_of(query, slots, lives):
        kv = take(kv_ref, slots)
        scores = lax.dot_general(
            q_ref[pl.ds(query * BLK, BLK), :], kv, NT, preferred_element_type=F32
        )
        return kv, scores + bias_row(lives)

    def near_one(query):
        kv, scores = scores_of(query, *near_slots(table_ref, block_of(place, query, nrows)))
        top = jnp.max(scores, axis=1, keepdims=True)
        weights = jnp.exp(scores - top)
        total = jnp.sum(weights, axis=1, keepdims=True)
        accum = jnp.dot(weights.astype(BF16), kv, preferred_element_type=F32)
        return finish(query, top, total, accum)

    def near_step(index, carry):
        for offset in range(unroll):
            pair = index * unroll + offset
            even, odd = near_one(2 * pair), near_one(2 * pair + 1)
            out_ref[pl.ds(pair * BLK, BLK), :] = jnp.where(upper, odd, swap_halves(even)).astype(BF16)
        return carry

    lax.fori_loop(0, nquery // (2 * unroll), near_step, 0)

    def long_body(query, block, chunks):
        def chunk_step(chunk, state):
            top, total, accum = state
            kv, scores = scores_of(query, *long_slots(place, table_ref, block, chunk, nrows))
            new_top = jnp.maximum(top, jnp.max(scores, axis=1, keepdims=True))
            weights = jnp.exp(scores - new_top)
            decay = jnp.exp(top - new_top)
            total = total * decay + jnp.sum(weights, axis=1, keepdims=True)
            accum = accum * decay + jnp.dot(weights.astype(BF16), kv, preferred_element_type=F32)
            return new_top, total, accum

        start = (
            jnp.full((BLK, 1), NEG, F32),
            jnp.zeros((BLK, 1), F32),
            jnp.zeros((BLK, WIDE), F32),
        )
        value = finish(query, *lax.fori_loop(0, chunks, chunk_step, start))
        spot = pl.ds(pl.multiple_of((query >> 1) * BLK, BLK), BLK)
        is_odd = (query & 1) == 1
        moved = jnp.where(is_odd, value, swap_halves(value))
        out_ref[spot, :] = jnp.where(upper == is_odd, moved, out_ref[spot, :].astype(F32)).astype(BF16)

    for_long(place, table_ref, nquery, nrows, long_body)


def backward_kernel(
    dims, nrows, unroll, table_ref, q_ref, do_ref, res_ref, kv_ref, dq_ref, dkv_ref, sum_ref
):
    place = Place(dims)
    nquery = q_ref.shape[0] // BLK
    upper = lax.broadcasted_iota(jnp.int32, (BLK, WIDE), 1) >= HEAD_DIM
    sum_ref[...] = jnp.zeros_like(sum_ref)

    def load(query, packed, is_odd):
        moved = jnp.where(is_odd, packed, swap_halves(packed))
        grad = jnp.where(upper, moved, 0.0)
        rows = pl.ds(query * BLK, BLK)
        both = jnp.concatenate([q_ref[rows, :], grad.astype(BF16)], axis=0)
        res = res_ref[rows, :]
        delta = jnp.sum(res * grad, axis=1, keepdims=True)
        return both, res[:, :1], delta

    def terms(both, log_total, delta, slots, lives):
        kv = take(kv_ref, slots)
        pair = lax.dot_general(both, kv, NT, preferred_element_type=F32)
        probs = jnp.exp(pair[:BLK] + bias_row(lives) - log_total)
        grad_scores = (probs * (pair[BLK:] - delta)).astype(BF16)
        weights = jnp.concatenate([grad_scores, probs.astype(BF16)], axis=0)
        dkv = lax.dot_general(weights, both, TN, preferred_element_type=F32)
        dq = jnp.dot(grad_scores, kv, preferred_element_type=F32)
        return dq, dkv

    def scatter(slots, dkv):
        for index, slot in enumerate(slots):
            sum_ref[pl.ds(slot, BLK), :] += dkv[index * BLK : (index + 1) * BLK]

    def near_step(index, carry):
        done = []
        for offset in range(unroll):
            pair = index * unroll + offset
            packed = do_ref[pl.ds(pair * BLK, BLK), :].astype(F32)
            grads = []
            for is_odd in (False, True):
                query = 2 * pair + int(is_odd)
                slots, lives = near_slots(table_ref, block_of(place, query, nrows))
                dq, dkv = terms(*load(query, packed, is_odd), slots, lives)
                grads.append(dq)
                done.append((slots, dkv))
            dq_ref[pl.ds(pair * BLK, BLK), :] = jnp.where(
                upper, swap_halves(grads[1]), grads[0]
            ).astype(BF16)
        for slots, dkv in done:
            scatter(slots, dkv)
        return carry

    lax.fori_loop(0, nquery // (2 * unroll), near_step, 0)

    def long_body(query, block, chunks):
        is_odd = (query & 1) == 1
        spot = pl.ds(pl.multiple_of((query >> 1) * BLK, BLK), BLK)
        loaded = load(query, do_ref[spot, :].astype(F32), is_odd)

        def chunk_step(chunk, total):
            slots, lives = long_slots(place, table_ref, block, chunk, nrows)
            dq, dkv = terms(*loaded, slots, lives)
            scatter(slots, dkv)
            return total + dq

        total = lax.fori_loop(0, chunks, chunk_step, jnp.zeros((BLK, WIDE), F32))
        moved = jnp.where(is_odd, swap_halves(total), total)
        dq_ref[spot, :] = jnp.where(upper == is_odd, moved, dq_ref[spot, :].astype(F32)).astype(BF16)

    for_long(place, table_ref, nquery, nrows, long_body)
    dkv_ref[...] = sum_ref[...].astype(BF16)


def local_call(kernel, name, out_shape, nvmem, scratch=()):
    return pl.pallas_call(
        kernel,
        out_shape=out_shape,
        in_specs=[IN_SMEM] + [IN_VMEM] * nvmem,
        out_specs=jax.tree.map(lambda _: IN_VMEM, out_shape),
        scratch_shapes=list(scratch),
        name=name,
        cost_estimate=pl.CostEstimate(flops=30 << 30, bytes_accessed=8 << 20, transcendentals=0),
        compiler_params=pltpu.CompilerParams(vmem_limit_bytes=56 << 20),
    )


class GradScatter:
    def __init__(self, place, source, bufs, sems):
        self.place, self.source = place, source
        self.land, self.pair, self.far = bufs
        self.send1, self.recv1, self.send2, self.recv2 = sems

    @staticmethod
    def buffers(dims, band, cols):
        heads, share = dims[:2]
        return [
            vmem(max(share - 1, 1), heads, band, cols),
            vmem(heads, band, cols),
            vmem(max(heads - 1, 1), band, cols),
        ]

    @staticmethod
    def semaphores(dims, count):
        return [dma(count, dims[1] - 1)] * 2 + [dma(count, dims[0] - 1)] * 2

    def near(self, step):
        other, device = self.place.partner(step)
        return remote(
            self.source.at[:, other], self.land.at[step - 1],
            self.send1.at[step - 1], self.recv1.at[step - 1], device,
        )

    def across(self, step):
        other, device = self.place.across(step)
        return remote(
            self.pair.at[other], self.far.at[step - 1],
            self.send2.at[step - 1], self.recv2.at[step - 1], device,
        )

    def start_near(self):
        for step in range(1, self.place.share):
            self.near(step).start()

    def start_across(self):
        place = self.place
        for step in range(1, place.share):
            self.near(step).wait_recv()

        def body(head, carry):
            parts = [self.source[head, place.part]]
            parts += [self.land[step, head] for step in range(place.share - 1)]
            self.pair[head] = add_up(*parts).astype(BF16)
            return carry

        lax.fori_loop(0, place.heads, body, 0)
        for step in range(1, place.heads):
            self.across(step).start()

    def result(self):
        heads = self.place.heads
        for step in range(1, heads):
            self.across(step).wait_recv()
        return add_up(self.pair[self.place.head], *[self.far[step] for step in range(heads - 1)])

    def finish(self):
        for step in range(1, self.place.share):
            self.near(step).wait_send()
        for step in range(1, self.place.heads):
            self.across(step).wait_send()


def gelu_pair(value):
    root = math.sqrt(2.0 / math.pi)
    square = value * value
    curve = jnp.tanh(root * value * (1.0 + 0.044715 * square))
    half = 0.5 * (1.0 + curve)
    slope = half + 0.5 * value * (1.0 - curve * curve) * (root * (1.0 + 3 * 0.044715 * square))
    return value * half, slope


def rounds_of(tokens):
    return max(1, min(ROUNDS, tokens // (2 * BLK)))


def middle_kernel(
    dims,
    o_ref, xt_ref, g_ref, wo_ref, ob_ref, gain_ref, shift_ref, wi_ref, ib_ref, wu_ref,
    sum_out, do_out, da_out, mixed_out, vec_out, gi_out, gu_out,
    o_in, x1, xhat, scale, h2, act, dpre, outb, terms, from_left, from_right, do_buf, ib_sum, gi, gu,
    *rest,
):
    place = Place(dims)
    heads, share, nseq, ntp = dims
    head, part, seq, tp = place.head, place.part, place.seq, place.tp
    lands, sems = rest[:6], rest[6:]
    (o_s, o_r, hr_s, hr_r, hl_s, hl_r, tr_s, tr_r, tl_s, tl_r, do_s, do_r,
     g1_s, g1_r, g2_s, g2_r, local) = sems
    rows, width = g_ref.shape[1:]
    features = width * ntp
    tokens = rows // ntp
    rounds = rounds_of(tokens)
    span = tokens // rounds
    places = 2 * ntp - 1
    band = features // heads
    per = features // WIDE

    def packed_rows(index, count=tokens // 2):
        return pl.ds(pl.multiple_of(index * count, count), count)

    def span_of(index):
        return pl.ds(pl.multiple_of(index * span, span), span)

    def o_copy(step):
        to_head, to_tp, device = place.apart(step)
        return remote(
            o_ref.at[to_head, packed_rows(to_tp)], o_in.at[tp * heads + head],
            o_s.at[step], o_r.at[step], device,
        )

    def do_copy(index, step):
        to_head, to_tp, device = place.apart(step)
        count = span // 2
        return remote(
            do_buf.at[to_tp * heads + to_head, packed_rows(index, count)],
            do_out.at[head, packed_rows(tp * rounds + index, count)],
            do_s.at[index, step], do_r.at[index, step], device,
        )

    def h2_copy(index, owner, right):
        spot = h2.at[owner, span_of(index)]
        if right:
            return remote(spot, spot, hr_s.at[index, owner], hr_r.at[index, owner], (seq, tp + 1))
        return remote(spot, spot, hl_s.at[index, owner], hl_r.at[index, owner], (seq, tp - 1))

    def term_copy(index, owner, right):
        here = span_of(index)
        if right:
            return remote(
                terms.at[owner, here], from_left.at[owner, here],
                tr_s.at[index, owner], tr_r.at[index, owner], (seq, tp + 1),
            )
        return remote(
            terms.at[owner, here], from_right.at[owner, here],
            tl_s.at[index, owner], tl_r.at[index, owner], (seq, tp - 1),
        )

    scatters = [
        GradScatter(
            place, source, lands[3 * k : 3 * k + 3], (g1_s.at[k], g1_r.at[k], g2_s.at[k], g2_r.at[k])
        )
        for k, source in enumerate((gi, gu))
    ]

    greet(
        [place.partner(step)[1] for step in range(1, share)]
        + [place.apart(step)[2] for step in range(1, heads * ntp)]
    )
    for step in range(heads * ntp - 1, 0, -1):
        o_copy(step).start()
    o_in[tp * heads + head] = o_ref[head, packed_rows(tp)]
    ib_sum[...] = jnp.zeros_like(ib_sum)
    for step in range(1, heads * ntp):
        o_copy(step).wait_recv()

    for index in range(rounds):
        here = slice(index * span, (index + 1) * span)
        half = slice(index * span // 2, (index + 1) * span // 2)
        mixed = jnp.concatenate(
            [unpack_pair(o_in[i, half], o_in[i + 1, half]) for i in range(0, heads * ntp, 2)], axis=1
        )
        mixed_out[here] = mixed
        base = jnp.concatenate([xt_ref[i, here] for i in range(ntp)], axis=1).astype(F32)
        value = base + ob_ref[...] + jnp.dot(mixed, wo_ref[...], preferred_element_type=F32)
        x1[here] = value
        centered = value - jnp.sum(value, axis=1, keepdims=True) * (1.0 / features)
        spread = jnp.sum(centered * centered, axis=1, keepdims=True) * (1.0 / features)
        inverse = lax.rsqrt(spread + 1e-05)
        normed = centered * inverse
        xhat[here] = normed
        scale[here] = jnp.broadcast_to(inverse, (span, WIDE))
        h2[tp, here] = (normed * gain_ref[...] + shift_ref[...]).astype(BF16)

        @pl.when(tp < ntp - 1)
        def _():
            h2_copy(index, tp, True).start()

        @pl.when(tp > 0)
        def _():
            h2_copy(index, tp, False).start()

    def spot_of(position):
        hop = (position + 1) // 2
        owner = tp + jnp.where(position % 2 == 1, -hop, hop)
        return owner, (owner >= 0) & (owner < ntp)

    def feed(index, owner):
        @pl.when(owner < tp)
        def _():
            h2_copy(index, owner, True).wait_recv()

            @pl.when(tp < ntp - 1)
            def _():
                h2_copy(index, owner, True).start()

        @pl.when(owner > tp)
        def _():
            h2_copy(index, owner, False).wait_recv()

            @pl.when(tp > 0)
            def _():
                h2_copy(index, owner, False).start()

        here = span_of(index)
        wide = span_of(owner * rounds + index)
        pre = jnp.dot(h2[owner, here], wi_ref[...], preferred_element_type=F32) + ib_ref[...]
        value, slope = gelu_pair(pre)
        value = value.astype(BF16)
        act[wide] = value
        grad = jnp.concatenate([g_ref[i, wide] for i in range(ntp)], axis=1)
        back = lax.dot_general(grad, wu_ref[...], NT, preferred_element_type=F32) * slope
        back = back.astype(BF16)
        dpre[wide] = back
        ib_sum[0:1, :] += jnp.sum(back.astype(F32), axis=0, keepdims=True)
        terms[owner, here] = lax.dot_general(
            back, wi_ref[...], NT, preferred_element_type=F32
        ).astype(BF16)

        @pl.when((owner > tp) & (tp == 0))
        def _():
            term_copy(index, owner, True).start()

        @pl.when((owner < tp) & (tp == ntp - 1))
        def _():
            term_copy(index, owner, False).start()

        out = jnp.dot(value, wu_ref[...], preferred_element_type=F32)
        out = out + jnp.where(owner == tp, x1[here], 0.0)
        for i in range(ntp):
            outb[i, wide] = out[:, i * width : (i + 1) * width].astype(BF16)

    def relay(index, step):
        here = span_of(index)
        owner = step

        @pl.when((owner > tp) & (tp > 0))
        def _():
            term_copy(index, owner, True).wait_recv()
            terms[owner, here] = add_up(terms[owner, here], from_left[owner, here]).astype(BF16)
            term_copy(index, owner, True).start()

        other = ntp - 1 - step

        @pl.when((other < tp) & (tp < ntp - 1))
        def _():
            term_copy(index, other, False).wait_recv()
            terms[other, here] = add_up(terms[other, here], from_right[other, here]).astype(BF16)
            term_copy(index, other, False).start()

    def feed_step(count, carry):
        index, position = count // places, count % places
        owner, inside = spot_of(position)

        @pl.when(inside)
        def _():
            feed(index, owner)

        @pl.when((index > 0) & (position > 0) & (position % 2 == 0))
        def _():
            relay(index - 1, position // 2)

        return carry

    lax.fori_loop(0, rounds * places, feed_step, 0)
    save = pltpu.make_async_copy(outb, sum_out, local.at[0])
    save.start()

    def inner_grad(index):
        left = h2[:, :, index * band : (index + 1) * band].reshape(rows, band)
        value = lax.dot_general(left, dpre[...], TN, preferred_element_type=F32)
        gi[index] = value.astype(BF16).reshape(gi.shape[1:])

    def outer_grad(index):
        many = ntp // heads
        left = jnp.concatenate([g_ref[i] for i in range(index * many, (index + 1) * many)], axis=1)
        value = lax.dot_general(left, act[...], TN, preferred_element_type=F32)
        gu[index] = value.astype(BF16).reshape(gu.shape[1:])

    work = [functools.partial(inner_grad, index) for index in range(heads)]
    work += [functools.partial(outer_grad, index) for index in range(heads)]
    share_out = -(-len(work) // (ntp - 1))
    for position in range(ntp - 1):
        relay(rounds - 1, position + 1)
        for item in work[position * share_out : (position + 1) * share_out]:
            item()
        if (position + 1) * share_out >= heads > position * share_out:
            scatters[0].start_near()
        if (position + 1) * share_out >= 2 * heads > position * share_out:
            scatters[1].start_near()

    for index in range(rounds):
        here = slice(index * span, (index + 1) * span)
        half = slice(index * span // 2, (index + 1) * span // 2)
        wide = span_of(tp * rounds + index)

        @pl.when(tp > 0)
        def _():
            term_copy(index, tp, True).wait_recv()

        @pl.when(tp < ntp - 1)
        def _():
            term_copy(index, tp, False).wait_recv()

        grad = terms[tp, here].astype(F32)
        grad = grad + jnp.where(tp > 0, from_left[tp, here].astype(F32), 0.0)
        grad = grad + jnp.where(tp < ntp - 1, from_right[tp, here].astype(F32), 0.0)
        hat = xhat[here]
        inner = grad * gain_ref[...]
        mean0 = jnp.sum(inner, axis=1, keepdims=True) * (1.0 / features)
        mean1 = jnp.sum(inner * hat, axis=1, keepdims=True) * (1.0 / features)
        tail = scale[here, 0:1] * (inner - mean0 - hat * mean1)
        cot = jnp.concatenate([g_ref[i, wide] for i in range(ntp)], axis=1).astype(F32)
        branch = (cot + tail).astype(BF16)
        da_out[here] = branch
        do = lax.dot_general(branch, wo_ref[...], NT, preferred_element_type=F32)
        for i in range(0, heads * ntp, 2):
            pair = pack_pair(do[:, i * HEAD_DIM : (i + 2) * HEAD_DIM])
            do_buf[i, half] = pair[0]
            do_buf[i + 1, half] = pair[1]
        for step in range(heads * ntp - 1, 0, -1):
            do_copy(index, step).start()
        sums = (
            jnp.sum(branch.astype(F32), axis=0, keepdims=True),
            jnp.sum(grad * hat, axis=0, keepdims=True),
            jnp.sum(grad, axis=0, keepdims=True),
        )
        for kind, value in enumerate(sums):
            for sub in range(per):
                row = slice(kind * per + sub, kind * per + sub + 1)
                piece = value[:, sub * WIDE : (sub + 1) * WIDE]
                if index == 0:
                    vec_out[row, :] = piece
                else:
                    vec_out[row, :] += piece
    own = pltpu.make_async_copy(
        do_buf.at[tp * heads + head], do_out.at[head, packed_rows(tp)], local.at[1]
    )
    own.start()
    for scatter in scatters:
        scatter.start_across()
    cot = jnp.sum(g_ref[tp].astype(F32), axis=0, keepdims=True)
    for sub in range(per):
        owner, lane = divmod(sub * WIDE, width)
        vec_out[3 * per + sub : 3 * per + sub + 1, :] = jnp.where(
            tp == owner, cot[:, lane : lane + WIDE], 0.0
        )
    for sub in range(ib_sum.shape[1] // WIDE):
        row = 4 * per + sub
        vec_out[row : row + 1, :] = ib_sum[0:1, sub * WIDE : (sub + 1) * WIDE]
    gi_out[...] = scatters[0].result()
    gu_out[...] = scatters[1].result()
    save.wait()
    own.wait()
    for step in range(1, heads * ntp):
        for index in range(rounds):
            do_copy(index, step).wait_recv()
    for step in range(1, heads * ntp):
        o_copy(step).wait_send()
        for index in range(rounds):
            do_copy(index, step).wait_send()
    for index in range(rounds):
        for owner in range(ntp):
            @pl.when((tp >= owner) & (tp < ntp - 1))
            def _():
                h2_copy(index, owner, True).wait_send()

            @pl.when((tp <= owner) & (tp > 0))
            def _():
                h2_copy(index, owner, False).wait_send()

            @pl.when(tp < owner)
            def _():
                term_copy(index, owner, True).wait_send()

            @pl.when(tp > owner)
            def _():
                term_copy(index, owner, False).wait_send()

    for scatter in scatters:
        scatter.finish()


def run_middle(dims, o, xt, g, wo, ob, gain, shift, wi, ib, wu):
    heads, share, nseq, ntp = dims
    _, rows, width = g.shape
    features, hidden = width * ntp, wi.shape[1]
    tokens, band = rows // ntp, features // nseq
    per = features // WIDE
    rounds = rounds_of(tokens)
    sds = jax.ShapeDtypeStruct
    outs = [
        sds((ntp, rows, width), BF16),
        sds((heads, rows // 2, WIDE), BF16),
        sds((tokens, features), BF16),
        sds((tokens, features), BF16),
        sds((4 * per + hidden // WIDE, WIDE), F32),
        sds((band, hidden), F32),
        sds((band, hidden), F32),
    ]
    count = heads * ntp
    scratch = [
        vmem(count, tokens // 2, WIDE),
        vmem(tokens, features, dtype=F32),
        vmem(tokens, features, dtype=F32),
        vmem(tokens, WIDE, dtype=F32),
        vmem(ntp, tokens, features),
        vmem(rows, hidden),
        vmem(rows, hidden),
        vmem(ntp, rows, width),
        vmem(ntp, tokens, features),
        vmem(ntp, tokens, features),
        vmem(ntp, tokens, features),
        vmem(count, tokens // 2, WIDE),
        vmem(8, hidden, dtype=F32),
        vmem(heads, share, band, hidden),
        vmem(heads, share, band, hidden),
        *GradScatter.buffers(dims, band, hidden),
        *GradScatter.buffers(dims, band, hidden),
    ]
    sems = (
        [dma(count)] * 2 + [dma(rounds, ntp)] * 8 + [dma(rounds, count)] * 2
        + GradScatter.semaphores(dims, 2) + [dma(2)]
    )
    return pl.pallas_call(
        functools.partial(middle_kernel, dims),
        out_shape=outs,
        in_specs=[IN_VMEM] * 10,
        out_specs=[ANYWHERE] * 2 + [IN_VMEM] * 5,
        scratch_shapes=scratch + sems,
        name="middle",
        compiler_params=pltpu.CompilerParams(
            collective_id=2, has_side_effects=True, vmem_limit_bytes=63 << 20
        ),
    )(o, xt, g, wo, ob, gain, shift, wi, ib, wu)


def tail_kernel(
    dims,
    dq_ref, dkv_ref, h1_ref, x_ref, stat_ref, gain_ref, wq_ref, wk_ref, wv_ref,
    da_ref, mixed_ref, vec_ref,
    gx_ref, ow_ref, oq_ref, vout_ref,
    dq_in, dkv_in, dkv_land, dkv_sum, all3, da_in, pbuf, from_left, from_right,
    sums, sums_land, vbuf, vec_land, vsum, vec_far, gw, g3, wbuf, wfar,
    *rest,
):
    place = Place(dims)
    heads, share, nseq, ntp = dims
    head, part, seq, tp = place.head, place.part, place.seq, place.tp
    lands, sems = rest[:6], rest[6:]
    (dq_s, dq_r, kv1_s, kv1_r, kv2_s, kv2_r, right_s, right_r, left_s, left_r,
     da_s, da_r, st_s, st_r, v1_s, v1_r, v2_s, v2_r, w_s, w_r, g1_s, g1_r, g2_s, g2_r) = sems
    rows, features = h1_ref.shape
    width = features // ntp
    tokens = rows // ntp
    local_width = wq_ref.shape[1]
    chunk_rows = rows // CHUNKS
    band = features // heads
    per = features // WIDE

    def chunk_of(chunk):
        return pl.ds(chunk * chunk_rows, chunk_rows)

    def half_of(chunk):
        return pl.ds(chunk * chunk_rows // 2, chunk_rows // 2)

    def columns_of(index):
        return pl.ds(pl.multiple_of(index * width, width), width)

    def dq_copy(chunk, step):
        other, device = place.across(step)
        return remote(
            dq_ref.at[other, half_of(chunk)], dq_in.at[head, half_of(chunk)],
            dq_s.at[chunk, step - 1], dq_r.at[chunk, step - 1], device,
        )

    def dkv_near(step):
        other, device = place.partner(step)
        return remote(
            dkv_ref.at[other], dkv_land.at[step - 1], kv1_s.at[step - 1], kv1_r.at[step - 1], device
        )

    def dkv_copy(chunk, step):
        other, device = place.across(step)
        return remote(
            dkv_sum.at[other, chunk_of(chunk)], dkv_in.at[head, chunk_of(chunk)],
            kv2_s.at[chunk, step - 1], kv2_r.at[chunk, step - 1], device,
        )

    def da_copy(step):
        other, device = place.along(step)
        return remote(
            da_ref.at[:, columns_of(other)], da_in.at[tp], da_s.at[step - 1], da_r.at[step - 1], device
        )

    def rightward(chunk, index):
        return remote(
            pbuf.at[chunk, index], from_left.at[chunk, index],
            right_s.at[chunk, index], right_r.at[chunk, index], (seq, tp + 1),
        )

    def leftward(chunk, index):
        return remote(
            pbuf.at[chunk, index], from_right.at[chunk, index],
            left_s.at[chunk, index], left_r.at[chunk, index], (seq, tp - 1),
        )

    def sums_copy(step):
        return remote(
            sums, sums_land.at[step - 1], st_s.at[step - 1], st_r.at[step - 1], place.along(step)[1]
        )

    def vec_copy(step):
        return remote(
            vbuf, vec_land.at[step - 1], v1_s.at[step - 1], v1_r.at[step - 1],
            (lax.rem(seq + step, nseq), tp),
        )

    def vec_far_copy(step):
        return remote(
            vsum, vec_far.at[step - 1], v2_s.at[step - 1], v2_r.at[step - 1], place.along(step)[1]
        )

    def w_copy(step):
        other, device = place.along(step)
        return remote(wbuf.at[other], wfar.at[step - 1], w_s.at[step - 1], w_r.at[step - 1], device)

    scatters = [
        GradScatter(
            place, source, lands[3 * k : 3 * k + 3], (g1_s.at[k], g1_r.at[k], g2_s.at[k], g2_r.at[k])
        )
        for k, source in enumerate((gw, g3))
    ]

    greet(
        [(lax.rem(seq + step, nseq), tp) for step in range(1, nseq)]
        + [place.along(step)[1] for step in range(1, ntp)]
    )
    for step in range(1, share):
        dkv_near(step).start()
    for chunk in range(CHUNKS):
        for step in range(1, heads):
            dq_copy(chunk, step).start()
    dq_in[head] = dq_ref[head]
    for index in range(heads):
        value = lax.dot_general(
            da_ref[:, index * band : (index + 1) * band], mixed_ref[...], TN, preferred_element_type=F32
        )
        gw[index] = value.astype(BF16).reshape(gw.shape[1:])
    for step in range(1, share):
        dkv_near(step).wait_recv()
    scatters[0].start_near()
    for chunk in range(CHUNKS):
        for target in range(heads):
            where = (target, chunk_of(chunk))
            parts = [dkv_ref[(part,) + where]]
            parts += [dkv_land[(step,) + where] for step in range(share - 1)]
            dkv_sum[where] = add_up(*parts).astype(BF16)
        for step in range(1, heads):
            dkv_copy(chunk, step).start()
    dkv_in[head] = dkv_sum[head]
    vbuf[: 2 * per] = jnp.zeros((2 * per, WIDE), F32)
    vbuf[2 * per : 6 * per] = vec_ref[: 4 * per]
    narrow = 3 * local_width // WIDE
    vbuf[6 * per : 6 * per + narrow] = jnp.zeros((narrow, WIDE), F32)
    vbuf[6 * per + narrow :] = vec_ref[4 * per :]
    scatters[0].start_across()

    gain = gain_ref[...]
    lane = lax.broadcasted_iota(jnp.int32, (chunk_rows, WIDE), 1)

    def partial_step(chunk):
        here, half = chunk_of(chunk), half_of(chunk)
        for step in range(1, heads):
            dq_copy(chunk, step).wait_recv()
            dkv_copy(chunk, step).wait_recv()
        three = [[], [], []]
        for i in range(0, heads, 2):
            three[0].append(unpack_pair(dq_in[i, half], dq_in[i + 1, half]))
            k, v = mix_pair(dkv_in[i, here].astype(F32), dkv_in[i + 1, here].astype(F32))
            three[1].append(k.astype(BF16))
            three[2].append(v.astype(BF16))
        three = [jnp.concatenate(item, axis=1) for item in three]
        grad = 0.125 * lax.dot_general(three[0], wq_ref[...], NT, preferred_element_type=F32)
        grad = grad + lax.dot_general(three[1], wk_ref[...], NT, preferred_element_type=F32)
        grad = grad + lax.dot_general(three[2], wv_ref[...], NT, preferred_element_type=F32)
        row = 6 * per
        for kind, value in enumerate(three):
            all3[here, kind * local_width : (kind + 1) * local_width] = value
            column = jnp.sum(value.astype(F32), axis=0, keepdims=True)
            for start in range(0, local_width, WIDE):
                vbuf[row : row + 1, :] += column[:, start : start + WIDE]
                row += 1
        mean, scale = stat_ref[here, 0:1], stat_ref[here, 1:2]
        sum0 = jnp.zeros((chunk_rows, 1), F32)
        sum1 = jnp.zeros((chunk_rows, 1), F32)
        for index in range(ntp):
            cols = slice(index * width, (index + 1) * width)
            piece = grad[:, cols]
            xhat = (x_ref[index, here].astype(F32) - mean) * scale
            weighted = piece * gain[:, cols]
            sum0 = sum0 + jnp.sum(weighted, axis=1, keepdims=True)
            sum1 = sum1 + jnp.sum(weighted * xhat, axis=1, keepdims=True)
            col0 = jnp.sum(piece * xhat, axis=0, keepdims=True)
            col1 = jnp.sum(piece, axis=0, keepdims=True)
            for sub in range(width // WIDE):
                row = index * (width // WIDE) + sub
                lanes = slice(sub * WIDE, (sub + 1) * WIDE)
                vbuf[row : row + 1, :] += col0[:, lanes]
                vbuf[per + row : per + row + 1, :] += col1[:, lanes]
            pbuf[chunk, index] = piece.astype(BF16)
        both = jnp.where(lane == 0, sum0, jnp.where(lane == 1, sum1, 0.0))
        sums[:, here] = both.T[:8]

    def pass_on(chunk):
        for step in range(ntp - 1):
            far = ntp - 1 - step

            @pl.when(tp < far)
            def _():
                @pl.when(tp > 0)
                def _():
                    rightward(chunk, far).wait_recv()
                    pbuf[chunk, far] = add_up(pbuf[chunk, far], from_left[chunk, far]).astype(BF16)

                rightward(chunk, far).start()

            @pl.when(tp > step)
            def _():
                @pl.when(tp < ntp - 1)
                def _():
                    leftward(chunk, step).wait_recv()
                    pbuf[chunk, step] = add_up(pbuf[chunk, step], from_right[chunk, step]).astype(BF16)

                leftward(chunk, step).start()

    for chunk in range(CHUNKS):
        partial_step(chunk)
        if chunk > 0:
            pass_on(chunk - 1)
    for step in range(1, ntp):
        sums_copy(step).start()
    for step in range(1, nseq):
        vec_copy(step).start()
    for step in range(1, ntp):
        da_copy(step).start()
    da_in[tp] = da_ref[:, columns_of(tp)]

    def grad_step(index, carry):
        left = h1_ref[:, pl.ds(pl.multiple_of(index * band, band), band)]
        value = lax.dot_general(left, all3[...], TN, preferred_element_type=F32)
        g3[index] = value.astype(BF16).reshape(g3.shape[1:])
        return carry

    lax.fori_loop(0, heads, grad_step, 0)
    scatters[1].start_near()
    pass_on(CHUNKS - 1)
    for step in range(1, nseq):
        vec_copy(step).wait_recv()
    total = vbuf[...]
    for step in range(nseq - 1):
        total = total + vec_land[step]
    vsum[...] = total
    for step in range(1, ntp):
        vec_far_copy(step).start()
    scatters[1].start_across()
    value = scatters[0].result().astype(BF16)
    for index in range(ntp):
        wbuf[index] = value[:, index * local_width : (index + 1) * local_width]
    for step in range(1, ntp):
        w_copy(step).start()

    for step in range(1, ntp):
        sums_copy(step).wait_recv()
        da_copy(step).wait_recv()
    my_gain = gain_ref[:, columns_of(tp)]
    da_rows = da_in.shape[1]
    for chunk in range(CHUNKS):
        here = chunk_of(chunk)
        both = sums[:, here]
        for step in range(ntp - 1):
            both = both + sums_land[step, :, here]
        both = jnp.concatenate([both, jnp.zeros((WIDE - 8, chunk_rows), F32)], axis=0).T
        both = both * (1.0 / features)

        @pl.when(tp > 0)
        def _():
            rightward(chunk, tp).wait_recv()

        @pl.when(tp < ntp - 1)
        def _():
            leftward(chunk, tp).wait_recv()

        grad = pbuf[chunk, tp].astype(F32)
        grad = grad + jnp.where(tp > 0, from_left[chunk, tp].astype(F32), 0.0)
        grad = grad + jnp.where(tp < ntp - 1, from_right[chunk, tp].astype(F32), 0.0)
        mean, scale = stat_ref[here, 0:1], stat_ref[here, 1:2]
        xhat = (x_ref[tp, here].astype(F32) - mean) * scale
        inner = grad * my_gain - both[:, 0:1] - xhat * both[:, 1:2]
        many = chunk_rows // da_rows
        branch = da_in[chunk * many : (chunk + 1) * many].reshape(chunk_rows, width)
        gx_ref[here] = branch.astype(F32) + scale * inner
    oq_ref[...] = scatters[1].result()
    for step in range(1, ntp):
        vec_far_copy(step).wait_recv()
        w_copy(step).wait_recv()
    vout_ref[...] = vsum[...]
    for step in range(ntp - 1):
        vout_ref[: 6 * per] += vec_far[step, : 6 * per]
    ow_ref[...] = add_up(wbuf[tp], *[wfar[step] for step in range(ntp - 1)])

    for step in range(1, share):
        dkv_near(step).wait_send()
    for chunk in range(CHUNKS):
        for step in range(1, heads):
            dq_copy(chunk, step).wait_send()
            dkv_copy(chunk, step).wait_send()
        for index in range(ntp):
            @pl.when(tp < index)
            def _():
                rightward(chunk, index).wait_send()

            @pl.when(tp > index)
            def _():
                leftward(chunk, index).wait_send()

    for step in range(1, ntp):
        sums_copy(step).wait_send()
        da_copy(step).wait_send()
        vec_far_copy(step).wait_send()
        w_copy(step).wait_send()
    for step in range(1, nseq):
        vec_copy(step).wait_send()
    for scatter in scatters:
        scatter.finish()


def run_tail(dims, dq, dkv, h1, x_parts, stats, gain, wq, wk, wv, da, mixed, vec):
    heads, share, nseq, ntp = dims
    rows, features = h1.shape
    width, tokens = features // ntp, rows // ntp
    band = features // nseq
    local_width = wq.shape[1]
    per = features // WIDE
    sds = jax.ShapeDtypeStruct
    nvec = vec.shape[0] + 2 * per + 3 * local_width // WIDE
    outs = [
        sds((rows, width), F32),
        sds((band, local_width), F32),
        sds((band, 3 * local_width), F32),
        sds((nvec, WIDE), F32),
    ]
    pieces = (CHUNKS, ntp, rows // CHUNKS, width)
    scratch = [
        vmem(heads, rows // 2, WIDE),
        vmem(heads, rows, WIDE),
        vmem(max(share - 1, 1), heads, rows, WIDE),
        vmem(heads, rows, WIDE),
        vmem(rows, 3 * local_width),
        vmem(ntp, tokens, width),
        vmem(*pieces),
        vmem(*pieces),
        vmem(*pieces),
        vmem(8, rows, dtype=F32),
        vmem(ntp - 1, 8, rows, dtype=F32),
        vmem(nvec, WIDE, dtype=F32),
        vmem(nseq - 1, nvec, WIDE, dtype=F32),
        vmem(nvec, WIDE, dtype=F32),
        vmem(ntp - 1, nvec, WIDE, dtype=F32),
        vmem(heads, share, band, features),
        vmem(heads, share, band, 3 * local_width),
        vmem(ntp, band, local_width),
        vmem(ntp - 1, band, local_width),
        *GradScatter.buffers(dims, band, features),
        *GradScatter.buffers(dims, band, 3 * local_width),
    ]
    sems = (
        [dma(CHUNKS, heads - 1)] * 2 + [dma(share - 1)] * 2 + [dma(CHUNKS, heads - 1)] * 2
        + [dma(CHUNKS, ntp)] * 4 + [dma(ntp - 1)] * 4 + [dma(nseq - 1)] * 2 + [dma(ntp - 1)] * 4
        + GradScatter.semaphores(dims, 2)
    )
    return pl.pallas_call(
        functools.partial(tail_kernel, dims),
        out_shape=outs,
        in_specs=[IN_VMEM] * 12,
        out_specs=[IN_VMEM] * len(outs),
        scratch_shapes=scratch + sems,
        name="tail",
        compiler_params=pltpu.CompilerParams(
            collective_id=3, has_side_effects=True, vmem_limit_bytes=60 << 20
        ),
    )(dq, dkv, h1, x_parts, stats, gain, wq, wk, wv, da, mixed, vec)


def on_device(
    hidden_in,
    norm_gain,
    norm_shift,
    query_weight,
    query_bias,
    key_weight,
    value_weight,
    value_bias,
    output_weight,
    output_bias,
    feed_gain,
    feed_shift,
    inner_weight,
    inner_bias,
    outer_weight,
    outer_bias,
    doc_blocks,
    doc_padding,
    random_picks,
    cotangent,
):
    nrows, block_len, width = hidden_in.shape
    rows = nrows * block_len
    nseq, ntp = lax.axis_size("seq"), lax.axis_size("tp")
    tp = lax.axis_index("tp")
    local_width = query_weight.shape[1]
    heads = local_width // HEAD_DIM
    share = nseq // heads
    dims = (heads, share, nseq, ntp)
    features = width * ntp
    per = features // WIDE
    g_parts = lax.all_gather(cotangent.reshape(rows, width), "tp", axis=0)
    output_full = lax.all_gather(output_weight, "tp", axis=0, tiled=True)
    q, kv, h1, x_parts, x_mine, stats, table = run_head(
        dims, nrows, doc_blocks, doc_padding, random_picks.T, hidden_in.reshape(rows, width),
        norm_gain[None, :], norm_shift[None, :], query_weight, query_bias[None, :],
        key_weight, value_weight, value_bias[None, :],
    )
    q = q.reshape(heads * rows, WIDE)
    kv = kv.reshape(nseq * rows, WIDE)
    sds = jax.ShapeDtypeStruct
    packed, res = local_call(
        functools.partial(forward_kernel, dims, nrows, 1),
        "attention_forward",
        (sds((heads * rows // 2, WIDE), BF16), sds((heads * rows, WIDE), F32)),
        2,
    )(table, q, kv)
    out_sum, do, da, mixed, vec, inner_part, outer_part = run_middle(
        dims, packed.reshape(heads, rows // 2, WIDE), x_mine, g_parts, output_full,
        output_bias[None, :], feed_gain[None, :], feed_shift[None, :],
        inner_weight, inner_bias[None, :], outer_weight,
    )
    result = lax.psum_scatter(out_sum, "tp", scatter_dimension=0)
    dq, dkv = local_call(
        functools.partial(backward_kernel, dims, nrows, 1),
        "attention_backward",
        (sds((heads * rows // 2, WIDE), BF16), sds((nseq * rows, WIDE), BF16)),
        4,
        [pltpu.VMEM((nseq * rows, WIDE), F32)],
    )(table, q, do.reshape(heads * rows // 2, WIDE), res, kv)
    grad_x, output_part, qkv_part, vectors = run_tail(
        dims, dq.reshape(heads, rows // 2, WIDE), dkv.reshape(share, heads, rows, WIDE), h1, x_parts,
        stats, norm_gain[None, :], query_weight, key_weight, value_weight, da, mixed, vec,
    )
    my_bias = lax.dynamic_slice_in_dim(outer_bias, tp * width, width, 0)
    layer_out = (result.astype(F32) + my_bias).astype(BF16).reshape(hidden_in.shape)
    wide = vectors[: 6 * per].reshape(6, features)
    narrow = vectors[6 * per :].reshape(-1)
    return (
        layer_out,
        grad_x.reshape(hidden_in.shape),
        wide[0],
        wide[1],
        0.125 * qkv_part[:, :local_width],
        0.125 * narrow[:local_width],
        qkv_part[:, local_width : 2 * local_width],
        qkv_part[:, 2 * local_width :],
        narrow[2 * local_width : 3 * local_width],
        output_part.T,
        wide[2],
        wide[3],
        wide[4],
        inner_part,
        narrow[3 * local_width :],
        outer_part.T,
        wide[5],
    )


def solution(mesh):
    return jax.shard_map(
        on_device,
        mesh=mesh,
        in_specs=(
            P(None, "seq", "tp"),
            P(),
            P(),
            P(None, "tp"),
            P("tp"),
            P(None, "tp"),
            P(None, "tp"),
            P("tp"),
            P("tp", None),
            P(),
            P(),
            P(),
            P(None, "tp"),
            P("tp"),
            P("tp", None),
            P(),
            P(),
            P(),
            P(),
            P(None, "seq", "tp"),
        ),
        out_specs=(
            P(None, "seq", "tp"),
            P(None, "seq", "tp"),
            P(),
            P(),
            P("seq", "tp"),
            P("tp"),
            P("seq", "tp"),
            P("seq", "tp"),
            P("tp"),
            P("tp", "seq"),
            P(),
            P(),
            P(),
            P("seq", "tp"),
            P("tp"),
            P("tp", "seq"),
            P(),
        ),
        check_vma=False,
    )
```

time: 583 us -> 391 us (0.67); the launches traced: 572 us -> 390 us
  waiting for transfers between devices: 246 us -> 1.4 us
  Pallas kernels: 147 us -> 363 us
  local copies, waits for them, and re-layouts: 53.9 us -> 6.63 us
  matrix products: 46.6 us -> 0 us
  other arithmetic: 41.4 us -> 5.05 us
  blocking collectives: 11.4 us -> 0 us
  starting transfers between devices: 11.5 us -> 0.11 us
    pallas_call x2 -> x4, Pallas kernels: 58.2 us -> 269 us  [the longest x1 127 us: run_middle(): pl.pallas_call(functools.partial(middle_kernel, dims), out_shape=outs, in...]
    all_gather x5 -> x2, waiting for transfers between devices: 146 us -> 0.01 us  [the longest x1 0.01 us: on_device(): g_parts = lax.all_gather(cotangent.reshape(rows, width), 'tp', axis=0)]
    reduce_scatter x3 -> x1, waiting for transfers between devices: 65.9 us -> 0.01 us  [on_device(): result = lax.psum_scatter(out_sum, 'tp', scatter_dimension=0)]
    dot_general x11 -> x0, matrix products: 46.6 us -> none  [the longest x3 14 us: cols_product(): return lax.dot_general(left, right, NT, preferred_element_type=jnp.float32)]
    all_to_all x3 -> x0, waiting for transfers between devices: 32.7 us -> none  [swap_heads(): lax.all_to_all(value, 'seq', 0, 0, axis_index_groups=across, tiled=True)]
    reduce_sum x13 -> x0, other arithmetic: 18.8 us -> none  [the longest x1 4.54 us: attention_tables(): lives = filled * jnp.sum(onehot * live[None, None, :], axis=2)]
    unnamed x81 -> x10, local copies, waits for them, and re-layouts: 21.3 us -> 4.52 us
    convert_element_type x7 -> x1, other arithmetic: 16.3 us -> 1.94 us  [on_device(): (result.astype(F32) + my_bias).astype(BF16).reshape(hidden_in.shape)]
  transfers between devices with their start and end apart: 11 -> 3, of which waited for: 9 -> 0; matrix products, arithmetic and copies ran while one was open for 16% -> 2% of each run, Pallas kernels for 21% -> 61%
where the time goes in v3:
time: 391 us; the launch traced here: 390 us
  Pallas kernels  363 us (93%)
  between operations  13.8 us (4%)
  local copies, waits for them, and re-layouts  6.63 us (2%)
  other arithmetic  5.05 us (1%)
    pallas_call x1, Pallas kernels, run_middle(): pl.pallas_call(functools.partial(middle_kernel, dims), out_shape=outs, in...  127 us
    pallas_call x1, Pallas kernels, run_tail(): pl.pallas_call(functools.partial(tail_kernel, dims), out_shape=outs, in_s...  94.6 us
    pallas_call x1, Pallas kernels, run_head(): pl.pallas_call(functools.partial(head_kernel, dims, nrows), out_shape=out...  79.9 us
    pallas_call x1, Pallas kernels, on_device(): local_call(functools.partial(backward_kernel, dims, nrows, 1), 'attention...  32.6 us
    pallas_call x1, Pallas kernels, on_device(): local_call(functools.partial(forward_kernel, dims, nrows, 1), 'attention_...  29.3 us
  transfers between devices with their start and end apart: 3, of which 0 were waited for; matrix products, arithmetic and copies ran while one was open for 2% of the time, Pallas kernels for 61%

profile of v3, /device:TPU:8, one launch (start us, length us, event | category | flops | bytes accessed | tf_op | source)
XLA Modules:
  0.0 390.2 jit_solution(5928829967441067721)
XLA Ops:
  7.2 0.0 all-gather.3.cloned.1.call-start
  7.2 0.7 all-gather.3.cloned.1.call-update
  7.9 0.0 all-gather.5.cloned.1.call-start
  8.0 0.7 all-gather.5.cloned.1.call-update
  8.7 0.0 reduce-scatter.2.cloned.1.call-start
  8.7 79.9 %head.1 = (bf16[4,1024,128]{2,1,0:T(8,128)(2,1)}, bf16[2,4,1024,128]{3,2,1,0:T(8,128)(2,1)}, bf16[1024,1024]{1,0:T(8,128)(2,1)}, bf16[4,1024,256]{2,1,0:T(8,128)...) custom-call(s32[32]{0:T(128)} %docs_ref.1, s32[32]{0:T(128)} %pads_ref.1, ...), custom_call_target="tpu_custom_call" | custom-call | tf_op jit(solution)/shard_map/head/pallas_call | solution.py:367
  88.6 29.3 %attention_forward.1 = (bf16[2048,128]{1,0:T(8,128)(2,1)}, f32[4096,128]{1,0:T(8,128)}) custom-call(s32[16,128]{1,0:T(8,128)} %get-tuple-element.39.table_ref, bf16[4096,128]{1,0:T(8,128)(2,1)} %bitcast.61, bf16[8192,128]{1,0:T(8,128)(2,1)} %bitcast.59), custom_call_target="tpu_custom_call" | custom-call | flops 32212254720 | bytes 8388608 | tf_op jit(solution)/shard_map/attention_forward/pallas_call | solution.py:1416
  117.9 126.8 %middle.1 = (bf16[4,1024,256]{2,1,0:T(8,128)(2,1)}, bf16[4,512,128]{2,1,0:T(8,128)(2,1)}, bf16[256,1024]{1,0:T(8,128)(2,1)}, bf16[256,1024]{1,0:T(8,128)(2,1)}, ...) custom-call(bf16[4,512,128]{2,1,0:T(8,128)(2,1)} %bitcast.42, ...), custom_call_target="tpu_custom_call" | custom-call | tf_op jit(solution)/shard_map/middle/pallas_call | solution.py:1004
  244.7 0.0 reduce-scatter.2.cloned.1.call-update
  244.8 0.8 dynamic_slice.3
  245.5 32.6 %attention_backward.1 = (bf16[2048,128]{1,0:T(8,128)(2,1)}, bf16[8192,128]{1,0:T(8,128)(2,1)}) custom-call(s32[16,128]{1,0:T(8,128)} %get-tuple-element.39.table_ref, bf16[4096,128]{1,0:T(8,128)(2,1)} %bitcast.62, bf16[2048,128]{1,0:T(8,128)(2,1)} %bitcast.63, f32[4096,128]{1,0:T(8,128)} %get-tuple-element.46.res_ref, bf16[8192,128]{1,0:T(8,128)(2,1)} %bitcast.60), custom_call_target="tpu_custom_call" | custom-call | flops 32212254720 | bytes 8388608 | tf_op jit(solution)/shard_map/attention_backward/pallas_call | solution.py:1428
  278.2 94.6 %tail.1 = (f32[1024,256]{1,0:T(8,128)}, f32[128,256]{1,0:T(8,128)}, f32[128,768]{1,0:T(8,128)}, f32[62,128]{1,0:T(8,128)}) custom-call(bf16[4,512,128]{2,1,0:T(8,128)(2,1)} %bitcast.43, bf16[2,4,1024,128]{3,2,1,0:T(8,128)(2,1)} %bitcast.40, bf16[1024,1024]{1,0:T(8,128)(2,1)} %get-tuple-element.49.h1_ref, bf16[4,1024,256]{2,1,0:T(8,128)(2,1)} %get-tuple-element.50.x_ref, ...), custom_call_target="tpu_custom_call" | custom-call | tf_op jit(solution)/shard_map/tail/pallas_call | solution.py:1361
  372.8 0.0 copy-start
  372.8 1.7 copy.39
  374.6 0.0 copy-done.2
  374.6 1.0 copy.40
  375.6 1.3 slice_bitcast_fusion.7
  376.9 1.3 slice_bitcast_fusion
  378.2 1.8 fusion.1
  380.0 1.9 fusion
  381.9 0.0 copy-done
  382.0 1.0 copy.43
  382.9 0.0 copy-done.1
  382.9 0.8 copy.44
  (5 shorter events, 0.0 us)
Async XLA Ops:
  7.2 110.7 %all-gather.3.cloned.1.call-start = ((), (), s32[]{:S(2)}) async-start(), calls=%async_computation.1 | async-start | bytes 2621440 | tf_op jit(solution)/shard_map/all_gather | solution.py:1406
  7.9 110.0 %all-gather.5.cloned.1.call-start = ((), (), s32[]{:S(2)}) async-start(), calls=%async_computation.2 | async-start | bytes 2621440 | tf_op jit(solution)/shard_map/all_gather | solution.py:1407
  8.7 371.3 %reduce-scatter.2.cloned.1.call-start = ((), (), s32[]{:S(2)}) async-start(), calls=%async_computation.3 | async-start | bytes 2621440 | tf_op jit(solution)/shard_map/reduce_scatter | solution.py:1427
  278.2 96.4 %copy-start.2 = (f32[128,1024]{1,0:T(8,128)S(1)}, f32[128,1024]{1,0:T(8,128)}, u32[]{:S(2)}) copy-start(f32[128,1024]{1,0:T(8,128)} %get-tuple-element.60) | copy-start | bytes 1572868
  372.8 9.2 %copy-start = (f32[1024,256]{1,0:T(8,128)S(1)}, f32[1024,256]{1,0:T(8,128)}, u32[]{:S(2)}) copy-start(f32[1024,256]{1,0:T(8,128)} %get-tuple-element.55) | copy-start | bytes 3145732
  375.5 7.4 %copy-start.1 = (f32[128,1024]{1,0:T(8,128)S(1)}, f32[128,1024]{1,0:T(8,128)}, u32[]{:S(2)}) copy-start(f32[128,1024]{1,0:T(8,128)} %get-tuple-element.137) | copy-start | bytes 1572868
Sparse Core Ops, SparseCore 0:
  9.6 57.9 all-gather.2
  69.2 46.7 all-gather.4
  244.9 44.7 reduce-scatter.1

commit v4 on v3

--- a/solution.py
+++ b/solution.py
@@ -14,6 +14,7 @@
 SLOTS = 8
 WIDE = 2 * HEAD_DIM
 CHUNKS = 4
+COT_CHUNKS = 1
 ROUNDS = 2
 NEG = -1e30
 NT = (((1,), (1,)), ((), ()))
@@ -174,9 +175,10 @@
 
 def head_kernel(
     dims, nrows, docs_ref, pads_ref, picks_ref, x_ref, gain_ref, shift_ref,
-    wq_ref, bq_ref, wk_ref, wv_ref, bv_ref,
-    q_out, kv_out, h1_out, xs_out, xt_out, stat_out, table_out,
-    xs, h1, qbuf, kvbuf, right_s, right_r, left_s, left_r, q_s, q_r, kv_s, kv_r, on_s, on_r, local,
+    wq_ref, bq_ref, wk_ref, wv_ref, bv_ref, cot_ref, wo_ref,
+    q_out, kv_out, h1_out, xs_out, g_out, rest_out, wo_out, xt_out, stat_out, table_out,
+    xs, h1, qbuf, kvbuf, right_s, right_r, left_s, left_r, q_s, q_r, kv_s, kv_r, on_s, on_r,
+    wz_s, wz_r, wa_s, wa_r, wp_s, wp_r, local,
 ):
     place = Place(dims)
     heads, share, nseq, ntp = dims
@@ -188,14 +190,19 @@
     def chunk_of(chunk):
         return pl.ds(chunk * chunk_rows, chunk_rows)
 
+    def traveller(chunk, index):
+        if chunk < CHUNKS:
+            return xs.at[index, chunk_of(chunk)]
+        return g_out.at[index, chunk_of(chunk - CHUNKS)]
+
     def rightward(chunk, index):
-        spot = xs.at[index, chunk_of(chunk)]
+        spot = traveller(chunk, index)
         return remote(
             spot, spot, right_s.at[chunk, index], right_r.at[chunk, index], (seq, tp + 1)
         )
 
     def leftward(chunk, index):
-        spot = xs.at[index, chunk_of(chunk)]
+        spot = traveller(chunk, index)
         return remote(spot, spot, left_s.at[chunk, index], left_r.at[chunk, index], (seq, tp - 1))
 
     def q_copy(chunk, step):
@@ -280,17 +287,50 @@
             for step in range(1, share):
                 kv_on(chunk, hop, step).start()
 
+    slice_rows = wo_out.shape[3]
+    half = lax.rem(part, 2)
+
+    def wo_along(step):
+        start = pl.multiple_of((head * 2 + half) * slice_rows, slice_rows)
+        return remote(
+            wo_ref.at[pl.ds(start, slice_rows)], wo_out.at[tp, head, half],
+            wz_s.at[step - 1], wz_r.at[step - 1], place.along(step)[1],
+        )
+
+    def wo_across(step):
+        spot = wo_out.at[:, head, half]
+        return remote(spot, spot, wa_s.at[step - 1], wa_r.at[step - 1], place.across(step)[1])
+
+    def wo_swap():
+        spot = wo_out.at[:, :, half]
+        return remote(spot, spot, wp_s.at[0], wp_r.at[0], (seq + 1 - 2 * half, tp))
+
     xs[tp] = x_ref[...]
+    own_rows = pl.ds(pl.multiple_of((head * 2 + half) * slice_rows, slice_rows), slice_rows)
+    early = [
+        pltpu.make_async_copy(wo_ref.at[own_rows], wo_out.at[tp, head, half], local.at[5]),
+        pltpu.make_async_copy(cot_ref.at[pl.ds(0, g_out.shape[1])], g_out.at[tp], local.at[6]),
+    ]
+    for copy in early:
+        copy.start()
     greet(
         [place.partner(step)[1] for step in range(1, share)]
         + [place.across(step)[1] for step in range(1, heads)]
         + [place.along(step)[1] for step in range(1, ntp)]
     )
+    for step in range(1, ntp):
+        wo_along(step).start()
     own_send(0)
     own_send(1)
     fill_table(place, docs_ref, pads_ref, picks_ref, table_out, nrows)
+    for copy in early:
+        copy.wait()
+    for step in range(1, ntp):
+        wo_along(step).wait_recv()
+    for step in range(1, heads):
+        wo_across(step).start()
     for chunk in range(CHUNKS):
-        if 0 < chunk < CHUNKS - 1:
+        if chunk > 0:
             own_send(chunk + 1)
         pass_on(chunk)
         compute(chunk)
@@ -300,11 +340,16 @@
             q_copy(chunk, step).start()
         if chunk > 0:
             hand_on(chunk - 1)
+        if chunk == 2:
+            for step in range(1, heads):
+                wo_across(step).wait_recv()
+            wo_swap().start()
     pairs = [
         (qbuf.at[head], q_out.at[head]),
         (kvbuf.at[head], kv_out.at[part, head]),
         (h1, h1_out),
         (xs, xs_out),
+        (cot_ref.at[pl.ds(g_out.shape[1], rest_out.shape[0])], rest_out),
     ]
     copies = [
         pltpu.make_async_copy(source, target, local.at[index])
@@ -315,6 +360,15 @@
     mine = pl.ds(pl.multiple_of(tp * (rows // ntp), rows // ntp), rows // ntp)
     xt_out[...] = xs[:, mine]
     hand_on(CHUNKS - 1)
+    for chunk in range(CHUNKS, CHUNKS + COT_CHUNKS):
+        if chunk + 1 < CHUNKS + COT_CHUNKS:
+            own_send(chunk + 1)
+        pass_on(chunk)
+    wo_swap().wait()
+    for step in range(1, ntp):
+        wo_along(step).wait_send()
+    for step in range(1, heads):
+        wo_across(step).wait_send()
     for copy in copies:
         copy.wait()
     for chunk in range(CHUNKS):
@@ -330,6 +384,7 @@
         for hop in range(heads):
             for step in range(1, share):
                 kv_on(chunk, hop, step).wait_send()
+    for chunk in range(CHUNKS + COT_CHUNKS):
         for index in range(ntp):
             @pl.when((tp >= index) & (tp < ntp - 1))
             def _():
@@ -344,12 +399,16 @@
     heads, share, nseq, ntp = dims
     rows, width = x.shape
     nblocks = picks.shape[1]
+    first = rows // CHUNKS * COT_CHUNKS
     sds = jax.ShapeDtypeStruct
     outs = [
         sds((heads, rows, WIDE), BF16),
         sds((share, heads, rows, WIDE), BF16),
         sds((rows, width * ntp), BF16),
         sds((ntp, rows, width), BF16),
+        sds((ntp, first, width), BF16),
+        sds((rows - first, width), BF16),
+        sds((ntp, heads, 2, params[-1].shape[0] // (2 * heads), params[-1].shape[1]), BF16),
         sds((ntp, rows // ntp, width), BF16),
         sds((rows, 2), F32),
         sds((16, nblocks), jnp.int32),
@@ -361,14 +420,15 @@
         vmem(heads, rows, WIDE),
     ]
     sems = (
-        [dma(CHUNKS, ntp)] * 4 + [dma(CHUNKS, heads - 1)] * 4
-        + [dma(CHUNKS, heads, share - 1)] * 2 + [dma(4)]
+        [dma(CHUNKS + COT_CHUNKS, ntp)] * 4 + [dma(CHUNKS, heads - 1)] * 4
+        + [dma(CHUNKS, heads, share - 1)] * 2 + [dma(ntp - 1)] * 2 + [dma(heads - 1)] * 2
+        + [dma(1)] * 2 + [dma(7)]
     )
     return pl.pallas_call(
         functools.partial(head_kernel, dims, nrows),
         out_shape=outs,
-        in_specs=[IN_SMEM, IN_SMEM] + [IN_VMEM] * (2 + len(params)),
-        out_specs=[ANYWHERE] * 4 + [IN_VMEM] * 3,
+        in_specs=[IN_SMEM, IN_SMEM] + [IN_VMEM] * len(params) + [ANYWHERE] * 2,
+        out_specs=[ANYWHERE] * 7 + [IN_VMEM] * 3,
         scratch_shapes=scratch + sems,
         name="head",
         compiler_params=pltpu.CompilerParams(
@@ -649,15 +709,11 @@
     return value * half, slope
 
 
-def rounds_of(tokens):
-    return max(1, min(ROUNDS, tokens // (2 * BLK)))
-
-
 def middle_kernel(
     dims,
-    o_ref, xt_ref, g_ref, wo_ref, ob_ref, gain_ref, shift_ref, wi_ref, ib_ref, wu_ref,
+    o_ref, g0_hbm, g1_hbm, wo_hbm, wi_hbm, wu_hbm, xt_ref, ob_ref, gain_ref, shift_ref, ib_ref,
     sum_out, do_out, da_out, mixed_out, vec_out, gi_out, gu_out,
-    o_in, x1, xhat, scale, h2, act, dpre, outb, terms, from_left, from_right, do_buf, ib_sum, gi, gu,
+    g_ref, wo_ref, wi_ref, wu_ref, o_in, x1, xhat, scale, h2, act, dpre, outb, terms, from_left, from_right, do_buf, ib_sum, gi, gu,
     *rest,
 ):
     place = Place(dims)
@@ -669,8 +725,9 @@
     rows, width = g_ref.shape[1:]
     features = width * ntp
     tokens = rows // ntp
-    rounds = rounds_of(tokens)
+    rounds = ROUNDS
     span = tokens // rounds
+    pieces = tokens // (2 * BLK)
     places = 2 * ntp - 1
     band = features // heads
     per = features // WIDE
@@ -690,10 +747,9 @@
 
     def do_copy(index, step):
         to_head, to_tp, device = place.apart(step)
-        count = span // 2
-        return remote(
-            do_buf.at[to_tp * heads + to_head, packed_rows(index, count)],
-            do_out.at[head, packed_rows(tp * rounds + index, count)],
+        return remote(
+            do_buf.at[to_tp * heads + to_head, packed_rows(index, BLK)],
+            do_out.at[head, packed_rows(tp * pieces + index, BLK)],
             do_s.at[index, step], do_r.at[index, step], device,
         )
 
@@ -722,42 +778,57 @@
         for k, source in enumerate((gi, gu))
     ]
 
+    first_rows = g0_hbm.shape[1]
+    loads = [
+        pltpu.make_async_copy(o_ref.at[head, packed_rows(tp)], o_in.at[tp * heads + head], local.at[2]),
+        pltpu.make_async_copy(wo_hbm, wo_ref, local.at[3]),
+        pltpu.make_async_copy(wi_hbm, wi_ref, local.at[4]),
+        pltpu.make_async_copy(wu_hbm, wu_ref, local.at[5]),
+        pltpu.make_async_copy(g0_hbm, g_ref.at[:, pl.ds(0, first_rows)], local.at[6]),
+        pltpu.make_async_copy(
+            g1_hbm, g_ref.at[:, pl.ds(first_rows, rows - first_rows)], local.at[7]
+        ),
+    ]
+    for load in loads:
+        load.start()
     greet(
         [place.partner(step)[1] for step in range(1, share)]
         + [place.apart(step)[2] for step in range(1, heads * ntp)]
     )
     for step in range(heads * ntp - 1, 0, -1):
         o_copy(step).start()
-    o_in[tp * heads + head] = o_ref[head, packed_rows(tp)]
     ib_sum[...] = jnp.zeros_like(ib_sum)
+    for load in loads:
+        load.wait()
     for step in range(1, heads * ntp):
         o_copy(step).wait_recv()
 
-    for index in range(rounds):
-        here = slice(index * span, (index + 1) * span)
-        half = slice(index * span // 2, (index + 1) * span // 2)
+    for index in range(pieces):
+        here = slice(index * 2 * BLK, (index + 1) * 2 * BLK)
+        half = slice(index * BLK, (index + 1) * BLK)
         mixed = jnp.concatenate(
             [unpack_pair(o_in[i, half], o_in[i + 1, half]) for i in range(0, heads * ntp, 2)], axis=1
         )
         mixed_out[here] = mixed
         base = jnp.concatenate([xt_ref[i, here] for i in range(ntp)], axis=1).astype(F32)
-        value = base + ob_ref[...] + jnp.dot(mixed, wo_ref[...], preferred_element_type=F32)
+        value = base + ob_ref[...] + jnp.dot(mixed, wo_ref[...].reshape(features, features), preferred_element_type=F32)
         x1[here] = value
         centered = value - jnp.sum(value, axis=1, keepdims=True) * (1.0 / features)
         spread = jnp.sum(centered * centered, axis=1, keepdims=True) * (1.0 / features)
         inverse = lax.rsqrt(spread + 1e-05)
         normed = centered * inverse
         xhat[here] = normed
-        scale[here] = jnp.broadcast_to(inverse, (span, WIDE))
+        scale[here] = jnp.broadcast_to(inverse, (2 * BLK, WIDE))
         h2[tp, here] = (normed * gain_ref[...] + shift_ref[...]).astype(BF16)
-
-        @pl.when(tp < ntp - 1)
-        def _():
-            h2_copy(index, tp, True).start()
-
-        @pl.when(tp > 0)
-        def _():
-            h2_copy(index, tp, False).start()
+        for part_index in range(index * rounds // pieces, (index + 1) * rounds // pieces):
+
+            @pl.when(tp < ntp - 1)
+            def _():
+                h2_copy(part_index, tp, True).start()
+
+            @pl.when(tp > 0)
+            def _():
+                h2_copy(part_index, tp, False).start()
 
     def spot_of(position):
         hop = (position + 1) // 2
@@ -809,23 +880,34 @@
         for i in range(ntp):
             outb[i, wide] = out[:, i * width : (i + 1) * width].astype(BF16)
 
-    def relay(index, step):
+    def relay_right(index):
         here = span_of(index)
-        owner = step
-
-        @pl.when((owner > tp) & (tp > 0))
+        for owner in range(1, ntp):
+
+            @pl.when((owner > tp) & (tp > 0))
+            def _():
+                term_copy(index, owner, True).wait_recv()
+                terms[owner, here] = add_up(terms[owner, here], from_left[owner, here]).astype(BF16)
+                term_copy(index, owner, True).start()
+
+    def relay_left(index):
+        here = span_of(index)
+        for owner in range(ntp - 2, -1, -1):
+
+            @pl.when((owner < tp) & (tp < ntp - 1))
+            def _():
+                term_copy(index, owner, False).wait_recv()
+                terms[owner, here] = add_up(terms[owner, here], from_right[owner, here]).astype(BF16)
+                term_copy(index, owner, False).start()
+
+    def relay(index, first):
+        @pl.when((tp < ntp // 2) == first)
         def _():
-            term_copy(index, owner, True).wait_recv()
-            terms[owner, here] = add_up(terms[owner, here], from_left[owner, here]).astype(BF16)
-            term_copy(index, owner, True).start()
-
-        other = ntp - 1 - step
-
-        @pl.when((other < tp) & (tp < ntp - 1))
+            relay_right(index)
+
+        @pl.when((tp < ntp // 2) != first)
         def _():
-            term_copy(index, other, False).wait_recv()
-            terms[other, here] = add_up(terms[other, here], from_right[other, here]).astype(BF16)
-            term_copy(index, other, False).start()
+            relay_left(index)
 
     def feed_step(count, carry):
         index, position = count // places, count % places
@@ -835,9 +917,13 @@
         def _():
             feed(index, owner)
 
-        @pl.when((index > 0) & (position > 0) & (position % 2 == 0))
+        @pl.when((index > 0) & (position == 2))
         def _():
-            relay(index - 1, position // 2)
+            relay(index - 1, True)
+
+        @pl.when((index > 0) & (position == places - 1))
+        def _():
+            relay(index - 1, False)
 
         return carry
 
@@ -858,9 +944,9 @@
 
     work = [functools.partial(inner_grad, index) for index in range(heads)]
     work += [functools.partial(outer_grad, index) for index in range(heads)]
-    share_out = -(-len(work) // (ntp - 1))
-    for position in range(ntp - 1):
-        relay(rounds - 1, position + 1)
+    share_out = -(-len(work) // 2)
+    for position in range(2):
+        relay(rounds - 1, position == 0)
         for item in work[position * share_out : (position + 1) * share_out]:
             item()
         if (position + 1) * share_out >= heads > position * share_out:
@@ -868,18 +954,19 @@
         if (position + 1) * share_out >= 2 * heads > position * share_out:
             scatters[1].start_near()
 
-    for index in range(rounds):
-        here = slice(index * span, (index + 1) * span)
-        half = slice(index * span // 2, (index + 1) * span // 2)
-        wide = span_of(tp * rounds + index)
-
-        @pl.when(tp > 0)
-        def _():
-            term_copy(index, tp, True).wait_recv()
-
-        @pl.when(tp < ntp - 1)
-        def _():
-            term_copy(index, tp, False).wait_recv()
+    for index in range(pieces):
+        here = slice(index * 2 * BLK, (index + 1) * 2 * BLK)
+        half = slice(index * BLK, (index + 1) * BLK)
+        wide = pl.ds(pl.multiple_of(tp * tokens + index * 2 * BLK, 2 * BLK), 2 * BLK)
+        for part_index in range(index * rounds // pieces, (index + 1) * rounds // pieces):
+
+            @pl.when(tp > 0)
+            def _():
+                term_copy(part_index, tp, True).wait_recv()
+
+            @pl.when(tp < ntp - 1)
+            def _():
+                term_copy(part_index, tp, False).wait_recv()
 
         grad = terms[tp, here].astype(F32)
         grad = grad + jnp.where(tp > 0, from_left[tp, here].astype(F32), 0.0)
@@ -892,7 +979,9 @@
         cot = jnp.concatenate([g_ref[i, wide] for i in range(ntp)], axis=1).astype(F32)
         branch = (cot + tail).astype(BF16)
         da_out[here] = branch
-        do = lax.dot_general(branch, wo_ref[...], NT, preferred_element_type=F32)
+        do = lax.dot_general(
+            branch, wo_ref[...].reshape(features, features), NT, preferred_element_type=F32
+        )
         for i in range(0, heads * ntp, 2):
             pair = pack_pair(do[:, i * HEAD_DIM : (i + 2) * HEAD_DIM])
             do_buf[i, half] = pair[0]
@@ -932,11 +1021,11 @@
     save.wait()
     own.wait()
     for step in range(1, heads * ntp):
-        for index in range(rounds):
+        for index in range(pieces):
             do_copy(index, step).wait_recv()
     for step in range(1, heads * ntp):
         o_copy(step).wait_send()
-        for index in range(rounds):
+        for index in range(pieces):
             do_copy(index, step).wait_send()
     for index in range(rounds):
         for owner in range(ntp):
@@ -960,13 +1049,13 @@
         scatter.finish()
 
 
-def run_middle(dims, o, xt, g, wo, ob, gain, shift, wi, ib, wu):
+def run_middle(dims, o, g0, g1, wo, wi, wu, xt, ob, gain, shift, ib):
     heads, share, nseq, ntp = dims
-    _, rows, width = g.shape
+    rows, width = g0.shape[1] + g1.shape[1], g0.shape[2]
     features, hidden = width * ntp, wi.shape[1]
     tokens, band = rows // ntp, features // nseq
     per = features // WIDE
-    rounds = rounds_of(tokens)
+    rounds, pieces = ROUNDS, tokens // (2 * BLK)
     sds = jax.ShapeDtypeStruct
     outs = [
         sds((ntp, rows, width), BF16),
@@ -979,6 +1068,10 @@
     ]
     count = heads * ntp
     scratch = [
+        vmem(ntp, rows, width),
+        vmem(*wo.shape),
+        vmem(*wi.shape),
+        vmem(*wu.shape),
         vmem(count, tokens // 2, WIDE),
         vmem(tokens, features, dtype=F32),
         vmem(tokens, features, dtype=F32),
@@ -998,28 +1091,27 @@
         *GradScatter.buffers(dims, band, hidden),
     ]
     sems = (
-        [dma(count)] * 2 + [dma(rounds, ntp)] * 8 + [dma(rounds, count)] * 2
-        + GradScatter.semaphores(dims, 2) + [dma(2)]
+        [dma(count)] * 2 + [dma(rounds, ntp)] * 8 + [dma(pieces, count)] * 2
+        + GradScatter.semaphores(dims, 2) + [dma(8)]
     )
     return pl.pallas_call(
         functools.partial(middle_kernel, dims),
         out_shape=outs,
-        in_specs=[IN_VMEM] * 10,
+        in_specs=[ANYWHERE] * 6 + [IN_VMEM] * 5,
         out_specs=[ANYWHERE] * 2 + [IN_VMEM] * 5,
         scratch_shapes=scratch + sems,
         name="middle",
         compiler_params=pltpu.CompilerParams(
             collective_id=2, has_side_effects=True, vmem_limit_bytes=63 << 20
         ),
-    )(o, xt, g, wo, ob, gain, shift, wi, ib, wu)
+    )(o, g0, g1, wo, wi, wu, xt, ob, gain, shift, ib)
 
 
 def tail_kernel(
     dims,
-    dq_ref, dkv_ref, h1_ref, x_ref, stat_ref, gain_ref, wq_ref, wk_ref, wv_ref,
-    da_ref, mixed_ref, vec_ref,
-    gx_ref, ow_ref, oq_ref, vout_ref,
-    dq_in, dkv_in, dkv_land, dkv_sum, all3, da_in, pbuf, from_left, from_right,
+    dq_ref, dkv_hbm, h1_hbm, x_hbm, da_ref, mixed_ref, stat_ref, gain_ref, wq_ref, wk_ref, wv_ref, vec_ref,
+    gx_ref, ow_ref, oq_ref, ok_ref, ov_ref, vout_ref,
+    dkv_own, h1_ref, x_ref, dq_in, dkv_in, dkv_land, dkv_sum, all3, da_in, pbuf, from_left, from_right,
     sums, sums_land, vbuf, vec_land, vsum, vec_far, gw, g3, wbuf, wfar,
     *rest,
 ):
@@ -1028,7 +1120,7 @@
     head, part, seq, tp = place.head, place.part, place.seq, place.tp
     lands, sems = rest[:6], rest[6:]
     (dq_s, dq_r, kv1_s, kv1_r, kv2_s, kv2_r, right_s, right_r, left_s, left_r,
-     da_s, da_r, st_s, st_r, v1_s, v1_r, v2_s, v2_r, w_s, w_r, g1_s, g1_r, g2_s, g2_r) = sems
+     da_s, da_r, st_s, st_r, v1_s, v1_r, v2_s, v2_r, w_s, w_r, g1_s, g1_r, g2_s, g2_r, load_s) = sems
     rows, features = h1_ref.shape
     width = features // ntp
     tokens = rows // ntp
@@ -1053,10 +1145,12 @@
             dq_s.at[chunk, step - 1], dq_r.at[chunk, step - 1], device,
         )
 
-    def dkv_near(step):
+    def dkv_near(chunk, step):
         other, device = place.partner(step)
-        return remote(
-            dkv_ref.at[other], dkv_land.at[step - 1], kv1_s.at[step - 1], kv1_r.at[step - 1], device
+        here = chunk_of(chunk)
+        return remote(
+            dkv_hbm.at[other, :, here], dkv_land.at[step - 1, :, here],
+            kv1_s.at[chunk, step - 1], kv1_r.at[chunk, step - 1], device,
         )
 
     def dkv_copy(chunk, step):
@@ -1111,39 +1205,50 @@
         for k, source in enumerate((gw, g3))
     ]
 
+    loads = [
+        pltpu.make_async_copy(dkv_hbm.at[part], dkv_own, load_s.at[0]),
+        pltpu.make_async_copy(dq_ref.at[head], dq_in.at[head], load_s.at[1]),
+        pltpu.make_async_copy(x_hbm, x_ref, load_s.at[2]),
+        pltpu.make_async_copy(h1_hbm, h1_ref, load_s.at[3]),
+    ]
+    for load in loads:
+        load.start()
     greet(
         [(lax.rem(seq + step, nseq), tp) for step in range(1, nseq)]
         + [place.along(step)[1] for step in range(1, ntp)]
     )
-    for step in range(1, share):
-        dkv_near(step).start()
     for chunk in range(CHUNKS):
-        for step in range(1, heads):
-            dq_copy(chunk, step).start()
-    dq_in[head] = dq_ref[head]
-    for index in range(heads):
-        value = lax.dot_general(
-            da_ref[:, index * band : (index + 1) * band], mixed_ref[...], TN, preferred_element_type=F32
-        )
-        gw[index] = value.astype(BF16).reshape(gw.shape[1:])
-    for step in range(1, share):
-        dkv_near(step).wait_recv()
-    scatters[0].start_near()
-    for chunk in range(CHUNKS):
-        for target in range(heads):
-            where = (target, chunk_of(chunk))
-            parts = [dkv_ref[(part,) + where]]
-            parts += [dkv_land[(step,) + where] for step in range(share - 1)]
-            dkv_sum[where] = add_up(*parts).astype(BF16)
-        for step in range(1, heads):
-            dkv_copy(chunk, step).start()
-    dkv_in[head] = dkv_sum[head]
+        for step in range(1, share):
+            dkv_near(chunk, step).start()
+    for step in range(1, ntp):
+        da_copy(step).start()
+    da_in[tp] = da_ref[:, columns_of(tp)]
     vbuf[: 2 * per] = jnp.zeros((2 * per, WIDE), F32)
     vbuf[2 * per : 6 * per] = vec_ref[: 4 * per]
     narrow = 3 * local_width // WIDE
     vbuf[6 * per : 6 * per + narrow] = jnp.zeros((narrow, WIDE), F32)
     vbuf[6 * per + narrow :] = vec_ref[4 * per :]
-    scatters[0].start_across()
+    loads[0].wait()
+    for chunk in range(CHUNKS):
+        for step in range(1, heads):
+            dq_copy(chunk, step).start()
+        for step in range(1, share):
+            dkv_near(chunk, step).wait_recv()
+        for target in range(heads):
+            where = (target, chunk_of(chunk))
+            parts = [dkv_own[where]] + [dkv_land[(step,) + where] for step in range(share - 1)]
+            dkv_sum[where] = add_up(*parts).astype(BF16)
+        for step in range(1, heads):
+            dkv_copy(chunk, step).start()
+    dkv_in[head] = dkv_sum[head]
+    for load in loads[1:]:
+        load.wait()
+
+    def output_grad(index):
+        value = lax.dot_general(
+            da_ref[:, index * band : (index + 1) * band], mixed_ref[...], TN, preferred_element_type=F32
+        )
+        gw[index] = value.astype(BF16).reshape(gw.shape[1:])
 
     gain = gain_ref[...]
     lane = lax.broadcasted_iota(jnp.int32, (chunk_rows, WIDE), 1)
@@ -1191,39 +1296,47 @@
         both = jnp.where(lane == 0, sum0, jnp.where(lane == 1, sum1, 0.0))
         sums[:, here] = both.T[:8]
 
-    def pass_on(chunk):
+    def set_off(chunk):
         for step in range(ntp - 1):
             far = ntp - 1 - step
 
-            @pl.when(tp < far)
-            def _():
-                @pl.when(tp > 0)
-                def _():
-                    rightward(chunk, far).wait_recv()
-                    pbuf[chunk, far] = add_up(pbuf[chunk, far], from_left[chunk, far]).astype(BF16)
-
+            @pl.when(tp == 0)
+            def _():
                 rightward(chunk, far).start()
 
-            @pl.when(tp > step)
-            def _():
-                @pl.when(tp < ntp - 1)
-                def _():
-                    leftward(chunk, step).wait_recv()
-                    pbuf[chunk, step] = add_up(pbuf[chunk, step], from_right[chunk, step]).astype(BF16)
-
+            @pl.when(tp == ntp - 1)
+            def _():
                 leftward(chunk, step).start()
 
-    for chunk in range(CHUNKS):
-        partial_step(chunk)
-        if chunk > 0:
-            pass_on(chunk - 1)
-    for step in range(1, ntp):
-        sums_copy(step).start()
-    for step in range(1, nseq):
-        vec_copy(step).start()
-    for step in range(1, ntp):
-        da_copy(step).start()
-    da_in[tp] = da_ref[:, columns_of(tp)]
+    def relay_right(chunk):
+        for step in range(ntp - 1):
+            far = ntp - 1 - step
+
+            @pl.when((tp < far) & (tp > 0))
+            def _():
+                rightward(chunk, far).wait_recv()
+                pbuf[chunk, far] = add_up(pbuf[chunk, far], from_left[chunk, far]).astype(BF16)
+                rightward(chunk, far).start()
+
+    def relay_left(chunk):
+        for step in range(ntp - 1):
+
+            @pl.when((tp > step) & (tp < ntp - 1))
+            def _():
+                leftward(chunk, step).wait_recv()
+                pbuf[chunk, step] = add_up(pbuf[chunk, step], from_right[chunk, step]).astype(BF16)
+                leftward(chunk, step).start()
+
+    def relay(chunk):
+        @pl.when(tp < ntp // 2)
+        def _():
+            relay_right(chunk)
+            relay_left(chunk)
+
+        @pl.when(tp >= ntp // 2)
+        def _():
+            relay_left(chunk)
+            relay_right(chunk)
 
     def grad_step(index, carry):
         left = h1_ref[:, pl.ds(pl.multiple_of(index * band, band), band)]
@@ -1231,9 +1344,24 @@
         g3[index] = value.astype(BF16).reshape(g3.shape[1:])
         return carry
 
+    for chunk in range(CHUNKS):
+        partial_step(chunk)
+        set_off(chunk)
+        if chunk == 0:
+            for index in range(heads):
+                output_grad(index)
+            scatters[0].start_near()
+        if chunk > 1:
+            relay(chunk - 2)
+    for step in range(1, ntp):
+        sums_copy(step).start()
+    for step in range(1, nseq):
+        vec_copy(step).start()
+    scatters[0].start_across()
     lax.fori_loop(0, heads, grad_step, 0)
     scatters[1].start_near()
-    pass_on(CHUNKS - 1)
+    relay(CHUNKS - 2)
+    scatters[1].start_across()
     for step in range(1, nseq):
         vec_copy(step).wait_recv()
     total = vbuf[...]
@@ -1242,12 +1370,12 @@
     vsum[...] = total
     for step in range(1, ntp):
         vec_far_copy(step).start()
-    scatters[1].start_across()
     value = scatters[0].result().astype(BF16)
     for index in range(ntp):
         wbuf[index] = value[:, index * local_width : (index + 1) * local_width]
     for step in range(1, ntp):
         w_copy(step).start()
+    relay(CHUNKS - 1)
 
     for step in range(1, ntp):
         sums_copy(step).wait_recv()
@@ -1279,7 +1407,10 @@
         many = chunk_rows // da_rows
         branch = da_in[chunk * many : (chunk + 1) * many].reshape(chunk_rows, width)
         gx_ref[here] = branch.astype(F32) + scale * inner
-    oq_ref[...] = scatters[1].result()
+    value = scatters[1].result()
+    oq_ref[...] = 0.125 * value[:, :local_width]
+    ok_ref[...] = value[:, local_width : 2 * local_width]
+    ov_ref[...] = value[:, 2 * local_width :]
     for step in range(1, ntp):
         vec_far_copy(step).wait_recv()
         w_copy(step).wait_recv()
@@ -1288,9 +1419,9 @@
         vout_ref[: 6 * per] += vec_far[step, : 6 * per]
     ow_ref[...] = add_up(wbuf[tp], *[wfar[step] for step in range(ntp - 1)])
 
-    for step in range(1, share):
-        dkv_near(step).wait_send()
     for chunk in range(CHUNKS):
+        for step in range(1, share):
+            dkv_near(chunk, step).wait_send()
         for step in range(1, heads):
             dq_copy(chunk, step).wait_send()
             dkv_copy(chunk, step).wait_send()
@@ -1314,7 +1445,7 @@
         scatter.finish()
 
 
-def run_tail(dims, dq, dkv, h1, x_parts, stats, gain, wq, wk, wv, da, mixed, vec):
+def run_tail(dims, dq, dkv, h1, x_parts, da, mixed, stats, gain, wq, wk, wv, vec):
     heads, share, nseq, ntp = dims
     rows, features = h1.shape
     width, tokens = features // ntp, rows // ntp
@@ -1326,11 +1457,16 @@
     outs = [
         sds((rows, width), F32),
         sds((band, local_width), F32),
-        sds((band, 3 * local_width), F32),
+        sds((band, local_width), F32),
+        sds((band, local_width), F32),
+        sds((band, local_width), F32),
         sds((nvec, WIDE), F32),
     ]
     pieces = (CHUNKS, ntp, rows // CHUNKS, width)
     scratch = [
+        vmem(heads, rows, WIDE),
+        vmem(rows, features),
+        vmem(ntp, rows, width),
         vmem(heads, rows // 2, WIDE),
         vmem(heads, rows, WIDE),
         vmem(max(share - 1, 1), heads, rows, WIDE),
@@ -1354,21 +1490,21 @@
         *GradScatter.buffers(dims, band, 3 * local_width),
     ]
     sems = (
-        [dma(CHUNKS, heads - 1)] * 2 + [dma(share - 1)] * 2 + [dma(CHUNKS, heads - 1)] * 2
+        [dma(CHUNKS, heads - 1)] * 2 + [dma(CHUNKS, share - 1)] * 2 + [dma(CHUNKS, heads - 1)] * 2
         + [dma(CHUNKS, ntp)] * 4 + [dma(ntp - 1)] * 4 + [dma(nseq - 1)] * 2 + [dma(ntp - 1)] * 4
-        + GradScatter.semaphores(dims, 2)
+        + GradScatter.semaphores(dims, 2) + [dma(4)]
     )
     return pl.pallas_call(
         functools.partial(tail_kernel, dims),
         out_shape=outs,
-        in_specs=[IN_VMEM] * 12,
+        in_specs=[ANYWHERE] * 4 + [IN_VMEM] * 8,
         out_specs=[IN_VMEM] * len(outs),
         scratch_shapes=scratch + sems,
         name="tail",
         compiler_params=pltpu.CompilerParams(
             collective_id=3, has_side_effects=True, vmem_limit_bytes=60 << 20
         ),
-    )(dq, dkv, h1, x_parts, stats, gain, wq, wk, wv, da, mixed, vec)
+    )(dq, dkv, h1, x_parts, da, mixed, stats, gain, wq, wk, wv, vec)
 
 
 def on_device(
@@ -1403,13 +1539,13 @@
     dims = (heads, share, nseq, ntp)
     features = width * ntp
     per = features // WIDE
-    g_parts = lax.all_gather(cotangent.reshape(rows, width), "tp", axis=0)
-    output_full = lax.all_gather(output_weight, "tp", axis=0, tiled=True)
-    q, kv, h1, x_parts, x_mine, stats, table = run_head(
+    cot = cotangent.reshape(rows, width)
+    q, kv, h1, x_parts, g_first, rest, output_full, x_mine, stats, table = run_head(
         dims, nrows, doc_blocks, doc_padding, random_picks.T, hidden_in.reshape(rows, width),
         norm_gain[None, :], norm_shift[None, :], query_weight, query_bias[None, :],
-        key_weight, value_weight, value_bias[None, :],
+        key_weight, value_weight, value_bias[None, :], cot, output_weight,
     )
+    g_rest = lax.all_gather(rest, "tp", axis=0)
     q = q.reshape(heads * rows, WIDE)
     kv = kv.reshape(nseq * rows, WIDE)
     sds = jax.ShapeDtypeStruct
@@ -1420,9 +1556,9 @@
         2,
     )(table, q, kv)
     out_sum, do, da, mixed, vec, inner_part, outer_part = run_middle(
-        dims, packed.reshape(heads, rows // 2, WIDE), x_mine, g_parts, output_full,
-        output_bias[None, :], feed_gain[None, :], feed_shift[None, :],
-        inner_weight, inner_bias[None, :], outer_weight,
+        dims, packed.reshape(heads, rows // 2, WIDE), g_first, g_rest, output_full,
+        inner_weight, outer_weight, x_mine, output_bias[None, :], feed_gain[None, :],
+        feed_shift[None, :], inner_bias[None, :],
     )
     result = lax.psum_scatter(out_sum, "tp", scatter_dimension=0)
     dq, dkv = local_call(
@@ -1432,9 +1568,9 @@
         4,
         [pltpu.VMEM((nseq * rows, WIDE), F32)],
     )(table, q, do.reshape(heads * rows // 2, WIDE), res, kv)
-    grad_x, output_part, qkv_part, vectors = run_tail(
+    grad_x, output_part, query_part, key_part, value_part, vectors = run_tail(
         dims, dq.reshape(heads, rows // 2, WIDE), dkv.reshape(share, heads, rows, WIDE), h1, x_parts,
-        stats, norm_gain[None, :], query_weight, key_weight, value_weight, da, mixed, vec,
+        da, mixed, stats, norm_gain[None, :], query_weight, key_weight, value_weight, vec,
     )
     my_bias = lax.dynamic_slice_in_dim(outer_bias, tp * width, width, 0)
     layer_out = (result.astype(F32) + my_bias).astype(BF16).reshape(hidden_in.shape)
@@ -1445,10 +1581,10 @@
         grad_x.reshape(hidden_in.shape),
         wide[0],
         wide[1],
-        0.125 * qkv_part[:, :local_width],
+        query_part,
         0.125 * narrow[:local_width],
-        qkv_part[:, local_width : 2 * local_width],
-        qkv_part[:, 2 * local_width :],
+        key_part,
+        value_part,
         narrow[2 * local_width : 3 * local_width],
         output_part.T,
         wide[2],

time: 391 us -> 345 us (0.88); the launches traced: 390 us -> 340 us
  Pallas kernels: 363 us -> 300 us
  waiting for transfers between devices: 1.4 us -> 14.3 us
    pallas_call x1, Pallas kernels: 94.6 us -> 65.5 us  [run_tail(): pl.pallas_call(functools.partial(tail_kernel, dims), out_shape=outs, in_s...]
    pallas_call x1, Pallas kernels: 79.9 us -> 59.4 us  [run_head(): pl.pallas_call(functools.partial(head_kernel, dims, nrows), out_shape=out...]
    pallas_call x1, Pallas kernels: 127 us -> 111 us  [run_middle(): pl.pallas_call(functools.partial(middle_kernel, dims), out_shape=outs, in...]
    all_gather x2 -> x1, waiting for transfers between devices: 0.01 us -> 14.2 us  [on_device(): g_rest = lax.all_gather(rest, 'tp', axis=0)]
  transfers between devices with their start and end apart: 3 -> 2, of which waited for: 0 -> 1; matrix products, arithmetic and copies ran while one was open for 2% -> 2% of each run, Pallas kernels for 61% -> 38%
where the time goes in v4:
time: 345 us; the launch traced here: 340 us
  Pallas kernels  300 us (87%)
  waiting for transfers between devices  14.3 us (4%)
  between operations  14.1 us (4%)
  local copies, waits for them, and re-layouts  8.6 us (2%)
    pallas_call x1, Pallas kernels, run_middle(): pl.pallas_call(functools.partial(middle_kernel, dims), out_shape=outs, in...  111 us
    pallas_call x1, Pallas kernels, run_tail(): pl.pallas_call(functools.partial(tail_kernel, dims), out_shape=outs, in_s...  65.5 us
    pallas_call x1, Pallas kernels, run_head(): pl.pallas_call(functools.partial(head_kernel, dims, nrows), out_shape=out...  59.4 us
    pallas_call x1, Pallas kernels, on_device(): local_call(functools.partial(backward_kernel, dims, nrows, 1), 'attention...  33.7 us
    pallas_call x1, Pallas kernels, on_device(): local_call(functools.partial(forward_kernel, dims, nrows, 1), 'attention_...  30.2 us
    all_gather x1, waiting for transfers between devices, on_device(): g_rest = lax.all_gather(rest, 'tp', axis=0)  14.2 us
  transfers between devices with their start and end apart: 2, of which 1 were waited for; matrix products, arithmetic and copies ran while one was open for 2% of the time, Pallas kernels for 38%

profile of v4, /device:TPU:8, one launch (start us, length us, event | category | flops | bytes accessed | tf_op | source)
XLA Modules:
  0.0 340.2 jit_solution(8856731378583660617)
XLA Ops:
  7.2 0.0 all-gather.3.cloned.1.call-start
  7.2 59.4 %head.1 = (bf16[4,1024,128]{2,1,0:T(8,128)(2,1)}, bf16[2,4,1024,128]{3,2,1,0:T(8,128)(2,1)}, bf16[1024,1024]{1,0:T(8,128)(2,1)}, bf16[4,1024,256]{2,1,0:T(8,128)...) custom-call(s32[32]{0:T(128)} %docs_ref.1, ...), custom_call_target="tpu_custom_call" | custom-call | tf_op jit(solution)/shard_map/head/pallas_call | solution.py:427
  66.7 0.0 all-gather.3.cloned.1.call-update
  66.7 0.0 reduce-scatter.2.cloned.1.call-start
  66.8 30.2 %attention_forward.1 = (bf16[2048,128]{1,0:T(8,128)(2,1)}, f32[4096,128]{1,0:T(8,128)}) custom-call(s32[16,128]{1,0:T(8,128)} %get-tuple-element.44.table_ref, bf16[4096,128]{1,0:T(8,128)(2,1)} %bitcast.63, bf16[8192,128]{1,0:T(8,128)(2,1)} %bitcast.61), custom_call_target="tpu_custom_call" | custom-call | flops 32212254720 | bytes 8388608 | tf_op jit(solution)/shard_map/attention_forward/pallas_call | solution.py:1552
  97.0 14.2 %all-gather.3.cloned.1.call-done = bf16[3072,256]{1,0:T(8,128)(2,1)} async-done(((bf16[768,256]{1,0:T(8,128)(2,1)}), bf16[3072,256]{1,0:T(8,128)(2,1)}) %all-gather.3.cloned.1.call-update) | async-done | bytes 1572880 | tf_op jit(solution)/shard_map/all_gather | solution.py:1548
  111.2 111.0 %middle.1 = (bf16[4,1024,256]{2,1,0:T(8,128)(2,1)}, bf16[4,512,128]{2,1,0:T(8,128)(2,1)}, bf16[256,1024]{1,0:T(8,128)(2,1)}, bf16[256,1024]{1,0:T(8,128)(2,1)}, ...) custom-call(bf16[4,512,128]{2,1,0:T(8,128)(2,1)} %bitcast.45, ...), custom_call_target="tpu_custom_call" | custom-call | tf_op jit(solution)/shard_map/middle/pallas_call | solution.py:1097
  222.2 0.0 reduce-scatter.2.cloned.1.call-update
  222.2 0.8 dynamic_slice.3
  223.0 33.7 %attention_backward.1 = (bf16[2048,128]{1,0:T(8,128)(2,1)}, bf16[8192,128]{1,0:T(8,128)(2,1)}) custom-call(s32[16,128]{1,0:T(8,128)} %get-tuple-element.44.table_ref, bf16[4096,128]{1,0:T(8,128)(2,1)} %bitcast.64, bf16[2048,128]{1,0:T(8,128)(2,1)} %bitcast.65, f32[4096,128]{1,0:T(8,128)} %get-tuple-element.54.res_ref, bf16[8192,128]{1,0:T(8,128)(2,1)} %bitcast.62), custom_call_target="tpu_custom_call" | custom-call | flops 32212254720 | bytes 8388608 | tf_op jit(solution)/shard_map/attention_backward/pallas_call | solution.py:1564
  256.7 65.5 %tail.1 = (f32[1024,256]{1,0:T(8,128)}, f32[128,256]{1,0:T(8,128)}, f32[128,256]{1,0:T(8,128)}, f32[128,256]{1,0:T(8,128)}, f32[128,256]{1,0:T(8,128)}, /*index=5*/f32[62,128]{1,0:T(8,128)}) custom-call(bf16[4,512,128]{2,1,0:T(8,128)(2,1)} %bitcast.44, bf16[2,4,1024,128]{3,2,1,0:T(8,128)(2,1)} %bitcast.41, bf16[1024,1024]{1,0:T(8,128)(2,1)} %get-tuple-element.57.h1_hbm, ...), custom_call_target="tpu_custom_call" | custom-call | tf_op jit(solution)/shard_map/tail/pallas_call | solution.py:1497
  322.2 1.7 copy.37
  324.0 1.0 copy.38
  325.0 1.3 slice_bitcast_fusion.7
  326.3 1.3 slice_bitcast_fusion
  327.7 0.0 reduce-scatter.2.cloned.1.call-done
  327.7 1.9 fusion
  329.6 0.0 copy-done
  329.6 1.0 copy.44
  330.6 0.0 copy-done.5
  330.6 0.7 copy.45
  331.2 0.7 copy.46
  331.9 0.7 copy.47
  332.6 0.8 copy.48
  (10 shorter events, 0.0 us)
Async XLA Ops:
  7.2 104.0 %all-gather.3.cloned.1.call-start = ((), (), s32[]{:S(2)}) async-start(), calls=%async_computation.2 | async-start | bytes 1966080 | tf_op jit(solution)/shard_map/all_gather | solution.py:1548
  66.7 260.9 %reduce-scatter.2.cloned.1.call-start = ((), (), s32[]{:S(2)}) async-start(), calls=%async_computation.1 | async-start | bytes 2621440 | tf_op jit(solution)/shard_map/reduce_scatter | solution.py:1563
  256.7 67.3 %copy-start.2 = (f32[128,1024]{1,0:T(8,128)S(1)}, f32[128,1024]{1,0:T(8,128)}, u32[]{:S(2)}) copy-start(f32[128,1024]{1,0:T(8,128)} %get-tuple-element.70) | copy-start | bytes 1572868
  322.2 7.4 %copy-start = (f32[1024,256]{1,0:T(8,128)S(1)}, f32[1024,256]{1,0:T(8,128)}, u32[]{:S(2)}) copy-start(f32[1024,256]{1,0:T(8,128)} %get-tuple-element.63) | copy-start | bytes 3145732
  324.0 6.6 %copy-start.5 = (f32[128,256]{1,0:T(8,128)S(1)}, f32[128,256]{1,0:T(8,128)}, u32[]{:S(2)}) copy-start(f32[128,256]{1,0:T(8,128)} %get-tuple-element.118) | copy-start | bytes 393220
  324.0 7.3 %copy-start.4 = (f32[128,256]{1,0:T(8,128)S(1)}, f32[128,256]{1,0:T(8,128)}, u32[]{:S(2)}) copy-start(f32[128,256]{1,0:T(8,128)} %get-tuple-element.120) | copy-start | bytes 393220
  325.0 6.9 %copy-start.3 = (f32[128,256]{1,0:T(8,128)S(1)}, f32[128,256]{1,0:T(8,128)}, u32[]{:S(2)}) copy-start(f32[128,256]{1,0:T(8,128)} %get-tuple-element.121) | copy-start | bytes 393220
  325.0 7.6 %copy-start.1 = (f32[128,1024]{1,0:T(8,128)S(1)}, f32[128,1024]{1,0:T(8,128)}, u32[]{:S(2)}) copy-start(f32[128,1024]{1,0:T(8,128)} %get-tuple-element.127) | copy-start | bytes 1572868
Sparse Core Ops, SparseCore 0:
  66.8 44.3 all-gather.2
  222.4 44.0 reduce-scatter.1

commit v5 on v4

--- a/solution.py
+++ b/solution.py
@@ -431,6 +431,7 @@
         out_specs=[ANYWHERE] * 7 + [IN_VMEM] * 3,
         scratch_shapes=scratch + sems,
         name="head",
+        cost_estimate=pl.CostEstimate(flops=60 << 30, bytes_accessed=8 << 20, transcendentals=0),
         compiler_params=pltpu.CompilerParams(
             collective_id=1, has_side_effects=True, vmem_limit_bytes=60 << 20
         ),
@@ -672,7 +673,7 @@
         for step in range(1, self.place.share):
             self.near(step).start()
 
-    def start_across(self):
+    def sum_near(self):
         place = self.place
         for step in range(1, place.share):
             self.near(step).wait_recv()
@@ -684,7 +685,10 @@
             return carry
 
         lax.fori_loop(0, place.heads, body, 0)
-        for step in range(1, place.heads):
+
+    def start_across(self):
+        self.sum_near()
+        for step in range(1, self.place.heads):
             self.across(step).start()
 
     def result(self):
@@ -693,9 +697,12 @@
             self.across(step).wait_recv()
         return add_up(self.pair[self.place.head], *[self.far[step] for step in range(heads - 1)])
 
-    def finish(self):
+    def finish_near(self):
         for step in range(1, self.place.share):
             self.near(step).wait_send()
+
+    def finish(self):
+        self.finish_near()
         for step in range(1, self.place.heads):
             self.across(step).wait_send()
 
@@ -713,13 +720,13 @@
     dims,
     o_ref, g0_hbm, g1_hbm, wo_hbm, wi_hbm, wu_hbm, xt_ref, ob_ref, gain_ref, shift_ref, ib_ref,
     sum_out, do_out, da_out, mixed_out, vec_out, gi_out, gu_out,
-    g_ref, wo_ref, wi_ref, wu_ref, o_in, x1, xhat, scale, h2, act, dpre, outb, terms, from_left, from_right, do_buf, ib_sum, gi, gu,
+    g_ref, wo_ref, wi_ref, wu_ref, o_in, x1, xhat, scale, h2, act, dpre, outb, terms, from_left, from_right, do_buf, ib_sum, gi, gu, land_i, land_u, pair_i, pair_u, far_i, far_u,
     *rest,
 ):
     place = Place(dims)
     heads, share, nseq, ntp = dims
     head, part, seq, tp = place.head, place.part, place.seq, place.tp
-    lands, sems = rest[:6], rest[6:]
+    sems = rest
     (o_s, o_r, hr_s, hr_r, hl_s, hl_r, tr_s, tr_r, tl_s, tl_r, do_s, do_r,
      g1_s, g1_r, g2_s, g2_r, local) = sems
     rows, width = g_ref.shape[1:]
@@ -772,10 +779,10 @@
         )
 
     scatters = [
-        GradScatter(
-            place, source, lands[3 * k : 3 * k + 3], (g1_s.at[k], g1_r.at[k], g2_s.at[k], g2_r.at[k])
-        )
-        for k, source in enumerate((gi, gu))
+        GradScatter(place, source, bufs, (g1_s.at[k], g1_r.at[k], g2_s.at[k], g2_r.at[k]))
+        for k, (source, bufs) in enumerate(
+            ((gi, (land_i, pair_i, far_i)), (gu, (land_u, pair_u, far_u)))
+        )
     ]
 
     first_rows = g0_hbm.shape[1]
@@ -944,17 +951,7 @@
 
     work = [functools.partial(inner_grad, index) for index in range(heads)]
     work += [functools.partial(outer_grad, index) for index in range(heads)]
-    share_out = -(-len(work) // 2)
-    for position in range(2):
-        relay(rounds - 1, position == 0)
-        for item in work[position * share_out : (position + 1) * share_out]:
-            item()
-        if (position + 1) * share_out >= heads > position * share_out:
-            scatters[0].start_near()
-        if (position + 1) * share_out >= 2 * heads > position * share_out:
-            scatters[1].start_near()
-
-    for index in range(pieces):
+    def finish(index):
         here = slice(index * 2 * BLK, (index + 1) * 2 * BLK)
         half = slice(index * BLK, (index + 1) * BLK)
         wide = pl.ds(pl.multiple_of(tp * tokens + index * 2 * BLK, 2 * BLK), 2 * BLK)
@@ -1001,12 +998,25 @@
                     vec_out[row, :] = piece
                 else:
                     vec_out[row, :] += piece
+    early = pieces * (rounds - 1) // rounds
+    for item in work[:heads]:
+        item()
+    scatters[0].start_near()
+    for index in range(early):
+        finish(index)
+    relay(rounds - 1, True)
+    scatters[0].start_across()
+    for item in work[heads:]:
+        item()
+    scatters[1].start_near()
+    relay(rounds - 1, False)
+    for index in range(early, pieces):
+        finish(index)
     own = pltpu.make_async_copy(
         do_buf.at[tp * heads + head], do_out.at[head, packed_rows(tp)], local.at[1]
     )
     own.start()
-    for scatter in scatters:
-        scatter.start_across()
+    scatters[1].start_across()
     cot = jnp.sum(g_ref[tp].astype(F32), axis=0, keepdims=True)
     for sub in range(per):
         owner, lane = divmod(sub * WIDE, width)
@@ -1017,7 +1027,7 @@
         row = 4 * per + sub
         vec_out[row : row + 1, :] = ib_sum[0:1, sub * WIDE : (sub + 1) * WIDE]
     gi_out[...] = scatters[0].result()
-    gu_out[...] = scatters[1].result()
+    gu_out[...] = scatters[1].result().T
     save.wait()
     own.wait()
     for step in range(1, heads * ntp):
@@ -1064,7 +1074,7 @@
         sds((tokens, features), BF16),
         sds((4 * per + hidden // WIDE, WIDE), F32),
         sds((band, hidden), F32),
-        sds((band, hidden), F32),
+        sds((hidden, band), F32),
     ]
     count = heads * ntp
     scratch = [
@@ -1087,8 +1097,12 @@
         vmem(8, hidden, dtype=F32),
         vmem(heads, share, band, hidden),
         vmem(heads, share, band, hidden),
-        *GradScatter.buffers(dims, band, hidden),
-        *GradScatter.buffers(dims, band, hidden),
+        vmem(max(share - 1, 1), heads, band, hidden),
+        vmem(max(share - 1, 1), heads, band, hidden),
+        vmem(heads, band, hidden),
+        vmem(heads, band, hidden),
+        vmem(max(heads - 1, 1), band, hidden),
+        vmem(max(heads - 1, 1), band, hidden),
     ]
     sems = (
         [dma(count)] * 2 + [dma(rounds, ntp)] * 8 + [dma(pieces, count)] * 2
@@ -1101,6 +1115,7 @@
         out_specs=[ANYWHERE] * 2 + [IN_VMEM] * 5,
         scratch_shapes=scratch + sems,
         name="middle",
+        cost_estimate=pl.CostEstimate(flops=110 << 30, bytes_accessed=8 << 20, transcendentals=0),
         compiler_params=pltpu.CompilerParams(
             collective_id=2, has_side_effects=True, vmem_limit_bytes=63 << 20
         ),
@@ -1338,30 +1353,31 @@
             relay_left(chunk)
             relay_right(chunk)
 
-    def grad_step(index, carry):
-        left = h1_ref[:, pl.ds(pl.multiple_of(index * band, band), band)]
+    def projection_grad(index):
+        left = h1_ref[:, pl.ds(index * band, band)]
         value = lax.dot_general(left, all3[...], TN, preferred_element_type=F32)
         g3[index] = value.astype(BF16).reshape(g3.shape[1:])
-        return carry
-
+
+    for index in range(heads):
+        output_grad(index)
+    scatters[0].start_near()
     for chunk in range(CHUNKS):
         partial_step(chunk)
         set_off(chunk)
         if chunk == 0:
-            for index in range(heads):
-                output_grad(index)
-            scatters[0].start_near()
+            scatters[0].start_across()
         if chunk > 1:
             relay(chunk - 2)
     for step in range(1, ntp):
         sums_copy(step).start()
     for step in range(1, nseq):
         vec_copy(step).start()
-    scatters[0].start_across()
-    lax.fori_loop(0, heads, grad_step, 0)
+    for index in range(heads // 2):
+        projection_grad(index)
+    relay(CHUNKS - 2)
+    for index in range(heads // 2, heads):
+        projection_grad(index)
     scatters[1].start_near()
-    relay(CHUNKS - 2)
-    scatters[1].start_across()
     for step in range(1, nseq):
         vec_copy(step).wait_recv()
     total = vbuf[...]
@@ -1370,12 +1386,13 @@
     vsum[...] = total
     for step in range(1, ntp):
         vec_far_copy(step).start()
+    scatters[1].start_across()
+    relay(CHUNKS - 1)
     value = scatters[0].result().astype(BF16)
     for index in range(ntp):
         wbuf[index] = value[:, index * local_width : (index + 1) * local_width]
     for step in range(1, ntp):
         w_copy(step).start()
-    relay(CHUNKS - 1)
 
     for step in range(1, ntp):
         sums_copy(step).wait_recv()
@@ -1417,7 +1434,7 @@
     vout_ref[...] = vsum[...]
     for step in range(ntp - 1):
         vout_ref[: 6 * per] += vec_far[step, : 6 * per]
-    ow_ref[...] = add_up(wbuf[tp], *[wfar[step] for step in range(ntp - 1)])
+    ow_ref[...] = add_up(wbuf[tp], *[wfar[step] for step in range(ntp - 1)]).T
 
     for chunk in range(CHUNKS):
         for step in range(1, share):
@@ -1456,7 +1473,7 @@
     nvec = vec.shape[0] + 2 * per + 3 * local_width // WIDE
     outs = [
         sds((rows, width), F32),
-        sds((band, local_width), F32),
+        sds((local_width, band), F32),
         sds((band, local_width), F32),
         sds((band, local_width), F32),
         sds((band, local_width), F32),
@@ -1501,6 +1518,7 @@
         out_specs=[IN_VMEM] * len(outs),
         scratch_shapes=scratch + sems,
         name="tail",
+        cost_estimate=pl.CostEstimate(flops=70 << 30, bytes_accessed=8 << 20, transcendentals=0),
         compiler_params=pltpu.CompilerParams(
             collective_id=3, has_side_effects=True, vmem_limit_bytes=60 << 20
         ),
@@ -1550,7 +1568,7 @@
     kv = kv.reshape(nseq * rows, WIDE)
     sds = jax.ShapeDtypeStruct
     packed, res = local_call(
-        functools.partial(forward_kernel, dims, nrows, 1),
+        functools.partial(forward_kernel, dims, nrows, 4),
         "attention_forward",
         (sds((heads * rows // 2, WIDE), BF16), sds((heads * rows, WIDE), F32)),
         2,
@@ -1562,15 +1580,15 @@
     )
     result = lax.psum_scatter(out_sum, "tp", scatter_dimension=0)
     dq, dkv = local_call(
-        functools.partial(backward_kernel, dims, nrows, 1),
+        functools.partial(backward_kernel, dims, nrows, 4),
         "attention_backward",
         (sds((heads * rows // 2, WIDE), BF16), sds((nseq * rows, WIDE), BF16)),
         4,
         [pltpu.VMEM((nseq * rows, WIDE), F32)],
     )(table, q, do.reshape(heads * rows // 2, WIDE), res, kv)
     grad_x, output_part, query_part, key_part, value_part, vectors = run_tail(
-        dims, dq.reshape(heads, rows // 2, WIDE), dkv.reshape(share, heads, rows, WIDE), h1, x_parts,
-        da, mixed, stats, norm_gain[None, :], query_weight, key_weight, value_weight, vec,
+        dims, dq.reshape(heads, rows // 2, WIDE), dkv.reshape(share, heads, rows, WIDE), h1,
+        x_parts, da, mixed, stats, norm_gain[None, :], query_weight, key_weight, value_weight, vec,
     )
     my_bias = lax.dynamic_slice_in_dim(outer_bias, tp * width, width, 0)
     layer_out = (result.astype(F32) + my_bias).astype(BF16).reshape(hidden_in.shape)
@@ -1586,13 +1604,13 @@
         key_part,
         value_part,
         narrow[2 * local_width : 3 * local_width],
-        output_part.T,
+        output_part,
         wide[2],
         wide[3],
         wide[4],
         inner_part,
         narrow[3 * local_width :],
-        outer_part.T,
+        outer_part,
         wide[5],
     )
 

time: 345 us -> 330 us (0.957)
  Pallas kernels: 300 us -> 285 us
    pallas_call x1, Pallas kernels: 111 us -> 96.2 us  [run_middle(): pl.pallas_call(functools.partial(middle_kernel, dims), out_shape=outs, in...]
    pallas_call x2, Pallas kernels: 63.9 us -> 55.5 us  [the longest x1 28.7 us: on_device(): local_call(functools.partial(backward_kernel, dims, nrows, 4), 'attention...]
    pallas_call x1, Pallas kernels: 65.5 us -> 73.8 us  [run_tail(): pl.pallas_call(functools.partial(tail_kernel, dims), out_shape=outs, in_s...]
  transfers between devices with their start and end apart: 2 -> 2, of which waited for: 1 -> 1; matrix products, arithmetic and copies ran while one was open for 2% -> 1% of each run, Pallas kernels for 38% -> 39%
where the time goes in v5:
time: 330 us; the launch traced here: 328 us
  Pallas kernels  285 us (86%)
  waiting for transfers between devices  16.1 us (5%)
  between operations  14.2 us (4%)
  local copies, waits for them, and re-layouts  9.26 us (3%)
  other arithmetic  3.33 us (1%)
    pallas_call x1, Pallas kernels, run_middle(): pl.pallas_call(functools.partial(middle_kernel, dims), out_shape=outs, in...  96.2 us
    pallas_call x1, Pallas kernels, run_tail(): pl.pallas_call(functools.partial(tail_kernel, dims), out_shape=outs, in_s...  73.8 us
    pallas_call x1, Pallas kernels, run_head(): pl.pallas_call(functools.partial(head_kernel, dims, nrows), out_shape=out...  59.5 us
    pallas_call x1, Pallas kernels, on_device(): local_call(functools.partial(backward_kernel, dims, nrows, 4), 'attention...  28.7 us
    pallas_call x1, Pallas kernels, on_device(): local_call(functools.partial(forward_kernel, dims, nrows, 4), 'attention_...  26.8 us
    all_gather x1, waiting for transfers between devices, on_device(): g_rest = lax.all_gather(rest, 'tp', axis=0)  16 us
  transfers between devices with their start and end apart: 2, of which 1 were waited for; matrix products, arithmetic and copies ran while one was open for 1% of the time, Pallas kernels for 39%

profile of v5, /device:TPU:8, one launch (start us, length us, event | category | flops | bytes accessed | tf_op | source)
XLA Modules:
  0.0 328.0 jit_solution(7382055957835030751)
XLA Ops:
  7.2 0.0 all-gather.3.cloned.1.call-start
  7.2 59.5 %head.1 = (bf16[4,1024,128]{2,1,0:T(8,128)(2,1)}, bf16[2,4,1024,128]{3,2,1,0:T(8,128)(2,1)}, bf16[1024,1024]{1,0:T(8,128)(2,1)}, bf16[4,1024,256]{2,1,0:T(8,128)...) custom-call(s32[32]{0:T(128)} %docs_ref.1, ...), custom_call_target="tpu_custom_call" | custom-call | flops 64424509440 | bytes 8388608 | tf_op jit(solution)/shard_map/head/pallas_call | solution.py:427
  66.7 0.0 all-gather.3.cloned.1.call-update
  66.8 0.2 reduce-scatter.2.cloned.1.call-start
  67.0 1.3 dynamic_slice.3
  68.3 26.8 %attention_forward.1 = (bf16[2048,128]{1,0:T(8,128)(2,1)}, f32[4096,128]{1,0:T(8,128)}) custom-call(s32[16,128]{1,0:T(8,128)} %get-tuple-element.44.table_ref, bf16[4096,128]{1,0:T(8,128)(2,1)} %bitcast.57, bf16[8192,128]{1,0:T(8,128)(2,1)} %bitcast.54), custom_call_target="tpu_custom_call" | custom-call | flops 32212254720 | bytes 8388608 | tf_op jit(solution)/shard_map/attention_forward/pallas_call | solution.py:1570
  95.1 16.0 %all-gather.3.cloned.1.call-done = bf16[3072,256]{1,0:T(8,128)(2,1)} async-done(((bf16[768,256]{1,0:T(8,128)(2,1)}), bf16[3072,256]{1,0:T(8,128)(2,1)}) %all-gather.3.cloned.1.call-update) | async-done | bytes 1572880 | tf_op jit(solution)/shard_map/all_gather | solution.py:1566
  111.1 96.2 %middle.1 = (bf16[4,1024,256]{2,1,0:T(8,128)(2,1)}, bf16[4,512,128]{2,1,0:T(8,128)(2,1)}, bf16[256,1024]{1,0:T(8,128)(2,1)}, bf16[256,1024]{1,0:T(8,128)(2,1)}, ...) custom-call(bf16[4,512,128]{2,1,0:T(8,128)(2,1)} %bitcast.61, ...), custom_call_target="tpu_custom_call" | custom-call | flops 118111600640 | bytes 8388608 | tf_op jit(solution)/shard_map/middle/pallas_call | solution.py:1111
  207.3 0.0 reduce-scatter.2.cloned.1.call-update
  207.3 28.7 %attention_backward.1 = (bf16[2048,128]{1,0:T(8,128)(2,1)}, bf16[8192,128]{1,0:T(8,128)(2,1)}) custom-call(s32[16,128]{1,0:T(8,128)} %get-tuple-element.44.table_ref, bf16[4096,128]{1,0:T(8,128)(2,1)} %bitcast.58, bf16[2048,128]{1,0:T(8,128)(2,1)} %bitcast.59, f32[4096,128]{1,0:T(8,128)} %get-tuple-element.54.res_ref, bf16[8192,128]{1,0:T(8,128)(2,1)} %bitcast.55), custom_call_target="tpu_custom_call" | custom-call | flops 32212254720 | bytes 8388608 | tf_op jit(solution)/shard_map/attention_backward/pallas_call | solution.py:1582
  236.0 73.8 %tail.1 = (f32[1024,256]{1,0:T(8,128)}, f32[256,128]{1,0:T(8,128)}, f32[128,256]{1,0:T(8,128)}, f32[128,256]{1,0:T(8,128)}, f32[128,256]{1,0:T(8,128)}, /*index=5*/f32[62,128]{1,0:T(8,128)}) custom-call(bf16[4,512,128]{2,1,0:T(8,128)(2,1)} %bitcast.60, bf16[2,4,1024,128]{3,2,1,0:T(8,128)(2,1)} %bitcast.56, bf16[1024,1024]{1,0:T(8,128)(2,1)} %get-tuple-element.57.h1_hbm, ...), custom_call_target="tpu_custom_call" | custom-call | flops 75161927680 | bytes 8388608 | tf_op jit(solution)/shard_map/tail/pallas_call | solution.py:1514
  309.9 1.3 slice_bitcast_fusion.7
  311.2 1.3 slice_bitcast_fusion
  312.5 0.0 reduce-scatter.2.cloned.1.call-done
  312.5 0.0 copy-done.6
  312.6 0.0 copy-start.1
  312.6 2.0 fusion
  314.6 2.4 copy.44
  316.9 0.7 copy.45
  317.6 0.7 copy.46
  318.2 0.7 copy.47
  318.9 0.7 copy.48
  319.6 0.8 copy.49
  320.3 0.8 copy.50
  (12 shorter events, 0.0 us)
Async XLA Ops:
  7.2 104.0 %all-gather.3.cloned.1.call-start = ((), (), s32[]{:S(2)}) async-start(), calls=%async_computation.2 | async-start | bytes 1966080 | tf_op jit(solution)/shard_map/all_gather | solution.py:1566
  66.8 245.8 %reduce-scatter.2.cloned.1.call-start = ((), (), s32[]{:S(2)}) async-start(), calls=%async_computation.1 | async-start | bytes 2621440 | tf_op jit(solution)/shard_map/reduce_scatter | solution.py:1581
  236.0 76.5 %copy-start.6 = (f32[256]{0:T(256)S(1)}, f32[256]{0:T(256)}, u32[]{:S(2)}) copy-start(f32[256]{0:T(256)} %dynamic_slice.3) | copy-start | bytes 3076
  309.8 7.1 %copy-start.5 = (f32[128,256]{1,0:T(8,128)S(1)}, f32[128,256]{1,0:T(8,128)}, u32[]{:S(2)}) copy-start(f32[128,256]{1,0:T(8,128)} %get-tuple-element.101) | copy-start | bytes 393220
  309.8 7.7 %copy-start.4 = (f32[128,256]{1,0:T(8,128)S(1)}, f32[128,256]{1,0:T(8,128)}, u32[]{:S(2)}) copy-start(f32[128,256]{1,0:T(8,128)} %get-tuple-element.103) | copy-start | bytes 393220
  309.8 8.4 %copy-start.3 = (f32[128,256]{1,0:T(8,128)S(1)}, f32[128,256]{1,0:T(8,128)}, u32[]{:S(2)}) copy-start(f32[128,256]{1,0:T(8,128)} %get-tuple-element.104) | copy-start | bytes 393220
  309.8 9.0 %copy-start.2 = (f32[256,128]{1,0:T(8,128)S(1)}, f32[256,128]{1,0:T(8,128)}, u32[]{:S(2)}) copy-start(f32[256,128]{1,0:T(8,128)} %get-tuple-element.106) | copy-start | bytes 393220
  312.6 7.0 %copy-start.1 = (f32[128,1024]{1,0:T(8,128)S(1)}, f32[128,1024]{1,0:T(8,128)}, u32[]{:S(2)}) copy-start(f32[128,1024]{1,0:T(8,128)} %get-tuple-element.110) | copy-start | bytes 1572868
  314.6 5.8 %copy-start = (f32[1024,128]{1,0:T(8,128)S(1)}, f32[1024,128]{1,0:T(8,128)}, u32[]{:S(2)}) copy-start(f32[1024,128]{1,0:T(8,128)} %get-tuple-element.112) | copy-start | bytes 1572868
Sparse Core Ops, SparseCore 0:
  66.9 44.2 all-gather.2
  207.5 57.1 reduce-scatter.1

commit v6 on v5

--- a/solution.py
+++ b/solution.py
@@ -313,6 +313,12 @@
     ]
     for copy in early:
         copy.start()
+    copies = [
+        pltpu.make_async_copy(
+            cot_ref.at[pl.ds(g_out.shape[1], rest_out.shape[0])], rest_out, local.at[2]
+        )
+    ]
+    copies[0].start()
     greet(
         [place.partner(step)[1] for step in range(1, share)]
         + [place.across(step)[1] for step in range(1, heads)]
@@ -334,6 +340,12 @@
             own_send(chunk + 1)
         pass_on(chunk)
         compute(chunk)
+        here = chunk_of(chunk)
+        for index, (source, target) in enumerate(
+            [(h1.at[here], h1_out.at[here]), (xs.at[:, here], xs_out.at[:, here])]
+        ):
+            copies.append(pltpu.make_async_copy(source, target, local.at[7 + 2 * chunk + index]))
+            copies[-1].start()
         for step in range(1, heads):
             kv_copy(chunk, step).start()
         for step in range(1, heads):
@@ -344,19 +356,11 @@
             for step in range(1, heads):
                 wo_across(step).wait_recv()
             wo_swap().start()
-    pairs = [
-        (qbuf.at[head], q_out.at[head]),
-        (kvbuf.at[head], kv_out.at[part, head]),
-        (h1, h1_out),
-        (xs, xs_out),
-        (cot_ref.at[pl.ds(g_out.shape[1], rest_out.shape[0])], rest_out),
-    ]
-    copies = [
-        pltpu.make_async_copy(source, target, local.at[index])
-        for index, (source, target) in enumerate(pairs)
-    ]
-    for copy in copies:
-        copy.start()
+    for index, (source, target) in enumerate(
+        [(qbuf.at[head], q_out.at[head]), (kvbuf.at[head], kv_out.at[part, head])]
+    ):
+        copies.append(pltpu.make_async_copy(source, target, local.at[index]))
+        copies[-1].start()
     mine = pl.ds(pl.multiple_of(tp * (rows // ntp), rows // ntp), rows // ntp)
     xt_out[...] = xs[:, mine]
     hand_on(CHUNKS - 1)
@@ -422,12 +426,12 @@
     sems = (
         [dma(CHUNKS + COT_CHUNKS, ntp)] * 4 + [dma(CHUNKS, heads - 1)] * 4
         + [dma(CHUNKS, heads, share - 1)] * 2 + [dma(ntp - 1)] * 2 + [dma(heads - 1)] * 2
-        + [dma(1)] * 2 + [dma(7)]
+        + [dma(1)] * 2 + [dma(7 + 2 * CHUNKS)]
     )
     return pl.pallas_call(
         functools.partial(head_kernel, dims, nrows),
         out_shape=outs,
-        in_specs=[IN_SMEM, IN_SMEM] + [IN_VMEM] * len(params) + [ANYWHERE] * 2,
+        in_specs=[IN_SMEM, IN_SMEM] + [IN_VMEM] * (2 + len(params)),
         out_specs=[ANYWHERE] * 7 + [IN_VMEM] * 3,
         scratch_shapes=scratch + sems,
         name="head",
@@ -718,7 +722,7 @@
 
 def middle_kernel(
     dims,
-    o_ref, g0_hbm, g1_hbm, wo_hbm, wi_hbm, wu_hbm, xt_ref, ob_ref, gain_ref, shift_ref, ib_ref,
+    o_ref, g0_hbm, g1_hbm, wo_hbm, wi_hbm, wu_hbm, xt_ref, ob_ref, gain_ref, shift_ref, ib_ref, ub_ref,
     sum_out, do_out, da_out, mixed_out, vec_out, gi_out, gu_out,
     g_ref, wo_ref, wi_ref, wu_ref, o_in, x1, xhat, scale, h2, act, dpre, outb, terms, from_left, from_right, do_buf, ib_sum, gi, gu, land_i, land_u, pair_i, pair_u, far_i, far_u,
     *rest,
@@ -883,7 +887,7 @@
             term_copy(index, owner, False).start()
 
         out = jnp.dot(value, wu_ref[...], preferred_element_type=F32)
-        out = out + jnp.where(owner == tp, x1[here], 0.0)
+        out = out + jnp.where(owner == tp, x1[here] + ub_ref[...], 0.0)
         for i in range(ntp):
             outb[i, wide] = out[:, i * width : (i + 1) * width].astype(BF16)
 
@@ -1059,7 +1063,7 @@
         scatter.finish()
 
 
-def run_middle(dims, o, g0, g1, wo, wi, wu, xt, ob, gain, shift, ib):
+def run_middle(dims, o, g0, g1, wo, wi, wu, xt, ob, gain, shift, ib, ub):
     heads, share, nseq, ntp = dims
     rows, width = g0.shape[1] + g1.shape[1], g0.shape[2]
     features, hidden = width * ntp, wi.shape[1]
@@ -1111,7 +1115,7 @@
     return pl.pallas_call(
         functools.partial(middle_kernel, dims),
         out_shape=outs,
-        in_specs=[ANYWHERE] * 6 + [IN_VMEM] * 5,
+        in_specs=[ANYWHERE] * 6 + [IN_VMEM] * 6,
         out_specs=[ANYWHERE] * 2 + [IN_VMEM] * 5,
         scratch_shapes=scratch + sems,
         name="middle",
@@ -1119,14 +1123,14 @@
         compiler_params=pltpu.CompilerParams(
             collective_id=2, has_side_effects=True, vmem_limit_bytes=63 << 20
         ),
-    )(o, g0, g1, wo, wi, wu, xt, ob, gain, shift, ib)
+    )(o, g0, g1, wo, wi, wu, xt, ob, gain, shift, ib, ub)
 
 
 def tail_kernel(
     dims,
     dq_ref, dkv_hbm, h1_hbm, x_hbm, da_ref, mixed_ref, stat_ref, gain_ref, wq_ref, wk_ref, wv_ref, vec_ref,
     gx_ref, ow_ref, oq_ref, ok_ref, ov_ref, vout_ref,
-    dkv_own, h1_ref, x_ref, dq_in, dkv_in, dkv_land, dkv_sum, all3, da_in, pbuf, from_left, from_right,
+    dkv_own, h1_ref, x_ref, dq_in, dkv_in, dkv_land, dkv_sum, all3, pbuf, from_left, from_right,
     sums, sums_land, vbuf, vec_land, vsum, vec_far, gw, g3, wbuf, wfar,
     *rest,
 ):
@@ -1135,7 +1139,7 @@
     head, part, seq, tp = place.head, place.part, place.seq, place.tp
     lands, sems = rest[:6], rest[6:]
     (dq_s, dq_r, kv1_s, kv1_r, kv2_s, kv2_r, right_s, right_r, left_s, left_r,
-     da_s, da_r, st_s, st_r, v1_s, v1_r, v2_s, v2_r, w_s, w_r, g1_s, g1_r, g2_s, g2_r, load_s) = sems
+     st_s, st_r, v1_s, v1_r, v2_s, v2_r, w_s, w_r, g1_s, g1_r, g2_s, g2_r, load_s) = sems
     rows, features = h1_ref.shape
     width = features // ntp
     tokens = rows // ntp
@@ -1173,12 +1177,6 @@
         return remote(
             dkv_sum.at[other, chunk_of(chunk)], dkv_in.at[head, chunk_of(chunk)],
             kv2_s.at[chunk, step - 1], kv2_r.at[chunk, step - 1], device,
-        )
-
-    def da_copy(step):
-        other, device = place.along(step)
-        return remote(
-            da_ref.at[:, columns_of(other)], da_in.at[tp], da_s.at[step - 1], da_r.at[step - 1], device
         )
 
     def rightward(chunk, index):
@@ -1235,9 +1233,6 @@
     for chunk in range(CHUNKS):
         for step in range(1, share):
             dkv_near(chunk, step).start()
-    for step in range(1, ntp):
-        da_copy(step).start()
-    da_in[tp] = da_ref[:, columns_of(tp)]
     vbuf[: 2 * per] = jnp.zeros((2 * per, WIDE), F32)
     vbuf[2 * per : 6 * per] = vec_ref[: 4 * per]
     narrow = 3 * local_width // WIDE
@@ -1308,6 +1303,16 @@
                 vbuf[row : row + 1, :] += col0[:, lanes]
                 vbuf[per + row : per + row + 1, :] += col1[:, lanes]
             pbuf[chunk, index] = piece.astype(BF16)
+            for sub in range(max(chunk_rows // tokens, 1)):
+                rows_here = slice(sub * tokens, sub * tokens + min(tokens, chunk_rows))
+
+                @pl.when(tp == chunk * chunk_rows // tokens + sub)
+                def _():
+                    start = chunk * chunk_rows % tokens
+                    carried = da_ref[start : start + min(tokens, chunk_rows), cols].astype(F32)
+                    carried = carried / (scale[rows_here] * gain[:, cols])
+                    pbuf[chunk, index, rows_here] = (piece[rows_here] + carried).astype(BF16)
+
         both = jnp.where(lane == 0, sum0, jnp.where(lane == 1, sum1, 0.0))
         sums[:, here] = both.T[:8]
 
@@ -1396,9 +1401,7 @@
 
     for step in range(1, ntp):
         sums_copy(step).wait_recv()
-        da_copy(step).wait_recv()
     my_gain = gain_ref[:, columns_of(tp)]
-    da_rows = da_in.shape[1]
     for chunk in range(CHUNKS):
         here = chunk_of(chunk)
         both = sums[:, here]
@@ -1420,10 +1423,7 @@
         grad = grad + jnp.where(tp < ntp - 1, from_right[chunk, tp].astype(F32), 0.0)
         mean, scale = stat_ref[here, 0:1], stat_ref[here, 1:2]
         xhat = (x_ref[tp, here].astype(F32) - mean) * scale
-        inner = grad * my_gain - both[:, 0:1] - xhat * both[:, 1:2]
-        many = chunk_rows // da_rows
-        branch = da_in[chunk * many : (chunk + 1) * many].reshape(chunk_rows, width)
-        gx_ref[here] = branch.astype(F32) + scale * inner
+        gx_ref[here] = scale * (grad * my_gain - both[:, 0:1] - xhat * both[:, 1:2])
     value = scatters[1].result()
     oq_ref[...] = 0.125 * value[:, :local_width]
     ok_ref[...] = value[:, local_width : 2 * local_width]
@@ -1453,7 +1453,6 @@
 
     for step in range(1, ntp):
         sums_copy(step).wait_send()
-        da_copy(step).wait_send()
         vec_far_copy(step).wait_send()
         w_copy(step).wait_send()
     for step in range(1, nseq):
@@ -1489,7 +1488,6 @@
         vmem(max(share - 1, 1), heads, rows, WIDE),
         vmem(heads, rows, WIDE),
         vmem(rows, 3 * local_width),
-        vmem(ntp, tokens, width),
         vmem(*pieces),
         vmem(*pieces),
         vmem(*pieces),
@@ -1508,7 +1506,7 @@
     ]
     sems = (
         [dma(CHUNKS, heads - 1)] * 2 + [dma(CHUNKS, share - 1)] * 2 + [dma(CHUNKS, heads - 1)] * 2
-        + [dma(CHUNKS, ntp)] * 4 + [dma(ntp - 1)] * 4 + [dma(nseq - 1)] * 2 + [dma(ntp - 1)] * 4
+        + [dma(CHUNKS, ntp)] * 4 + [dma(ntp - 1)] * 2 + [dma(nseq - 1)] * 2 + [dma(ntp - 1)] * 4
         + GradScatter.semaphores(dims, 2) + [dma(4)]
     )
     return pl.pallas_call(
@@ -1550,7 +1548,6 @@
     nrows, block_len, width = hidden_in.shape
     rows = nrows * block_len
     nseq, ntp = lax.axis_size("seq"), lax.axis_size("tp")
-    tp = lax.axis_index("tp")
     local_width = query_weight.shape[1]
     heads = local_width // HEAD_DIM
     share = nseq // heads
@@ -1576,7 +1573,7 @@
     out_sum, do, da, mixed, vec, inner_part, outer_part = run_middle(
         dims, packed.reshape(heads, rows // 2, WIDE), g_first, g_rest, output_full,
         inner_weight, outer_weight, x_mine, output_bias[None, :], feed_gain[None, :],
-        feed_shift[None, :], inner_bias[None, :],
+        feed_shift[None, :], inner_bias[None, :], outer_bias[None, :],
     )
     result = lax.psum_scatter(out_sum, "tp", scatter_dimension=0)
     dq, dkv = local_call(
@@ -1590,12 +1587,10 @@
         dims, dq.reshape(heads, rows // 2, WIDE), dkv.reshape(share, heads, rows, WIDE), h1,
         x_parts, da, mixed, stats, norm_gain[None, :], query_weight, key_weight, value_weight, vec,
     )
-    my_bias = lax.dynamic_slice_in_dim(outer_bias, tp * width, width, 0)
-    layer_out = (result.astype(F32) + my_bias).astype(BF16).reshape(hidden_in.shape)
     wide = vectors[: 6 * per].reshape(6, features)
     narrow = vectors[6 * per :].reshape(-1)
     return (
-        layer_out,
+        result.reshape(hidden_in.shape),
         grad_x.reshape(hidden_in.shape),
         wide[0],
         wide[1],

time: 330 us -> 311 us (0.942)
  Pallas kernels: 285 us -> 274 us
  waiting for transfers between devices: 16.1 us -> 12 us
    pallas_call x1, Pallas kernels: 73.8 us -> 66.4 us  [run_tail(): pl.pallas_call(functools.partial(tail_kernel, dims), out_shape=outs, in_s...]
    all_gather x1, waiting for transfers between devices: 16 us -> 11.9 us  [on_device(): g_rest = lax.all_gather(rest, 'tp', axis=0)]
where the time goes in v6:
time: 311 us; the launch traced here: 309 us
  Pallas kernels  274 us (88%)
  between operations  14.2 us (5%)
  waiting for transfers between devices  12 us (4%)
  local copies, waits for them, and re-layouts  7.93 us (3%)
    pallas_call x1, Pallas kernels, run_middle(): pl.pallas_call(functools.partial(middle_kernel, dims), out_shape=outs, in...  96 us
    pallas_call x1, Pallas kernels, run_tail(): pl.pallas_call(functools.partial(tail_kernel, dims), out_shape=outs, in_s...  66.4 us
    pallas_call x1, Pallas kernels, run_head(): pl.pallas_call(functools.partial(head_kernel, dims, nrows), out_shape=out...  57.9 us
    pallas_call x1, Pallas kernels, on_device(): local_call(functools.partial(backward_kernel, dims, nrows, 4), 'attention...  27.6 us
    pallas_call x1, Pallas kernels, on_device(): local_call(functools.partial(forward_kernel, dims, nrows, 4), 'attention_...  25.9 us
    all_gather x1, waiting for transfers between devices, on_device(): g_rest = lax.all_gather(rest, 'tp', axis=0)  11.9 us
    unnamed x19, local copies, waits for them, and re-layouts  6.58 us
  transfers between devices with their start and end apart: 2, of which 1 were waited for; matrix products, arithmetic and copies ran while one was open for 1% of the time, Pallas kernels for 39%

profile of v6, /device:TPU:8, one launch (start us, length us, event | category | flops | bytes accessed | tf_op | source)
XLA Modules:
  0.0 309.5 jit_solution(15270895764479217816)
XLA Ops:
  7.2 0.0 all-gather.3.cloned.1.call-start
  7.2 57.9 %head.1 = (bf16[4,1024,128]{2,1,0:T(8,128)(2,1)}, bf16[2,4,1024,128]{3,2,1,0:T(8,128)(2,1)}, bf16[1024,1024]{1,0:T(8,128)(2,1)}, bf16[4,1024,256]{2,1,0:T(8,128)...) custom-call(s32[32]{0:T(128)} %docs_ref.1, ...), custom_call_target="tpu_custom_call" | custom-call | flops 64424509440 | bytes 8388608 | tf_op jit(solution)/shard_map/head/pallas_call | solution.py:431
  65.2 0.0 all-gather.3.cloned.1.call-update
  65.2 0.2 reduce-scatter.2.cloned.1.call-start
  65.4 25.9 %attention_forward.1 = (bf16[2048,128]{1,0:T(8,128)(2,1)}, f32[4096,128]{1,0:T(8,128)}) custom-call(s32[16,128]{1,0:T(8,128)} %get-tuple-element.44.table_ref, bf16[4096,128]{1,0:T(8,128)(2,1)} %bitcast.58, bf16[8192,128]{1,0:T(8,128)(2,1)} %bitcast.55), custom_call_target="tpu_custom_call" | custom-call | flops 32212254720 | bytes 8388608 | tf_op jit(solution)/shard_map/attention_forward/pallas_call | solution.py:1567
  91.3 11.9 %all-gather.3.cloned.1.call-done = bf16[3072,256]{1,0:T(8,128)(2,1)} async-done(((bf16[768,256]{1,0:T(8,128)(2,1)}), bf16[3072,256]{1,0:T(8,128)(2,1)}) %all-gather.3.cloned.1.call-update) | async-done | bytes 1572880 | tf_op jit(solution)/shard_map/all_gather | solution.py:1563
  103.3 96.0 %middle.1 = (bf16[4,1024,256]{2,1,0:T(8,128)(2,1)}, bf16[4,512,128]{2,1,0:T(8,128)(2,1)}, bf16[256,1024]{1,0:T(8,128)(2,1)}, bf16[256,1024]{1,0:T(8,128)(2,1)}, ...) custom-call(bf16[4,512,128]{2,1,0:T(8,128)(2,1)} %bitcast.62, ...), custom_call_target="tpu_custom_call" | custom-call | flops 118111600640 | bytes 8388608 | tf_op jit(solution)/shard_map/middle/pallas_call | solution.py:1115
  199.3 0.0 reduce-scatter.2.cloned.1.call-update
  199.3 27.6 %attention_backward.1 = (bf16[2048,128]{1,0:T(8,128)(2,1)}, bf16[8192,128]{1,0:T(8,128)(2,1)}) custom-call(s32[16,128]{1,0:T(8,128)} %get-tuple-element.44.table_ref, bf16[4096,128]{1,0:T(8,128)(2,1)} %bitcast.59, bf16[2048,128]{1,0:T(8,128)(2,1)} %bitcast.60, f32[4096,128]{1,0:T(8,128)} %get-tuple-element.54.res_ref, bf16[8192,128]{1,0:T(8,128)(2,1)} %bitcast.56), custom_call_target="tpu_custom_call" | custom-call | flops 32212254720 | bytes 8388608 | tf_op jit(solution)/shard_map/attention_backward/pallas_call | solution.py:1579
  226.9 66.4 %tail.1 = (f32[1024,256]{1,0:T(8,128)}, f32[256,128]{1,0:T(8,128)}, f32[128,256]{1,0:T(8,128)}, f32[128,256]{1,0:T(8,128)}, f32[128,256]{1,0:T(8,128)}, /*index=5*/f32[62,128]{1,0:T(8,128)}) custom-call(bf16[4,512,128]{2,1,0:T(8,128)(2,1)} %bitcast.61, bf16[2,4,1024,128]{3,2,1,0:T(8,128)(2,1)} %bitcast.57, bf16[1024,1024]{1,0:T(8,128)(2,1)} %get-tuple-element.57.h1_hbm, ...), custom_call_target="tpu_custom_call" | custom-call | flops 75161927680 | bytes 8388608 | tf_op jit(solution)/shard_map/tail/pallas_call | solution.py:1512
  293.4 1.3 slice_bitcast_fusion.7
  294.7 1.3 slice_bitcast_fusion
  296.0 0.0 reduce-scatter.2.cloned.1.call-done
  296.0 0.0 copy-start
  296.1 2.4 copy.44
  298.4 0.0 copy-done.5
  298.4 0.7 copy.45
  299.1 0.0 copy-done.4
  299.1 0.7 copy.46
  299.7 0.7 copy.47
  300.4 0.7 copy.48
  301.0 0.8 copy.49
  301.8 0.0 copy-done
  301.8 0.8 copy.50
  (8 shorter events, 0.0 us)
Async XLA Ops:
  7.2 96.1 %all-gather.3.cloned.1.call-start = ((), (), s32[]{:S(2)}) async-start(), calls=%async_computation.2 | async-start | bytes 1966080 | tf_op jit(solution)/shard_map/all_gather | solution.py:1563
  65.2 230.8 %reduce-scatter.2.cloned.1.call-start = ((), (), s32[]{:S(2)}) async-start(), calls=%async_computation.1 | async-start | bytes 2621440 | tf_op jit(solution)/shard_map/reduce_scatter | solution.py:1578
  293.3 5.1 %copy-start.5 = (f32[128,256]{1,0:T(8,128)S(1)}, f32[128,256]{1,0:T(8,128)}, u32[]{:S(2)}) copy-start(f32[128,256]{1,0:T(8,128)} %get-tuple-element.101) | copy-start | bytes 393220
  293.3 5.8 %copy-start.4 = (f32[128,256]{1,0:T(8,128)S(1)}, f32[128,256]{1,0:T(8,128)}, u32[]{:S(2)}) copy-start(f32[128,256]{1,0:T(8,128)} %get-tuple-element.103) | copy-start | bytes 393220
  293.3 6.4 %copy-start.3 = (f32[128,256]{1,0:T(8,128)S(1)}, f32[128,256]{1,0:T(8,128)}, u32[]{:S(2)}) copy-start(f32[128,256]{1,0:T(8,128)} %get-tuple-element.104) | copy-start | bytes 393220
  293.3 7.0 %copy-start.2 = (f32[256,128]{1,0:T(8,128)S(1)}, f32[256,128]{1,0:T(8,128)}, u32[]{:S(2)}) copy-start(f32[256,128]{1,0:T(8,128)} %get-tuple-element.106) | copy-start | bytes 393220
  293.3 7.7 %copy-start.1 = (f32[128,1024]{1,0:T(8,128)S(1)}, f32[128,1024]{1,0:T(8,128)}, u32[]{:S(2)}) copy-start(f32[128,1024]{1,0:T(8,128)} %get-tuple-element.110) | copy-start | bytes 1572868
  296.0 5.8 %copy-start = (f32[1024,128]{1,0:T(8,128)S(1)}, f32[1024,128]{1,0:T(8,128)}, u32[]{:S(2)}) copy-start(f32[1024,128]{1,0:T(8,128)} %get-tuple-element.112) | copy-start | bytes 1572868
Sparse Core Ops, SparseCore 0:
  65.3 37.9 all-gather.2
  199.5 44.6 reduce-scatter.1

commit v7 on v6

--- a/solution.py
+++ b/solution.py
@@ -16,6 +16,7 @@
 CHUNKS = 4
 COT_CHUNKS = 1
 ROUNDS = 2
+SPLIT = 2
 NEG = -1e30
 NT = (((1,), (1,)), ((), ()))
 TN = (((0,), (0,)), ((), ()))
@@ -770,8 +771,11 @@
             return remote(spot, spot, hr_s.at[index, owner], hr_r.at[index, owner], (seq, tp + 1))
         return remote(spot, spot, hl_s.at[index, owner], hl_r.at[index, owner], (seq, tp - 1))
 
+    def term_rows(index):
+        return pl.ds(pl.multiple_of(index * (span // SPLIT), span // SPLIT), span // SPLIT)
+
     def term_copy(index, owner, right):
-        here = span_of(index)
+        here = term_rows(index)
         if right:
             return remote(
                 terms.at[owner, here], from_left.at[owner, here],
@@ -847,22 +851,6 @@
         return owner, (owner >= 0) & (owner < ntp)
 
     def feed(index, owner):
-        @pl.when(owner < tp)
-        def _():
-            h2_copy(index, owner, True).wait_recv()
-
-            @pl.when(tp < ntp - 1)
-            def _():
-                h2_copy(index, owner, True).start()
-
-        @pl.when(owner > tp)
-        def _():
-            h2_copy(index, owner, False).wait_recv()
-
-            @pl.when(tp > 0)
-            def _():
-                h2_copy(index, owner, False).start()
-
         here = span_of(index)
         wide = span_of(owner * rounds + index)
         pre = jnp.dot(h2[owner, here], wi_ref[...], preferred_element_type=F32) + ib_ref[...]
@@ -880,11 +868,13 @@
 
         @pl.when((owner > tp) & (tp == 0))
         def _():
-            term_copy(index, owner, True).start()
+            for sub in range(SPLIT):
+                term_copy(index * SPLIT + sub, owner, True).start()
 
         @pl.when((owner < tp) & (tp == ntp - 1))
         def _():
-            term_copy(index, owner, False).start()
+            for sub in range(SPLIT):
+                term_copy(index * SPLIT + sub, owner, False).start()
 
         out = jnp.dot(value, wu_ref[...], preferred_element_type=F32)
         out = out + jnp.where(owner == tp, x1[here] + ub_ref[...], 0.0)
@@ -892,24 +882,28 @@
             outb[i, wide] = out[:, i * width : (i + 1) * width].astype(BF16)
 
     def relay_right(index):
-        here = span_of(index)
         for owner in range(1, ntp):
 
             @pl.when((owner > tp) & (tp > 0))
             def _():
-                term_copy(index, owner, True).wait_recv()
-                terms[owner, here] = add_up(terms[owner, here], from_left[owner, here]).astype(BF16)
-                term_copy(index, owner, True).start()
+                for sub in range(SPLIT):
+                    piece = index * SPLIT + sub
+                    here = term_rows(piece)
+                    term_copy(piece, owner, True).wait_recv()
+                    terms[owner, here] = add_up(terms[owner, here], from_left[owner, here]).astype(BF16)
+                    term_copy(piece, owner, True).start()
 
     def relay_left(index):
-        here = span_of(index)
         for owner in range(ntp - 2, -1, -1):
 
             @pl.when((owner < tp) & (tp < ntp - 1))
             def _():
-                term_copy(index, owner, False).wait_recv()
-                terms[owner, here] = add_up(terms[owner, here], from_right[owner, here]).astype(BF16)
-                term_copy(index, owner, False).start()
+                for sub in range(SPLIT):
+                    piece = index * SPLIT + sub
+                    here = term_rows(piece)
+                    term_copy(piece, owner, False).wait_recv()
+                    terms[owner, here] = add_up(terms[owner, here], from_right[owner, here]).astype(BF16)
+                    term_copy(piece, owner, False).start()
 
     def relay(index, first):
         @pl.when((tp < ntp // 2) == first)
@@ -920,9 +914,32 @@
         def _():
             relay_left(index)
 
+    def pass_on(index, hop):
+        below, above = tp - hop, tp + hop
+
+        @pl.when(below >= 0)
+        def _():
+            h2_copy(index, below, True).wait_recv()
+
+            @pl.when(tp < ntp - 1)
+            def _():
+                h2_copy(index, below, True).start()
+
+        @pl.when(above < ntp)
+        def _():
+            h2_copy(index, above, False).wait_recv()
+
+            @pl.when(tp > 0)
+            def _():
+                h2_copy(index, above, False).start()
+
     def feed_step(count, carry):
         index, position = count // places, count % places
         owner, inside = spot_of(position)
+
+        @pl.when(position % 2 == 1)
+        def _():
+            pass_on(index, (position + 1) // 2)
 
         @pl.when(inside)
         def _():
@@ -959,7 +976,8 @@
         here = slice(index * 2 * BLK, (index + 1) * 2 * BLK)
         half = slice(index * BLK, (index + 1) * BLK)
         wide = pl.ds(pl.multiple_of(tp * tokens + index * 2 * BLK, 2 * BLK), 2 * BLK)
-        for part_index in range(index * rounds // pieces, (index + 1) * rounds // pieces):
+        finer = rounds * SPLIT
+        for part_index in range(index * finer // pieces, (index + 1) * finer // pieces):
 
             @pl.when(tp > 0)
             def _():
@@ -1051,13 +1069,14 @@
             def _():
                 h2_copy(index, owner, False).wait_send()
 
-            @pl.when(tp < owner)
-            def _():
-                term_copy(index, owner, True).wait_send()
-
-            @pl.when(tp > owner)
-            def _():
-                term_copy(index, owner, False).wait_send()
+            for sub in range(SPLIT):
+                @pl.when(tp < owner)
+                def _():
+                    term_copy(index * SPLIT + sub, owner, True).wait_send()
+
+                @pl.when(tp > owner)
+                def _():
+                    term_copy(index * SPLIT + sub, owner, False).wait_send()
 
     for scatter in scatters:
         scatter.finish()
@@ -1109,7 +1128,7 @@
         vmem(max(heads - 1, 1), band, hidden),
     ]
     sems = (
-        [dma(count)] * 2 + [dma(rounds, ntp)] * 8 + [dma(pieces, count)] * 2
+        [dma(count)] * 2 + [dma(rounds, ntp)] * 4 + [dma(rounds * SPLIT, ntp)] * 4 + [dma(pieces, count)] * 2
         + GradScatter.semaphores(dims, 2) + [dma(8)]
     )
     return pl.pallas_call(
@@ -1521,6 +1540,47 @@
             collective_id=3, has_side_effects=True, vmem_limit_bytes=60 << 20
         ),
     )(dq, dkv, h1, x_parts, da, mixed, stats, gain, wq, wk, wv, vec)
+
+
+def deliver_kernel(sizes, *refs):
+    many = (len(refs) - 2 - len(sizes)) // 3
+    vec, sources = refs[0], refs[1 : 1 + many]
+    pieces, targets = refs[1 + many : 1 + many + len(sizes)], refs[1 + many + len(sizes) : 1 + 2 * many + len(sizes)]
+    held, sems = refs[1 + 2 * many + len(sizes) : -1], refs[-1]
+    loads = [
+        pltpu.make_async_copy(source, buf, sems.at[0, index])
+        for index, (source, buf) in enumerate(zip(sources, held))
+    ]
+    saves = [
+        pltpu.make_async_copy(buf, target, sems.at[1, index])
+        for index, (target, buf) in enumerate(zip(targets, held))
+    ]
+    for load in loads:
+        load.start()
+    start = 0
+    for index, (size, factor) in enumerate(sizes):
+        pieces[index][...] = factor * vec[start : start + size]
+        start += size
+    for load, save in zip(loads, saves):
+        load.wait()
+        save.start()
+    for save in saves:
+        save.wait()
+
+
+def deliver(vec, sizes, arrays):
+    sds = jax.ShapeDtypeStruct
+    outs = [sds((size, WIDE), F32) for size, _ in sizes] + [sds(a.shape, a.dtype) for a in arrays]
+    results = pl.pallas_call(
+        functools.partial(deliver_kernel, sizes),
+        out_shape=outs,
+        in_specs=[IN_VMEM] + [ANYWHERE] * len(arrays),
+        out_specs=[IN_VMEM] * len(sizes) + [ANYWHERE] * len(arrays),
+        scratch_shapes=[vmem(*a.shape, dtype=a.dtype) for a in arrays] + [dma(2, len(arrays))],
+        name="deliver",
+        compiler_params=pltpu.CompilerParams(vmem_limit_bytes=60 << 20),
+    )(vec, *arrays)
+    return [item.reshape(-1) for item in results[: len(sizes)]], results[len(sizes) :]
 
 
 def on_device(
@@ -1587,26 +1647,33 @@
         dims, dq.reshape(heads, rows // 2, WIDE), dkv.reshape(share, heads, rows, WIDE), h1,
         x_parts, da, mixed, stats, norm_gain[None, :], query_weight, key_weight, value_weight, vec,
     )
-    wide = vectors[: 6 * per].reshape(6, features)
-    narrow = vectors[6 * per :].reshape(-1)
+    lines = local_width // WIDE
+    sizes = [(per, 1.0)] * 6 + [(lines, 0.125), (lines, 1.0), (lines, 1.0)]
+    sizes += [(vectors.shape[0] - 6 * per - 3 * lines, 1.0)]
+    sums, arrays = deliver(
+        vectors,
+        tuple(sizes),
+        [grad_x, output_part, query_part, key_part, value_part, inner_part, outer_part],
+    )
+    grad_x, output_part, query_part, key_part, value_part, inner_part, outer_part = arrays
     return (
         result.reshape(hidden_in.shape),
         grad_x.reshape(hidden_in.shape),
-        wide[0],
-        wide[1],
+        sums[0],
+        sums[1],
         query_part,
-        0.125 * narrow[:local_width],
+        sums[6],
         key_part,
         value_part,
-        narrow[2 * local_width : 3 * local_width],
+        sums[8],
         output_part,
-        wide[2],
-        wide[3],
-        wide[4],
+        sums[2],
+        sums[3],
+        sums[4],
         inner_part,
-        narrow[3 * local_width :],
+        sums[9],
         outer_part,
-        wide[5],
+        sums[5],
     )
 
 

time: 311 us -> 305 us (0.981)
  local copies, waits for them, and re-layouts: 7.93 us -> 0 us
    unnamed x19 -> x0, local copies, waits for them, and re-layouts: 6.58 us -> none
    pallas_call x0 -> x1, Pallas kernels: none -> 4.24 us  [deliver(): pl.pallas_call(functools.partial(deliver_kernel, sizes), out_shape=outs,...]
  transfers between devices with their start and end apart: 2 -> 2, of which waited for: 1 -> 1; matrix products, arithmetic and copies ran while one was open for 1% -> 0% of each run, Pallas kernels for 39% -> 40%
where the time goes in v7:
time: 305 us; the launch traced here: 303 us
  Pallas kernels  277 us (91%)
  between operations  14.1 us (5%)
  waiting for transfers between devices  11.9 us (4%)
    pallas_call x1, Pallas kernels, run_middle(): pl.pallas_call(functools.partial(middle_kernel, dims), out_shape=outs, in...  96.3 us
    pallas_call x1, Pallas kernels, run_tail(): pl.pallas_call(functools.partial(tail_kernel, dims), out_shape=outs, in_s...  64.7 us
    pallas_call x1, Pallas kernels, run_head(): pl.pallas_call(functools.partial(head_kernel, dims, nrows), out_shape=out...  57.9 us
    pallas_call x1, Pallas kernels, on_device(): local_call(functools.partial(backward_kernel, dims, nrows, 4), 'attention...  27.5 us
    pallas_call x1, Pallas kernels, on_device(): local_call(functools.partial(forward_kernel, dims, nrows, 4), 'attention_...  25.9 us
    all_gather x1, waiting for transfers between devices, on_device(): g_rest = lax.all_gather(rest, 'tp', axis=0)  11.8 us
  transfers between devices with their start and end apart: 2, of which 1 were waited for; matrix products, arithmetic and copies ran while one was open for 0% of the time, Pallas kernels for 40%

profile of v7, /device:TPU:8, one launch (start us, length us, event | category | flops | bytes accessed | tf_op | source)
XLA Modules:
  0.0 302.9 jit_solution(8741730314621199772)
XLA Ops:
  7.2 0.0 all-gather.3.cloned.1.call-start
  7.2 57.9 %head.1 = (bf16[4,1024,128]{2,1,0:T(8,128)(2,1)}, bf16[2,4,1024,128]{3,2,1,0:T(8,128)(2,1)}, bf16[1024,1024]{1,0:T(8,128)(2,1)}, bf16[4,1024,256]{2,1,0:T(8,128)...) custom-call(s32[32]{0:T(128)} %docs_ref.1, ...), custom_call_target="tpu_custom_call" | custom-call | flops 64424509440 | bytes 8388608 | tf_op jit(solution)/shard_map/head/pallas_call | solution.py:432
  65.1 0.0 all-gather.3.cloned.1.call-update
  65.2 0.2 reduce-scatter.2.cloned.1.call-start
  65.4 25.9 %attention_forward.1 = (bf16[2048,128]{1,0:T(8,128)(2,1)}, f32[4096,128]{1,0:T(8,128)}) custom-call(s32[16,128]{1,0:T(8,128)} %get-tuple-element.60.table_ref, bf16[4096,128]{1,0:T(8,128)(2,1)} %bitcast.58, bf16[8192,128]{1,0:T(8,128)(2,1)} %bitcast.55), custom_call_target="tpu_custom_call" | custom-call | flops 32212254720 | bytes 8388608 | tf_op jit(solution)/shard_map/attention_forward/pallas_call | solution.py:1627
  91.3 11.8 %all-gather.3.cloned.1.call-done = bf16[3072,256]{1,0:T(8,128)(2,1)} async-done(((bf16[768,256]{1,0:T(8,128)(2,1)}), bf16[3072,256]{1,0:T(8,128)(2,1)}) %all-gather.3.cloned.1.call-update) | async-done | bytes 1572880 | tf_op jit(solution)/shard_map/all_gather | solution.py:1623
  103.2 96.3 %middle.1 = (bf16[4,1024,256]{2,1,0:T(8,128)(2,1)}, bf16[4,512,128]{2,1,0:T(8,128)(2,1)}, bf16[256,1024]{1,0:T(8,128)(2,1)}, bf16[256,1024]{1,0:T(8,128)(2,1)}, ...) custom-call(bf16[4,512,128]{2,1,0:T(8,128)(2,1)} %bitcast.62, ...), custom_call_target="tpu_custom_call" | custom-call | flops 118111600640 | bytes 8388608 | tf_op jit(solution)/shard_map/middle/pallas_call | solution.py:1134
  199.5 0.0 reduce-scatter.2.cloned.1.call-update
  199.5 27.5 %attention_backward.1 = (bf16[2048,128]{1,0:T(8,128)(2,1)}, bf16[8192,128]{1,0:T(8,128)(2,1)}) custom-call(s32[16,128]{1,0:T(8,128)} %get-tuple-element.60.table_ref, bf16[4096,128]{1,0:T(8,128)(2,1)} %bitcast.59, bf16[2048,128]{1,0:T(8,128)(2,1)} %bitcast.60, f32[4096,128]{1,0:T(8,128)} %get-tuple-element.70.res_ref, bf16[8192,128]{1,0:T(8,128)(2,1)} %bitcast.56), custom_call_target="tpu_custom_call" | custom-call | flops 32212254720 | bytes 8388608 | tf_op jit(solution)/shard_map/attention_backward/pallas_call | solution.py:1639
  227.1 64.7 %tail.1 = (f32[1024,256]{1,0:T(8,128)}, f32[256,128]{1,0:T(8,128)}, f32[128,256]{1,0:T(8,128)}, f32[128,256]{1,0:T(8,128)}, f32[128,256]{1,0:T(8,128)}, /*index=5*/f32[62,128]{1,0:T(8,128)}) custom-call(bf16[4,512,128]{2,1,0:T(8,128)(2,1)} %bitcast.61, bf16[2,4,1024,128]{3,2,1,0:T(8,128)(2,1)} %bitcast.57, bf16[1024,1024]{1,0:T(8,128)(2,1)} %get-tuple-element.73.h1_hbm, ...), custom_call_target="tpu_custom_call" | custom-call | flops 75161927680 | bytes 8388608 | tf_op jit(solution)/shard_map/tail/pallas_call | solution.py:1531
  291.8 4.2 %deliver.1 = (f32[8,128]{1,0:T(8,128)}, f32[8,128]{1,0:T(8,128)}, f32[8,128]{1,0:T(8,128)}, f32[8,128]{1,0:T(8,128)}, f32[8,128]{1,0:T(8,128)}, /*index=5*/f32[8...) custom-call(f32[62,128]{1,0:T(8,128)} %get-tuple-element.79.refs_0_,, ...), custom_call_target="tpu_custom_call" | custom-call | tf_op jit(solution)/shard_map/deliver/pallas_call | solution.py:1574
  296.0 0.0 reduce-scatter.2.cloned.1.call-done
Async XLA Ops:
  7.2 96.0 %all-gather.3.cloned.1.call-start = ((), (), s32[]{:S(2)}) async-start(), calls=%async_computation.2 | async-start | bytes 1966080 | tf_op jit(solution)/shard_map/all_gather | solution.py:1623
  65.2 230.9 %reduce-scatter.2.cloned.1.call-start = ((), (), s32[]{:S(2)}) async-start(), calls=%async_computation.1 | async-start | bytes 2621440 | tf_op jit(solution)/shard_map/reduce_scatter | solution.py:1638
Sparse Core Ops, SparseCore 0:
  65.3 37.8 all-gather.2
  199.7 45.2 reduce-scatter.1

commit v8 on v7

--- a/solution.py
+++ b/solution.py
@@ -1637,7 +1637,7 @@
     )
     result = lax.psum_scatter(out_sum, "tp", scatter_dimension=0)
     dq, dkv = local_call(
-        functools.partial(backward_kernel, dims, nrows, 4),
+        functools.partial(backward_kernel, dims, nrows, 8),
         "attention_backward",
         (sds((heads * rows // 2, WIDE), BF16), sds((nseq * rows, WIDE), BF16)),
         4,

time: 305 us -> 305 us (level)
  no operation moved by 1% of the time
where the time goes in v8:
time: 305 us; the launch traced here: 303 us
  Pallas kernels  277 us (91%)
  between operations  14.1 us (5%)
  waiting for transfers between devices  11.9 us (4%)
    pallas_call x1, Pallas kernels, run_middle(): pl.pallas_call(functools.partial(middle_kernel, dims), out_shape=outs, in...  96.3 us
    pallas_call x1, Pallas kernels, run_tail(): pl.pallas_call(functools.partial(tail_kernel, dims), out_shape=outs, in_s...  65.6 us
    pallas_call x1, Pallas kernels, run_head(): pl.pallas_call(functools.partial(head_kernel, dims, nrows), out_shape=out...  57.9 us
    pallas_call x1, Pallas kernels, on_device(): local_call(functools.partial(backward_kernel, dims, nrows, 8), 'attention...  26.7 us
    pallas_call x1, Pallas kernels, on_device(): local_call(functools.partial(forward_kernel, dims, nrows, 4), 'attention_...  25.9 us
    all_gather x1, waiting for transfers between devices, on_device(): g_rest = lax.all_gather(rest, 'tp', axis=0)  11.8 us
  transfers between devices with their start and end apart: 2, of which 1 were waited for; matrix products, arithmetic and copies ran while one was open for 0% of the time, Pallas kernels for 40%

profile of v8, /device:TPU:8, one launch (start us, length us, event | category | flops | bytes accessed | tf_op | source)
XLA Modules:
  0.0 303.0 jit_solution(7151331674287427682)
XLA Ops:
  7.2 0.0 all-gather.3.cloned.1.call-start
  7.2 57.9 %head.1 = (bf16[4,1024,128]{2,1,0:T(8,128)(2,1)}, bf16[2,4,1024,128]{3,2,1,0:T(8,128)(2,1)}, bf16[1024,1024]{1,0:T(8,128)(2,1)}, bf16[4,1024,256]{2,1,0:T(8,128)...) custom-call(s32[32]{0:T(128)} %docs_ref.1, ...), custom_call_target="tpu_custom_call" | custom-call | flops 64424509440 | bytes 8388608 | tf_op jit(solution)/shard_map/head/pallas_call | solution.py:432
  65.1 0.0 all-gather.3.cloned.1.call-update
  65.2 0.2 reduce-scatter.2.cloned.1.call-start
  65.4 25.9 %attention_forward.1 = (bf16[2048,128]{1,0:T(8,128)(2,1)}, f32[4096,128]{1,0:T(8,128)}) custom-call(s32[16,128]{1,0:T(8,128)} %get-tuple-element.60.table_ref, bf16[4096,128]{1,0:T(8,128)(2,1)} %bitcast.58, bf16[8192,128]{1,0:T(8,128)(2,1)} %bitcast.55), custom_call_target="tpu_custom_call" | custom-call | flops 32212254720 | bytes 8388608 | tf_op jit(solution)/shard_map/attention_forward/pallas_call | solution.py:1627
  91.3 11.8 %all-gather.3.cloned.1.call-done = bf16[3072,256]{1,0:T(8,128)(2,1)} async-done(((bf16[768,256]{1,0:T(8,128)(2,1)}), bf16[3072,256]{1,0:T(8,128)(2,1)}) %all-gather.3.cloned.1.call-update) | async-done | bytes 1572880 | tf_op jit(solution)/shard_map/all_gather | solution.py:1623
  103.2 96.3 %middle.1 = (bf16[4,1024,256]{2,1,0:T(8,128)(2,1)}, bf16[4,512,128]{2,1,0:T(8,128)(2,1)}, bf16[256,1024]{1,0:T(8,128)(2,1)}, bf16[256,1024]{1,0:T(8,128)(2,1)}, ...) custom-call(bf16[4,512,128]{2,1,0:T(8,128)(2,1)} %bitcast.62, ...), custom_call_target="tpu_custom_call" | custom-call | flops 118111600640 | bytes 8388608 | tf_op jit(solution)/shard_map/middle/pallas_call | solution.py:1134
  199.5 0.0 reduce-scatter.2.cloned.1.call-update
  199.5 26.7 %attention_backward.1 = (bf16[2048,128]{1,0:T(8,128)(2,1)}, bf16[8192,128]{1,0:T(8,128)(2,1)}) custom-call(s32[16,128]{1,0:T(8,128)} %get-tuple-element.60.table_ref, bf16[4096,128]{1,0:T(8,128)(2,1)} %bitcast.59, bf16[2048,128]{1,0:T(8,128)(2,1)} %bitcast.60, f32[4096,128]{1,0:T(8,128)} %get-tuple-element.70.res_ref, bf16[8192,128]{1,0:T(8,128)(2,1)} %bitcast.56), custom_call_target="tpu_custom_call" | custom-call | flops 32212254720 | bytes 8388608 | tf_op jit(solution)/shard_map/attention_backward/pallas_call | solution.py:1639
  226.3 65.6 %tail.1 = (f32[1024,256]{1,0:T(8,128)}, f32[256,128]{1,0:T(8,128)}, f32[128,256]{1,0:T(8,128)}, f32[128,256]{1,0:T(8,128)}, f32[128,256]{1,0:T(8,128)}, /*index=5*/f32[62,128]{1,0:T(8,128)}) custom-call(bf16[4,512,128]{2,1,0:T(8,128)(2,1)} %bitcast.61, bf16[2,4,1024,128]{3,2,1,0:T(8,128)(2,1)} %bitcast.57, bf16[1024,1024]{1,0:T(8,128)(2,1)} %get-tuple-element.73.h1_hbm, ...), custom_call_target="tpu_custom_call" | custom-call | flops 75161927680 | bytes 8388608 | tf_op jit(solution)/shard_map/tail/pallas_call | solution.py:1531
  291.9 4.2 %deliver.1 = (f32[8,128]{1,0:T(8,128)}, f32[8,128]{1,0:T(8,128)}, f32[8,128]{1,0:T(8,128)}, f32[8,128]{1,0:T(8,128)}, f32[8,128]{1,0:T(8,128)}, /*index=5*/f32[8...) custom-call(f32[62,128]{1,0:T(8,128)} %get-tuple-element.79.refs_0_,, ...), custom_call_target="tpu_custom_call" | custom-call | tf_op jit(solution)/shard_map/deliver/pallas_call | solution.py:1574
  296.1 0.0 reduce-scatter.2.cloned.1.call-done
Async XLA Ops:
  7.2 96.0 %all-gather.3.cloned.1.call-start = ((), (), s32[]{:S(2)}) async-start(), calls=%async_computation.2 | async-start | bytes 1966080 | tf_op jit(solution)/shard_map/all_gather | solution.py:1623
  65.2 231.0 %reduce-scatter.2.cloned.1.call-start = ((), (), s32[]{:S(2)}) async-start(), calls=%async_computation.1 | async-start | bytes 2621440 | tf_op jit(solution)/shard_map/reduce_scatter | solution.py:1638
Sparse Core Ops, SparseCore 0:
  65.3 37.8 all-gather.2
  199.7 44.2 reduce-scatter.1
